TPU v7x, 32 devices: a whole 2x2x4 slice. The times are simulated.
32 devices in a mesh: cand: 4 (over x, core), row: 4 (over z), col: 2 (over y).
Axes of the slice: x: 2, y: 2, z: 4, core: 2. Of those that a mesh axis runs over, the one named last changes fastest.
Arguments:
- embedding: bfloat16 [1024, 1536], P(('row', 'col')), may hold values from -6 to 6
- bases_table: bfloat16 [4, 1536], replicated, may hold values from -10 to 10
- edit_pos: int32 [256], P('cand'), parts along dimension 0, may hold values from 0 to 1023
- edit_tok: int32 [256], P('cand'), parts along dimension 0, may hold values from 0 to 3
- w_row: bfloat16 [1536, 128], replicated, may hold values from -0.15625 to 0.15625
- w_col: bfloat16 [1536, 128], replicated, may hold values from -0.15625 to 0.15625
- dist_gain: float32 [128], replicated, may hold values from -4 to 4
- first_kernel: bfloat16 [3, 3, 128, 128], replicated, may hold values from -0.1875 to 0.1875
- second_kernel: bfloat16 [3, 3, 128, 128], replicated, may hold values from -0.1875 to 0.1875
- head_weight: bfloat16 [128], replicated, may hold values from -0.5 to 0.5
Outputs:
- contact: float32 [1024, 256], P(('cand', 'row'), 'col'), parts along dimension 0
There are 4 independent parts, one for each index of `cand`. A program takes and returns all parts, laid end to end along the dimension named above; an argument that names none is the same for every part. Nothing has to cross between parts.
Inputs may be any that keep to these rules, and one draw needn't show every extreme that they name: `edit_pos`: two substitutions may fall on the same input bin.
All inputs are finite; a program needn't handle non-finite values.
Results may differ from a plain program's by a relative error of at most 0.015.
Values may be sent and summed in bfloat16 or wider, within the bound.
No kernel may reach another device: no remote copies, remote signals or barrier semaphores. Data moves between devices by JAX's collectives and lax.ppermute only.
A program may use at most 64 MiB of HBM per device.

v0:
```python
import functools
import math

import jax
import jax.numpy as jnp
from jax import lax
from jax.experimental import pallas as pl
from jax.experimental.pallas import tpu as pltpu
from jax.sharding import PartitionSpec as P

POOL = 4
FIRST_SPACING = 2
SECOND_SPACING = 4
BASES = 4
MARGIN = FIRST_SPACING + SECOND_SPACING
PAD = 8
GROUP = 8
OUTSIDE = -1e30


def project_kernel(
    at_ref, embedding_ref, bases_ref, pos_ref, tok_ref, w_row_ref, w_col_ref, copies_ref
):
    shard_bins = embedding_ref.shape[0]
    copies, pooled_bins, _ = copies_ref.shape
    edits = pos_ref.shape[1]
    bins = at_ref[0] + lax.broadcasted_iota(jnp.int32, (pooled_bins, edits), 0) * POOL
    ahead = pos_ref[...] - bins
    in_bin = ((ahead >= 0) & (ahead < POOL)).astype(jnp.float32)
    back = lax.broadcasted_iota(jnp.int32, (pooled_bins, shard_bins), 1) - POOL * (
        lax.broadcasted_iota(jnp.int32, (pooled_bins, shard_bins), 0)
    )
    take = ((back >= 0) & (back < POOL)).astype(jnp.float32).astype(jnp.bfloat16)
    summed = jnp.dot(take, embedding_ref[...], preferred_element_type=jnp.float32)
    for base in range(BASES):
        is_base = (tok_ref[...] == base).astype(jnp.float32)
        count = jnp.sum(in_bin * is_base, axis=1, keepdims=True)
        summed = summed + count * bases_ref[base : base + 1].astype(jnp.float32)
    pooled = (summed * (1.0 / POOL)).astype(jnp.bfloat16)
    both = jnp.concatenate(
        [
            jnp.dot(pooled, ref[...], preferred_element_type=jnp.float32).astype(jnp.bfloat16)
            for ref in (w_row_ref, w_col_ref)
        ],
        axis=1,
    )
    for k in range(copies):
        copies_ref[k] = both


def projected(embedding, bases_table, edit_pos, edit_tok, w_row, w_col, first_bin, copies):
    vmem = pl.BlockSpec(memory_space=pltpu.VMEM)
    return pl.pallas_call(
        project_kernel,
        out_shape=jax.ShapeDtypeStruct(
            (copies, embedding.shape[0] // POOL, 2 * w_row.shape[1]), jnp.bfloat16
        ),
        in_specs=[pl.BlockSpec(memory_space=pltpu.SMEM)] + [vmem] * 6,
        out_specs=vmem,
        compiler_params=pltpu.CompilerParams(vmem_limit_bytes=16 * 1024 * 1024),
    )(first_bin[None].astype(jnp.int32), embedding, bases_table, edit_pos[None], edit_tok[None], w_row, w_col)


def gathered(copies):
    got = lax.all_to_all(copies, ("row", "col"), 0, 0)
    return got.reshape(-1, got.shape[2])


def join_kernel(wide, at_ref, score_ref, *refs):
    *received_refs, out_ref = refs
    parts = len(received_refs)
    size = min(score_ref.shape)
    pieces = [ref[...].T for ref in received_refs]
    for sub in range(parts):
        piece = pieces[0]
        for turn in range(1, parts):
            piece = jnp.where((sub + turn) % parts == at_ref[0], pieces[turn], piece)
        along = slice(sub * size, (sub + 1) * size)
        where = (slice(None), along) if wide else (along, slice(None))
        out_ref[where] = 0.5 * (score_ref[where] + piece)


def symmetrised(score):
    n_rows, n_cols = lax.axis_size("row"), lax.axis_size("col")
    row_at, col_at = lax.axis_index("row"), lax.axis_index("col")
    height, breadth = score.shape
    size = min(height, breadth)
    wide = breadth > height
    parts = max(height, breadth) // size
    own = (row_at if wide else col_at) % parts
    received = []
    for turn in range(parts):
        pairs = []
        for r in range(n_rows):
            for c in range(n_cols):
                if wide:
                    to = (parts * c + (turn + r) % parts, r // parts)
                else:
                    to = (c // parts, parts * r + (turn + c) % parts)
                pairs.append((r * n_cols + c, to[0] * n_cols + to[1]))
        first = ((own + turn) % parts) * size
        piece = lax.dynamic_slice(score, (0, first) if wide else (first, 0), (size, size))
        received.append(lax.ppermute(piece, ("row", "col"), pairs))
    vmem = pl.BlockSpec(memory_space=pltpu.VMEM)
    return pl.pallas_call(
        functools.partial(join_kernel, wide),
        out_shape=jax.ShapeDtypeStruct(score.shape, jnp.float32),
        in_specs=[pl.BlockSpec(memory_space=pltpu.SMEM)] + [vmem] * (1 + parts),
        out_specs=vmem,
    )(own[None].astype(jnp.int32), score, *received)


def relu(x):
    return jnp.maximum(x, 0.0)


def map_kernel(
    map_bins, height, breadth, at_ref, proj_ref, gain_ref, first_ref, second_ref, head_ref,
    score_ref, row_ref, col_ref, dist_ref, pair_ref, hidden_ref, pairs_one_ref, pairs_two_ref,
):
    channels = gain_ref.shape[1]
    wide = breadth + 2 * PAD
    pair_rows = height + 2 * MARGIN
    hidden_rows = height + 2 * SECOND_SPACING
    row_start = pl.multiple_of(at_ref[0], height)
    col_start = pl.multiple_of(at_ref[1], breadth)
    depth = 3 * channels
    for ref, given in ((pairs_one_ref, first_ref), (pairs_two_ref, second_ref)):
        ref[: 3 * depth, :channels] = given[...]
        ref[3 * depth :, :channels] = jnp.zeros((depth, channels), jnp.bfloat16)
        ref[:depth, channels:] = jnp.zeros((depth, channels), jnp.bfloat16)
        ref[depth:, channels:] = given[...]
    outside = jnp.full((PAD, channels), OUTSIDE, jnp.float32)
    for part, ref in enumerate((row_ref, col_ref)):
        ref[:PAD] = outside
        ref[PAD + map_bins :] = outside
        ref[PAD : PAD + map_bins] = proj_ref[:, part * channels : (part + 1) * channels].astype(
            jnp.float32
        )
    span = dist_ref.shape[0]
    step = lax.broadcasted_iota(jnp.int32, (span, channels), 0) - (pair_rows - 1)
    apart = jnp.abs(step + (col_start - PAD - row_start + MARGIN)).astype(jnp.float32)
    dist_ref[...] = gain_ref[...] * (jnp.log1p(apart) * (1.0 / math.log(map_bins)))
    at_edge = lax.broadcasted_iota(jnp.int32, (PAD, channels), 0)
    edge = SECOND_SPACING
    left = jnp.where((at_edge >= edge) | (col_start > 0), 1.0, 0.0)
    right = jnp.where((at_edge < PAD - edge) | (col_start < map_bins - breadth), 1.0, 0.0)
    above = jnp.where(row_start > 0, 1.0, 0.0)
    below = jnp.where(row_start < map_bins - height, 1.0, 0.0)

    def build(p):
        row_part = row_ref[pl.ds(row_start + (PAD - MARGIN + p), 1)]
        value = relu(
            col_ref[pl.ds(col_start, wide)] + dist_ref[pair_rows - 1 - p : pair_rows - 1 - p + wide] + row_part
        )
        shifted = [pltpu.roll(value, FIRST_SPACING, 0), value, pltpu.roll(value, wide - FIRST_SPACING, 0)]
        pair_ref[p] = jnp.concatenate([x.astype(jnp.bfloat16) for x in shifted], axis=1)

    def paired(ref, start, offsets, spacing, weight):
        lhs = jnp.concatenate(
            [
                jnp.concatenate([ref[start + base + k * spacing] for k in range(4)], axis=1)
                for base in offsets
            ],
            axis=0,
        )
        return jnp.dot(lhs, weight[...], preferred_element_type=jnp.float32)

    def keep_hidden(start, offsets, out):
        for n, base in enumerate(offsets):
            for half in range(2):
                a = start + base + half * FIRST_SPACING
                conv = out[n * wide : (n + 1) * wide, half * channels : (half + 1) * channels]
                own = pair_ref[a + FIRST_SPACING, :, channels : 2 * channels].astype(jnp.float32)
                value = own + relu(conv)
                if a < edge:
                    value = value * above
                if a >= hidden_rows - edge:
                    value = value * below
                ahead = pltpu.roll(value, wide - edge, 0)
                taps = [
                    jnp.concatenate([ahead[:PAD] * left, ahead[PAD:breadth]], axis=0),
                    value[PAD : PAD + breadth],
                    jnp.concatenate([ahead[PAD:breadth], ahead[breadth : breadth + PAD] * right], axis=0),
                ]
                hidden_ref[a] = jnp.concatenate([x.astype(jnp.bfloat16) for x in taps], axis=1)

    def keep_score(start, offsets, out):
        last = []
        for n, base in enumerate(offsets):
            halves = []
            for half in range(2):
                o = start + base + half * edge
                conv = out[n * breadth : (n + 1) * breadth, half * channels : (half + 1) * channels]
                own = hidden_ref[o + edge, :, channels : 2 * channels].astype(jnp.float32)
                halves.append((own + relu(conv)).astype(jnp.bfloat16))
            last.append(jnp.concatenate(halves, axis=1))
        got = lax.dot_general(
            head_ref[...],
            jnp.concatenate(last, axis=0),
            (((1,), (1,)), ((), ())),
            preferred_element_type=jnp.float32,
        )
        count = len(offsets)
        lines = [got[half : half + 1, n * breadth : (n + 1) * breadth] for half in range(2) for n in range(count)]
        score_ref[start : start + 8] = jnp.concatenate(lines, axis=0)

    first_offsets, second_offsets = (0, 1, 4, 5), (0, 1, 2, 3)
    first_groups, second_groups = hidden_rows // GROUP, height // GROUP
    for p in range(2 * GROUP):
        build(p)
    for s in range(first_groups + 1):
        one = two = None
        if s < first_groups:
            one = paired(pair_ref, s * GROUP, first_offsets, FIRST_SPACING, pairs_one_ref)
        for p in range((s + 2) * GROUP, min((s + 3) * GROUP, pair_rows)):
            build(p)
        if 0 <= s - 2 < second_groups:
            two = paired(hidden_ref, (s - 2) * GROUP, second_offsets, SECOND_SPACING, pairs_two_ref)
        if one is not None:
            keep_hidden(s * GROUP, first_offsets, one)
        if two is not None:
            keep_score((s - 2) * GROUP, second_offsets, two)


def tile_scores(every, at, dist_gain, first_kernel, second_kernel, head_weight, height, breadth):
    map_bins = every.shape[0]
    channels = dist_gain.shape[0]
    wide = breadth + 2 * PAD
    pair_rows = height + 2 * MARGIN
    span = -(-(pair_rows + wide) // 8) * 8
    zero = jnp.zeros_like(head_weight)
    head = jnp.stack(
        [jnp.concatenate([head_weight, zero]), jnp.concatenate([zero, head_weight])]
        + [jnp.concatenate([zero, zero])] * 14
    )
    return pl.pallas_call(
        functools.partial(map_kernel, map_bins, height, breadth),
        out_shape=jax.ShapeDtypeStruct((height, breadth), jnp.float32),
        in_specs=[pl.BlockSpec(memory_space=pltpu.SMEM)] + [pl.BlockSpec(memory_space=pltpu.VMEM)] * 5,
        out_specs=pl.BlockSpec(memory_space=pltpu.VMEM),
        scratch_shapes=[
            pltpu.VMEM((map_bins + 2 * PAD, channels), jnp.float32),
            pltpu.VMEM((map_bins + 2 * PAD, channels), jnp.float32),
            pltpu.VMEM((span, channels), jnp.float32),
            pltpu.VMEM((pair_rows, wide, 3 * channels), jnp.bfloat16),
            pltpu.VMEM((height + 2 * SECOND_SPACING, breadth, 3 * channels), jnp.bfloat16),
            pltpu.VMEM((12 * channels, 2 * channels), jnp.bfloat16),
            pltpu.VMEM((12 * channels, 2 * channels), jnp.bfloat16),
        ],
        compiler_params=pltpu.CompilerParams(vmem_limit_bytes=40 * 1024 * 1024),
    )(
        at,
        every,
        dist_gain[None],
        first_kernel.reshape(9 * channels, channels),
        second_kernel.reshape(9 * channels, channels),
        head,
    )


def on_device(
    embedding,
    bases_table,
    edit_pos,
    edit_tok,
    w_row,
    w_col,
    dist_gain,
    first_kernel,
    second_kernel,
    head_weight,
):
    n_rows, n_cols = lax.axis_size("row"), lax.axis_size("col")
    row_at, col_at = lax.axis_index("row"), lax.axis_index("col")
    shard_bins = embedding.shape[0]
    map_bins = shard_bins * n_rows * n_cols // POOL
    height, breadth = map_bins // n_rows, map_bins // n_cols
    first_bin = (row_at * n_cols + col_at) * shard_bins
    copies = projected(
        embedding, bases_table, edit_pos, edit_tok, w_row, w_col, first_bin, n_rows * n_cols
    )
    at = jnp.stack([row_at * height, col_at * breadth]).astype(jnp.int32)
    score = tile_scores(
        gathered(copies), at, dist_gain, first_kernel, second_kernel, head_weight, height, breadth
    )
    return symmetrised(score)


def solution(mesh):
    placed = (P(("row", "col"), None), P(), P("cand"), P("cand"), P(), P(), P(), P(), P(), P())
    return jax.shard_map(
        on_device, mesh=mesh, in_specs=placed, out_specs=P(("cand", "row"), "col"), check_vma=False
    )
```

profile of v0, /device:TPU:4, one launch (start us, length us, event | category | flops | bytes accessed | tf_op | source)
XLA Modules:
  0.0 40.0 jit_solution(17289809938409565991)
XLA Ops:
  0.0 0.0 copy-start.6
  0.0 0.0 copy-start.7
  0.0 0.0 copy-start.8
  0.0 0.7 %copy-done.6 = bf16[4,1536]{1,0:T(4,128)(2,1)S(1)} copy-done((bf16[4,1536]{1,0:T(4,128)(2,1)S(1)}, bf16[4,1536]{1,0:T(4,128)(2,1)}, u32[]{:S(2)}) %copy-start.6) | copy-done | bytes 12312
  0.7 0.0 copy-done.7
  0.7 0.0 copy-done.8
  0.7 0.0 copy-start.1
  0.7 1.0 %copy-done.1 = bf16[128,1536]{1,0:T(8,128)(2,1)S(1)} copy-done((bf16[128,1536]{1,0:T(8,128)(2,1)S(1)}, bf16[128,1536]{1,0:T(8,128)(2,1)}, u32[]{:S(2)}) %copy-start.1) | copy-done | bytes 393240
  1.7 0.0 copy-start.2
  1.7 1.0 %copy-done.2 = bf16[1536,128]{1,0:T(8,128)(2,1)S(1)} copy-done((bf16[1536,128]{1,0:T(8,128)(2,1)S(1)}, bf16[1536,128]{1,0:T(8,128)(2,1)}, u32[]{:S(2)}) %copy-start.2) | copy-done | bytes 393240
  2.7 0.0 copy-start.3
  2.7 1.0 %copy-done.3 = bf16[1536,128]{1,0:T(8,128)(2,1)S(1)} copy-done((bf16[1536,128]{1,0:T(8,128)(2,1)S(1)}, bf16[1536,128]{1,0:T(8,128)(2,1)}, u32[]{:S(2)}) %copy-start.3) | copy-done | bytes 393240
  3.7 0.0 copy-start.5
  3.7 1.1 %shard_map.100 = bf16[8,32,256]{2,1,0:T(8,128)(2,1)} custom-call(s32[1]{0:T(128)} %bitcast.3.at_ref, bf16[128,1536]{1,0:T(8,128)(2,1)S(1)} %copy-done.1, bf16[4,1536]{1,0:T(4,128)(2,1)S(1)} %copy-done.6, s32[1,64]{1,0:T(1,128)S(1)} %bitcast.13, s32[1,64]{1,0:T(1,128)S(1)} %bitcast.14, bf16[1536,128]{1,0:T(8,128)(2,1)S(1)} %copy-done.2, ...), custom_call_target="tpu_custom_call" | custom-call | tf_op jit(solution)/shard_map/pallas_call | solution.py:53
  4.8 0.0 copy-start.4
  4.8 6.5 %all-to-all-start = ((bf16[8,32,256]{2,1,0:T(8,128)(2,1)}), bf16[8,32,256]{2,1,0:T(8,128)(2,1)S(1)}, u32[]{:S(2)}, u32[]{:S(2)}) async-start(bf16[8,32,256]{2,1,0:T(8,128)(2,1)} %shard_map.100), calls=%async_computation | async-start | bytes 262144 | tf_op jit(solution)/shard_map/all_to_all | solution.py:65
  11.3 0.0 copy-start.12
  11.3 0.7 %copy-done.12 = bf16[128]{0:T(256)(128)(2,1)S(1)} copy-done((bf16[128]{0:T(256)(128)(2,1)S(1)}, bf16[128]{0:T(256)(128)(2,1)}, u32[]{:S(2)}) %copy-start.12) | copy-done | bytes 280
  12.0 0.1 pad_add_fusion.at_ref
  12.1 4.7 %all-to-all-done = bf16[8,32,256]{2,1,0:T(8,128)(2,1)S(1)} async-done(((bf16[8,32,256]{2,1,0:T(8,128)(2,1)}), bf16[8,32,256]{2,1,0:T(8,128)(2,1)S(1)}, u32[]{:S(2)}, u32[]{:S(2)}) %all-to-all-start) | async-done | bytes 131104 | tf_op jit(solution)/shard_map/all_to_all | solution.py:65
  16.8 0.0 copy-start.9
  16.8 0.0 copy-done.5
  16.8 0.0 copy-done.4
  16.8 0.6 %copy-done.9 = f32[128]{0:T(128)S(1)} copy-done((f32[128]{0:T(128)S(1)}, f32[128]{0:T(128)}, u32[]{:S(2)}) %copy-start.9) | copy-done | bytes 536
  17.5 9.6 %shard_map.101.score_ref = f32[64,128]{1,0:T(8,128)S(1)} custom-call(s32[2]{0:T(128)S(1)} %pad_add_fusion.at_ref, bf16[256,256]{1,0:T(8,128)(2,1)S(1)} %bitcast.10, f32[1,128]{1,0:T(1,128)S(1)} %bitcast.15, bf16[1152,128]{1,0:T(8,128)(2,1)S(1)} %bitcast.11, bf16[1152,128]{1,0:T(8,128)(2,1)S(1)} %bitcast.12, bf16[16,256]{1,0:T(8,128)(2,1)S(1)} %stack.35.head_ref), custom_call_target="tpu_custom_call" | custom-call | tf_op jit(solution)/shard_map/pallas_call | solution.py:237
  27.0 0.0 copy-start
  27.0 0.1 constant_dynamic-slice_fusion
  27.1 0.5 %copy-done = f32[64,128]{1,0:T(8,128)} copy-done((f32[64,128]{1,0:T(8,128)}, f32[64,128]{1,0:T(8,128)S(1)}, u32[]{:S(2)}) %copy-start) | copy-done | bytes 32792
  27.7 3.5 %collective-permute-start = (f32[64,64]{1,0:T(8,128)S(1)}, f32[64,64]{1,0:T(8,128)S(1)}, u32[]{:S(2)}, u32[]{:S(2)}) collective-permute-start(f32[64,64]{1,0:T(8,128)S(1)} %get-tuple-element.6), channel_id=1, source_target_pairs={{0,0},{1,4},{2,2},{3,6},{4,1},{5,5},{6,3},{7,7},{8,8},{9,12},{10,1... | collective-permute-start | bytes 49160 | tf_op jit(solution)/shard_map/ppermute | solution.py:103
  31.2 2.8 %collective-permute-start.1 = (f32[64,64]{1,0:T(8,128)S(1)}, f32[64,64]{1,0:T(8,128)S(1)}, u32[]{:S(2)}, u32[]{:S(2)}) collective-permute-start(f32[64,64]{1,0:T(8,128)S(1)} %get-tuple-element.5), channel_id=1, source_target_pairs={{0,2},{1,6},{2,0},{3,4},{4,3},{5,7},{6,1},{7,5},{8,10},{9,14},{10,... | collective-permute-start | bytes 49160 | tf_op jit(solution)/shard_map/ppermute | solution.py:103
  34.0 2.0 %collective-permute-done.refs_0_ = f32[64,64]{1,0:T(8,128)S(1)} collective-permute-done((f32[64,64]{1,0:T(8,128)S(1)}, f32[64,64]{1,0:T(8,128)S(1)}, u32[]{:S(2)}, u32[]{:S(2)}) %collective-permute-start) | collective-permute-done | bytes 16416 | tf_op jit(solution)/shard_map/ppermute | solution.py:103
  36.0 0.0 copy-start.10
  36.0 1.9 %collective-permute-done.1.refs_1_ = f32[64,64]{1,0:T(8,128)S(1)} collective-permute-done((f32[64,64]{1,0:T(8,128)S(1)}, f32[64,64]{1,0:T(8,128)S(1)}, u32[]{:S(2)}, u32[]{:S(2)}) %collective-permute-start.1) | collective-permute-done | bytes 16416 | tf_op jit(solution)/shard_map/ppermute | solution.py:103
  37.9 0.0 copy-start.11
  37.9 0.0 copy-done.10
  37.9 0.6 %copy-done.11 = f32[64,64]{1,0:T(8,128)} copy-done((f32[64,64]{1,0:T(8,128)}, f32[64,64]{1,0:T(8,128)S(1)}, u32[]{:S(2)}) %copy-start.11) | copy-done | bytes 16408
  38.5 1.6 %shard_map.102 = f32[64,128]{1,0:T(8,128)} custom-call(s32[1]{0:T(128)} %bitcast.at_ref, f32[64,128]{1,0:T(8,128)} %copy-done, f32[64,64]{1,0:T(8,128)} %copy-done.10, f32[64,64]{1,0:T(8,128)} %copy-done.11), custom_call_target="tpu_custom_call" | custom-call | tf_op jit(solution)/shard_map/pallas_call | solution.py:105
  (7 shorter events, 0.1 us)
Async XLA Ops:
  0.0 0.7 %copy-start.6 = (bf16[4,1536]{1,0:T(4,128)(2,1)S(1)}, bf16[4,1536]{1,0:T(4,128)(2,1)}, u32[]{:S(2)}) copy-start(bf16[4,1536]{1,0:T(4,128)(2,1)} %bases_ref.1) | copy-start | bytes 36868
  0.0 0.7 %copy-start.7 = (s32[64]{0:T(128)S(1)}, s32[64]{0:T(128)}, u32[]{:S(2)}) copy-start(s32[64]{0:T(128)} %param.12) | copy-start | bytes 772
  0.0 0.7 %copy-start.8 = (s32[64]{0:T(128)S(1)}, s32[64]{0:T(128)}, u32[]{:S(2)}) copy-start(s32[64]{0:T(128)} %param.13) | copy-start | bytes 772
  0.7 1.0 %copy-start.1 = (bf16[128,1536]{1,0:T(8,128)(2,1)S(1)}, bf16[128,1536]{1,0:T(8,128)(2,1)}, u32[]{:S(2)}) copy-start(bf16[128,1536]{1,0:T(8,128)(2,1)} %embedding_ref.1) | copy-start | bytes 1179652
  1.7 1.0 %copy-start.2 = (bf16[1536,128]{1,0:T(8,128)(2,1)S(1)}, bf16[1536,128]{1,0:T(8,128)(2,1)}, u32[]{:S(2)}) copy-start(bf16[1536,128]{1,0:T(8,128)(2,1)} %w_row_ref.1) | copy-start | bytes 1179652
  2.7 1.0 %copy-start.3 = (bf16[1536,128]{1,0:T(8,128)(2,1)S(1)}, bf16[1536,128]{1,0:T(8,128)(2,1)}, u32[]{:S(2)}) copy-start(bf16[1536,128]{1,0:T(8,128)(2,1)} %w_col_ref.1) | copy-start | bytes 1179652
  3.7 13.1 %copy-start.5 = (bf16[3,3,128,128]{3,2,1,0:T(8,128)(2,1)S(1)}, bf16[3,3,128,128]{3,2,1,0:T(8,128)(2,1)}, u32[]{:S(2)}) copy-start(bf16[3,3,128,128]{3,2,1,0:T(8,128)(2,1)} %param.18) | copy-start | bytes 884740
  4.8 12.0 %copy-start.4 = (bf16[3,3,128,128]{3,2,1,0:T(8,128)(2,1)S(1)}, bf16[3,3,128,128]{3,2,1,0:T(8,128)(2,1)}, u32[]{:S(2)}) copy-start(bf16[3,3,128,128]{3,2,1,0:T(8,128)(2,1)} %param.17) | copy-start | bytes 884740
  4.8 12.0 %all-to-all-start = ((bf16[8,32,256]{2,1,0:T(8,128)(2,1)}), bf16[8,32,256]{2,1,0:T(8,128)(2,1)S(1)}, u32[]{:S(2)}, u32[]{:S(2)}) async-start(bf16[8,32,256]{2,1,0:T(8,128)(2,1)} %shard_map.100), calls=%async_computation | async-start | bytes 262144 | tf_op jit(solution)/shard_map/all_to_all | solution.py:65
  11.3 0.7 %copy-start.12 = (bf16[128]{0:T(256)(128)(2,1)S(1)}, bf16[128]{0:T(256)(128)(2,1)}, u32[]{:S(2)}) copy-start(bf16[128]{0:T(256)(128)(2,1)} %param.19) | copy-start | bytes 772
  16.8 0.7 %copy-start.9 = (f32[128]{0:T(128)S(1)}, f32[128]{0:T(128)}, u32[]{:S(2)}) copy-start(f32[128]{0:T(128)} %param.16) | copy-start | bytes 1540
  27.0 0.6 %copy-start = (f32[64,128]{1,0:T(8,128)}, f32[64,128]{1,0:T(8,128)S(1)}, u32[]{:S(2)}) copy-start(f32[64,128]{1,0:T(8,128)S(1)} %shard_map.101.score_ref) | copy-start | bytes 98308
  27.7 8.3 %collective-permute-start = (f32[64,64]{1,0:T(8,128)S(1)}, f32[64,64]{1,0:T(8,128)S(1)}, u32[]{:S(2)}, u32[]{:S(2)}) collective-permute-start(f32[64,64]{1,0:T(8,128)S(1)} %get-tuple-element.6), channel_id=1, source_target_pairs={{0,0},{1,4},{2,2},{3,6},{4,1},{5,5},{6,3},{7,7},{8,8},{9,12},{10,1... | collective-permute-start | bytes 49160 | tf_op jit(solution)/shard_map/ppermute | solution.py:103
  31.2 6.7 %collective-permute-start.1 = (f32[64,64]{1,0:T(8,128)S(1)}, f32[64,64]{1,0:T(8,128)S(1)}, u32[]{:S(2)}, u32[]{:S(2)}) collective-permute-start(f32[64,64]{1,0:T(8,128)S(1)} %get-tuple-element.5), channel_id=1, source_target_pairs={{0,2},{1,6},{2,0},{3,4},{4,3},{5,7},{6,1},{7,5},{8,10},{9,14},{10,... | collective-permute-start | bytes 49160 | tf_op jit(solution)/shard_map/ppermute | solution.py:103
  36.0 1.9 %copy-start.10 = (f32[64,64]{1,0:T(8,128)}, f32[64,64]{1,0:T(8,128)S(1)}, u32[]{:S(2)}) copy-start(f32[64,64]{1,0:T(8,128)S(1)} %collective-permute-done.refs_0_) | copy-start | bytes 49156
  37.9 0.6 %copy-start.11 = (f32[64,64]{1,0:T(8,128)}, f32[64,64]{1,0:T(8,128)S(1)}, u32[]{:S(2)}) copy-start(f32[64,64]{1,0:T(8,128)S(1)} %collective-permute-done.1.refs_1_) | copy-start | bytes 49156
where the time goes:
time: 40.5 us; the launch traced here: 40 us
  starting transfers between devices  12.8 us (32%)
  Pallas kernels  12.2 us (30%)
  waiting for transfers between devices  8.61 us (21%)
  local copies, waits for them, and re-layouts  6.3 us (16%)
    pallas_call x1, Pallas kernels, tile_scores(): pl.pallas_call(functools.partial(map_kernel, map_bins, height, breadth),...  9.57 us
    all_to_all x1, starting transfers between devices, gathered(): got = lax.all_to_all(copies, ('row', 'col'), 0, 0)  6.47 us
    ppermute x2, starting transfers between devices, symmetrised(): received.append(lax.ppermute(piece, ('row', 'col'), pairs))  6.31 us
    unnamed x26, local copies, waits for them, and re-layouts  6.15 us
    all_to_all x1, waiting for transfers between devices, gathered(): got = lax.all_to_all(copies, ('row', 'col'), 0, 0)  4.71 us
    ppermute x2, waiting for transfers between devices, symmetrised(): received.append(lax.ppermute(piece, ('row', 'col'), pairs))  3.9 us
    pallas_call x1, Pallas kernels, symmetrised(): pl.pallas_call(functools.partial(join_kernel, wide), out_shape=jax.ShapeD...  1.56 us
    pallas_call x1, Pallas kernels, projected(): pl.pallas_call(project_kernel, out_shape=jax.ShapeDtypeStruct((copies, em...  1.08 us
  transfers between devices with their start and end apart: 3, of which 3 were waited for; matrix products, arithmetic and copies ran while one was open for 0% of the time, Pallas kernels for 0%

commit v1 on v0

v1 whole, which is shorter than its diff:
```python
import functools
import math

import jax
import jax.numpy as jnp
from jax import lax
from jax.experimental import pallas as pl
from jax.experimental.pallas import tpu as pltpu
from jax.sharding import PartitionSpec as P

POOL = 4
FIRST_SPACING = 2
SECOND_SPACING = 4
BASES = 4
MARGIN = FIRST_SPACING + SECOND_SPACING
PAD = 8
GROUP = 8
OUTSIDE = -1e30


def plan(n_rows, n_cols):
    wide = n_rows > n_cols
    blocks = max(n_rows, n_cols)
    assert blocks == 2 * min(n_rows, n_cols)

    def owner(i, j):
        return i * n_cols + j // 2 if wide else (i // 2) * n_cols + j

    held = {}
    for i in range(blocks):
        for j in range(blocks):
            held.setdefault(owner(i, j), []).append((i, j))

    def other(device, block):
        return next(b for b in held[device] if b != block)

    jobs, target = {}, {}

    def assign(device, kept, sent):
        place = held[device].index(kept)
        jobs[device] = (*kept, *sent, int(kept[0] == kept[1]), place)
        target[device] = owner(*sent)

    def walk(device, block):
        while device not in jobs:
            if block[0] == block[1]:
                return device, block
            sent = (block[1], block[0])
            assign(device, block, sent)
            device = owner(*sent)
            block = other(device, sent)
        return None, None

    for d in range(blocks):
        start = owner(d, d)
        if start not in jobs:
            end, last = walk(start, other(start, (d, d)))
            assign(end, last, (d, d))
    for device in sorted(held):
        if device not in jobs:
            walk(device, held[device][0])
    return [jobs[device] for device in sorted(jobs)], target


def relu(x):
    return jnp.maximum(x, 0.0)


def lookup(table):
    n_cols = lax.axis_size("col")
    here = lax.axis_index("row") * n_cols + lax.axis_index("col")
    found = []
    for values in zip(*table):
        value = jnp.int32(values[0])
        for device in range(1, len(values)):
            value = jnp.where(here == device, jnp.int32(values[device]), value)
        found.append(value)
    return found


def project_kernel(
    map_bins, embedding_hbm, bases_hbm, pos_hbm, tok_hbm, w_row_hbm, w_col_hbm, gain_hbm, head_hbm,
    copies_ref, dist_ref, head_ref,
    embedding_ref, bases_ref, pos_ref, tok_ref, w_row_ref, w_col_ref, gain_ref, weight_ref, arrived,
):
    moves = [
        pltpu.make_async_copy(source, target, arrived.at[n])
        for n, (source, target) in enumerate(
            (
                (embedding_hbm, embedding_ref),
                (w_row_hbm, w_row_ref),
                (w_col_hbm, w_col_ref),
                (pos_hbm, pos_ref),
                (tok_hbm, tok_ref),
                (bases_hbm, bases_ref),
                (gain_hbm, gain_ref),
                (head_hbm, weight_ref),
            )
        )
    ]
    for move in moves:
        move.start()
    got_embedding, got_w_row, got_w_col, *small = moves
    shard_bins = embedding_ref.shape[0]
    copies, pooled_bins, _ = copies_ref.shape
    channels = gain_ref.shape[1]
    edits = pos_ref.shape[1]
    span = dist_ref.shape[0]
    apart = jnp.abs(lax.broadcasted_iota(jnp.int32, (span, channels), 0) - span // 2)
    feature = jnp.log1p(apart.astype(jnp.float32)) * (1.0 / math.log(map_bins))
    first_bin = (lax.axis_index("row") * lax.axis_size("col") + lax.axis_index("col")) * shard_bins
    bins = first_bin + lax.broadcasted_iota(jnp.int32, (pooled_bins, edits), 0) * POOL
    back = lax.broadcasted_iota(jnp.int32, (pooled_bins, shard_bins), 1) - POOL * (
        lax.broadcasted_iota(jnp.int32, (pooled_bins, shard_bins), 0)
    )
    take = ((back >= 0) & (back < POOL)).astype(jnp.float32).astype(jnp.bfloat16)
    for move in small:
        move.wait()
    dist_ref[...] = gain_ref[...] * feature
    weight = jnp.concatenate([weight_ref[...].astype(jnp.float32)] * 2, axis=1)
    line = lax.broadcasted_iota(jnp.int32, head_ref.shape, 0)
    half = lax.broadcasted_iota(jnp.int32, head_ref.shape, 1) >= channels
    head_ref[...] = jnp.where(line == half.astype(jnp.int32), weight, 0.0).astype(jnp.bfloat16)
    ahead = pos_ref[...] - bins
    in_bin = ((ahead >= 0) & (ahead < POOL)).astype(jnp.float32)
    edited = None
    for base in range(BASES):
        is_base = (tok_ref[...] == base).astype(jnp.float32)
        count = jnp.sum(in_bin * is_base, axis=1, keepdims=True)
        term = count * bases_ref[base : base + 1].astype(jnp.float32)
        edited = term if edited is None else edited + term
    got_embedding.wait()
    summed = edited + jnp.dot(take, embedding_ref[...], preferred_element_type=jnp.float32)
    pooled = (summed * (1.0 / POOL)).astype(jnp.bfloat16)
    sides = []
    for move, ref in ((got_w_row, w_row_ref), (got_w_col, w_col_ref)):
        move.wait()
        sides.append(jnp.dot(pooled, ref[...], preferred_element_type=jnp.float32).astype(jnp.bfloat16))
    both = jnp.concatenate(sides, axis=1)
    for k in range(copies):
        copies_ref[k] = both


def projected(embedding, bases_table, edit_pos, edit_tok, w_row, w_col, dist_gain, head_weight, map_bins, copies):
    vmem = pl.BlockSpec(memory_space=pltpu.VMEM)
    operands = (
        embedding,
        bases_table,
        edit_pos[None],
        edit_tok[None],
        w_row,
        w_col,
        dist_gain[None],
        head_weight[None],
    )
    channels = w_row.shape[1]
    return pl.pallas_call(
        functools.partial(project_kernel, map_bins),
        out_shape=(
            jax.ShapeDtypeStruct((copies, embedding.shape[0] // POOL, 2 * channels), jnp.bfloat16),
            jax.ShapeDtypeStruct((2 * map_bins + 4 * PAD, channels), jnp.float32),
            jax.ShapeDtypeStruct((16, 2 * channels), jnp.bfloat16),
        ),
        in_specs=[pl.BlockSpec(memory_space=pltpu.HBM)] * 8,
        out_specs=(vmem, vmem, vmem),
        scratch_shapes=[pltpu.VMEM(x.shape, x.dtype) for x in operands] + [pltpu.SemaphoreType.DMA((8,))],
        compiler_params=pltpu.CompilerParams(vmem_limit_bytes=16 * 1024 * 1024),
    )(*operands)


def map_kernel(
    map_bins, size, table, proj_ref, dist_table_ref, first_ref, second_ref, head_ref,
    kept_ref, sent_ref, row_ref, col_ref, pair_ref, hidden_ref, pairs_one_ref, pairs_two_ref, score_ref,
):
    channels = dist_table_ref.shape[1]
    block_wide = size + 2 * PAD
    wide = 2 * block_wide
    breadth = 2 * size
    pair_rows = size + 2 * MARGIN
    hidden_rows = size + 2 * SECOND_SPACING
    depth = 3 * channels
    edge = SECOND_SPACING
    row_a, col_a, row_b, col_b, diagonal, _ = lookup(table)
    blocks = [
        (pl.multiple_of(row_a * size, size), pl.multiple_of(col_a * size, size)),
        (pl.multiple_of(row_b * size, size), pl.multiple_of(col_b * size, size)),
    ]
    outside = jnp.full((PAD, channels), OUTSIDE, jnp.float32)
    for part, ref in enumerate((row_ref, col_ref)):
        ref[:PAD] = outside
        ref[PAD + map_bins :] = outside
        ref[PAD : PAD + map_bins] = proj_ref[:, part * channels : (part + 1) * channels].astype(
            jnp.float32
        )
    for ref, given in ((pairs_one_ref, first_ref), (pairs_two_ref, second_ref)):
        ref[: 3 * depth, :channels] = given[...]
        ref[3 * depth :, :channels] = jnp.zeros((depth, channels), jnp.bfloat16)
        ref[:depth, channels:] = jnp.zeros((depth, channels), jnp.bfloat16)
        ref[depth:, channels:] = given[...]
    zero_apart = dist_table_ref.shape[0] // 2
    at_edge = lax.broadcasted_iota(jnp.int32, (PAD, channels), 0)
    last_start = map_bins - size
    left = [jnp.where((at_edge >= edge) | (col > 0), 1.0, 0.0) for _, col in blocks]
    right = [jnp.where((at_edge < PAD - edge) | (col < last_start), 1.0, 0.0) for _, col in blocks]
    above = [jnp.where(row > 0, 1.0, 0.0) for row, _ in blocks]
    below = [jnp.where(row < last_start, 1.0, 0.0) for row, _ in blocks]

    def build(p):
        values = []
        for row, col in blocks:
            row_part = row_ref[pl.ds(row + (PAD - MARGIN + p), 1)]
            apart = dist_table_ref[pl.ds(col - row + (zero_apart - PAD + MARGIN - p), block_wide)]
            values.append(relu(col_ref[pl.ds(col, block_wide)] + apart + row_part))
        value = jnp.concatenate(values, axis=0)
        shifted = [pltpu.roll(value, FIRST_SPACING, 0), value, pltpu.roll(value, wide - FIRST_SPACING, 0)]
        pair_ref[p] = jnp.concatenate([x.astype(jnp.bfloat16) for x in shifted], axis=1)

    def paired(ref, start, offsets, spacing, weight):
        lhs = jnp.concatenate(
            [
                jnp.concatenate([ref[start + base + k * spacing] for k in range(4)], axis=1)
                for base in offsets
            ],
            axis=0,
        )
        return jnp.dot(lhs, weight[...], preferred_element_type=jnp.float32)

    def keep_hidden(start, offsets, out):
        for n, base in enumerate(offsets):
            for half in range(2):
                a = start + base + half * FIRST_SPACING
                conv = out[n * wide : (n + 1) * wide, half * channels : (half + 1) * channels]
                own = pair_ref[a + FIRST_SPACING, :, channels : 2 * channels].astype(jnp.float32)
                value = own + relu(conv)
                for rows, flags in ((a < edge, above), (a >= hidden_rows - edge, below)):
                    if rows:
                        value = jnp.concatenate(
                            [value[:block_wide] * flags[0], value[block_wide:] * flags[1]], axis=0
                        )
                ahead = pltpu.roll(value, wide - edge, 0)
                before, middle, after = [], [], []
                for b in range(2):
                    at = b * block_wide
                    before += [ahead[at : at + PAD] * left[b], ahead[at + PAD : at + size]]
                    middle += [value[at + PAD : at + PAD + size]]
                    after += [ahead[at + PAD : at + size], ahead[at + size : at + size + PAD] * right[b]]
                hidden_ref[a] = jnp.concatenate(
                    [jnp.concatenate(x, axis=0).astype(jnp.bfloat16) for x in (before, middle, after)], axis=1
                )

    def keep_score(start, offsets, out):
        last = []
        for n, base in enumerate(offsets):
            halves = []
            for half in range(2):
                o = start + base + half * edge
                conv = out[n * breadth : (n + 1) * breadth, half * channels : (half + 1) * channels]
                own = hidden_ref[o + edge, :, channels : 2 * channels].astype(jnp.float32)
                halves.append((own + relu(conv)).astype(jnp.bfloat16))
            last.append(jnp.concatenate(halves, axis=1))
        got = lax.dot_general(
            head_ref[...],
            jnp.concatenate(last, axis=0),
            (((1,), (1,)), ((), ())),
            preferred_element_type=jnp.float32,
        )
        count = len(offsets)
        lines = [got[half : half + 1, n * breadth : (n + 1) * breadth] for half in range(2) for n in range(count)]
        score_ref[start : start + 8] = jnp.concatenate(lines, axis=0)

    first_offsets, second_offsets = (0, 1, 4, 5), (0, 1, 2, 3)
    first_groups, second_groups = hidden_rows // GROUP, size // GROUP
    for p in range(2 * GROUP):
        build(p)
    for s in range(first_groups + 1):
        one = two = None
        if s < first_groups:
            one = paired(pair_ref, s * GROUP, first_offsets, FIRST_SPACING, pairs_one_ref)
        for p in range((s + 2) * GROUP, min((s + 3) * GROUP, pair_rows)):
            build(p)
        if 0 <= s - 2 < second_groups:
            two = paired(hidden_ref, (s - 2) * GROUP, second_offsets, SECOND_SPACING, pairs_two_ref)
        if one is not None:
            keep_hidden(s * GROUP, first_offsets, one)
        if two is not None:
            keep_score((s - 2) * GROUP, second_offsets, two)
    score = score_ref[...]
    turned = score.T
    first, second = score[:, :size], score[:, size:]
    turned_first, turned_second = turned[:size], turned[size:]
    alone = diagonal == 1
    kept_ref[...] = 0.5 * (first + jnp.where(alone, turned_first, turned_second))
    sent_ref[...] = 0.5 * (second + jnp.where(alone, turned_second, turned_first))


def block_scores(every, dist_table, first_kernel, second_kernel, head, size, table):
    map_bins = every.shape[0]
    channels = dist_table.shape[1]
    wide = 2 * (size + 2 * PAD)
    vmem = pl.BlockSpec(memory_space=pltpu.VMEM)
    block = jax.ShapeDtypeStruct((size, size), jnp.float32)
    return pl.pallas_call(
        functools.partial(map_kernel, map_bins, size, table),
        out_shape=(block, block),
        in_specs=[vmem] * 5,
        out_specs=(vmem, vmem),
        scratch_shapes=[
            pltpu.VMEM((map_bins + 2 * PAD, channels), jnp.float32),
            pltpu.VMEM((map_bins + 2 * PAD, channels), jnp.float32),
            pltpu.VMEM((size + 2 * MARGIN, wide, 3 * channels), jnp.bfloat16),
            pltpu.VMEM((size + 2 * SECOND_SPACING, 2 * size, 3 * channels), jnp.bfloat16),
            pltpu.VMEM((12 * channels, 2 * channels), jnp.bfloat16),
            pltpu.VMEM((12 * channels, 2 * channels), jnp.bfloat16),
            pltpu.VMEM((size, 2 * size), jnp.float32),
        ],
        compiler_params=pltpu.CompilerParams(vmem_limit_bytes=40 * 1024 * 1024),
    )(
        every,
        dist_table,
        first_kernel.reshape(9 * channels, channels),
        second_kernel.reshape(9 * channels, channels),
        head,
    )


def on_device(
    embedding,
    bases_table,
    edit_pos,
    edit_tok,
    w_row,
    w_col,
    dist_gain,
    first_kernel,
    second_kernel,
    head_weight,
):
    n_rows, n_cols = lax.axis_size("row"), lax.axis_size("col")
    devices = n_rows * n_cols
    map_bins = embedding.shape[0] * devices // POOL
    table, target = plan(n_rows, n_cols)
    size = map_bins // max(n_rows, n_cols)
    copies, dist_table, head = projected(
        embedding, bases_table, edit_pos, edit_tok, w_row, w_col, dist_gain, head_weight, map_bins, devices
    )
    got = lax.all_to_all(copies, ("row", "col"), 0, 0)
    every = got.reshape(map_bins, got.shape[2])
    kept, sent = block_scores(every, dist_table, first_kernel, second_kernel, head, size, table)
    received = lax.ppermute(sent, ("row", "col"), [(device, target[device]) for device in range(devices)])
    place = lookup(table)[5]
    axis = 1 if n_rows > n_cols else 0
    return jnp.where(
        place == 0,
        jnp.concatenate([kept, received], axis=axis),
        jnp.concatenate([received, kept], axis=axis),
    )


def solution(mesh):
    placed = (P(("row", "col"), None), P(), P("cand"), P("cand"), P(), P(), P(), P(), P(), P())
    return jax.shard_map(
        on_device, mesh=mesh, in_specs=placed, out_specs=P(("cand", "row"), "col"), check_vma=False
    )
```

time: 40.5 us -> 35.1 us (0.87)
  blocking collectives: 0 us -> 11.7 us
  starting transfers between devices: 12.8 us -> 1.66 us
  waiting for transfers between devices: 8.61 us -> 4.97 us
  local copies, waits for them, and re-layouts: 6.3 us -> 4.39 us
  Pallas kernels: 12.2 us -> 11.3 us
  other arithmetic: 0.08 us -> 0.7 us
    all_to_all x0 -> x1, blocking collectives: none -> 11.7 us  [on_device(): got = lax.all_to_all(copies, ('row', 'col'), 0, 0)]
    all_to_all x1 -> x0, starting transfers between devices: 6.47 us -> none  [gathered(): got = lax.all_to_all(copies, ('row', 'col'), 0, 0)]
    all_to_all x1 -> x0, waiting for transfers between devices: 4.71 us -> none  [gathered(): got = lax.all_to_all(copies, ('row', 'col'), 0, 0)]
    ppermute x2 -> x1, starting transfers between devices: 6.31 us -> 1.66 us  [on_device(): lax.ppermute(sent, ('row', 'col'), [(device, target[device]) for device i...]
    unnamed x26 -> x20, local copies, waits for them, and re-layouts: 6.15 us -> 4.39 us
    ppermute x2 -> x1, waiting for transfers between devices: 3.9 us -> 4.97 us  [on_device(): lax.ppermute(sent, ('row', 'col'), [(device, target[device]) for device i...]
    pallas_call x3 -> x2, Pallas kernels: 12.2 us -> 11.3 us  [the longest x1 9.82 us: block_scores(): pl.pallas_call(functools.partial(map_kernel, map_bins, size, table), out_...]
    select_n x0 -> x1, other arithmetic: none -> 0.7 us  [on_device(): jnp.where(place == 0, jnp.concatenate([kept, received], axis=axis), jnp.c...]
  transfers between devices with their start and end apart: 3 -> 1, of which waited for: 3 -> 1; matrix products, arithmetic and copies ran while one was open for 0% -> 0% of each run, Pallas kernels for 0% -> 0%
where the time goes in v1:
time: 35.1 us; the launch traced here: 34.7 us
  blocking collectives  11.7 us (33%)
  Pallas kernels  11.3 us (32%)
  waiting for transfers between devices  4.97 us (14%)
  local copies, waits for them, and re-layouts  4.39 us (13%)
  starting transfers between devices  1.66 us (5%)
  other arithmetic  0.7 us (2%)
    all_to_all x1, blocking collectives, on_device(): got = lax.all_to_all(copies, ('row', 'col'), 0, 0)  11.7 us
    pallas_call x1, Pallas kernels, block_scores(): pl.pallas_call(functools.partial(map_kernel, map_bins, size, table), out_...  9.82 us
    ppermute x1, waiting for transfers between devices, on_device(): lax.ppermute(sent, ('row', 'col'), [(device, target[device]) for device i...  4.97 us
    unnamed x20, local copies, waits for them, and re-layouts  4.39 us
    ppermute x1, starting transfers between devices, on_device(): lax.ppermute(sent, ('row', 'col'), [(device, target[device]) for device i...  1.66 us
    pallas_call x1, Pallas kernels, projected(): pl.pallas_call(functools.partial(project_kernel, map_bins), out_shape=(ja...  1.5 us
    select_n x1, other arithmetic, on_device(): jnp.where(place == 0, jnp.concatenate([kept, received], axis=axis), jnp.c...  0.7 us
  transfers between devices with their start and end apart: 1, of which 1 were waited for; matrix products, arithmetic and copies ran while one was open for 0% of the time, Pallas kernels for 0%

profile of v1, /device:TPU:4, one launch (start us, length us, event | category | flops | bytes accessed | tf_op | source)
XLA Modules:
  0.0 34.7 jit_solution(16789851611573253486)
XLA Ops:
  0.0 0.0 copy-start.9
  0.0 0.0 copy-start.6
  0.0 0.0 copy-start.7
  0.0 0.0 copy-start.8
  0.0 0.6 %copy-done.9 = bf16[128]{0:T(256)(128)(2,1)S(1)} copy-done((bf16[128]{0:T(256)(128)(2,1)S(1)}, bf16[128]{0:T(256)(128)(2,1)}, u32[]{:S(2)}) %copy-start.9) | copy-done | bytes 280
  0.7 0.0 copy-done.6
  0.7 0.0 copy-done.7
  0.7 0.0 copy-done.8
  0.7 0.0 copy-start
  0.7 1.0 %copy-done = bf16[128,1536]{1,0:T(8,128)(2,1)S(1)} copy-done((bf16[128,1536]{1,0:T(8,128)(2,1)S(1)}, bf16[128,1536]{1,0:T(8,128)(2,1)}, u32[]{:S(2)}) %copy-start) | copy-done | bytes 393240
  1.7 0.0 copy-start.1
  1.7 1.0 %copy-done.1 = bf16[1536,128]{1,0:T(8,128)(2,1)S(1)} copy-done((bf16[1536,128]{1,0:T(8,128)(2,1)S(1)}, bf16[1536,128]{1,0:T(8,128)(2,1)}, u32[]{:S(2)}) %copy-start.1) | copy-done | bytes 393240
  2.7 0.0 copy-start.2
  2.7 1.0 %copy-done.2 = bf16[1536,128]{1,0:T(8,128)(2,1)S(1)} copy-done((bf16[1536,128]{1,0:T(8,128)(2,1)S(1)}, bf16[1536,128]{1,0:T(8,128)(2,1)}, u32[]{:S(2)}) %copy-start.2) | copy-done | bytes 393240
  3.7 0.0 copy-start.5
  3.7 0.7 %copy-done.5 = bf16[4,1536]{1,0:T(4,128)(2,1)S(1)} copy-done((bf16[4,1536]{1,0:T(4,128)(2,1)S(1)}, bf16[4,1536]{1,0:T(4,128)(2,1)}, u32[]{:S(2)}) %copy-start.5) | copy-done | bytes 12312
  4.4 0.0 copy-start.3
  4.4 0.0 copy-start.4
  4.4 1.5 %shard_map.100 = (bf16[8,32,256]{2,1,0:T(8,128)(2,1)S(1)}, f32[544,128]{1,0:T(8,128)S(1)}, bf16[16,256]{1,0:T(8,128)(2,1)S(1)}) custom-call(bf16[128,1536]{1,0:T(8,128)(2,1)S(1)} %copy-done, bf16[4,1536]{1,0:T(4,128)(2,1)S(1)} %copy-done.5, s32[1,64]{1,0:T(1,128)S(1)} %bitcast.10, s32[1,64]{1,0:T(1,128)S(1)} %bitcast.11, bf16[1536,128]{1,0:T(8,128)(2,1)S(1)} %copy-done.1, ...), custom_call_target="tpu_custom_call" | custom-call | tf_op jit(solution)/shard_map/pallas_call | solution.py:157
  5.9 11.7 %all_to_all.5 = bf16[8,32,256]{2,1,0:T(8,128)(2,1)S(1)} all-to-all(bf16[8,32,256]{2,1,0:T(8,128)(2,1)S(1)} %get-tuple-element.10), channel_id=1, replica_groups=mesh['cand'=4,'row'=4,'col'=2] {'row','col'}, dimensions={0} | all-to-all | bytes 262144 | tf_op jit(solution)/shard_map/all_to_all | solution.py:346
  17.6 0.0 copy-done.3
  17.6 0.0 copy-done.4
  17.6 9.8 %shard_map.101 = (f32[64,64]{1,0:T(8,128)S(1)}, f32[64,64]{1,0:T(8,128)S(1)}) custom-call(bf16[256,256]{1,0:T(8,128)(2,1)S(1)} %bitcast.7, f32[544,128]{1,0:T(8,128)S(1)} %get-tuple-element.11.dist_table_ref, bf16[1152,128]{1,0:T(8,128)(2,1)S(1)} %bitcast.8, bf16[1152,128]{1,0:T(8,128)(2,1)S(1)} %bitcast.9, bf16[16,256]{1,0:T(8,128)(2,1)S(1)} %get-tuple-element.12.head_ref), custom_call_target="tpu_custom_call" | custom-call | tf_op jit(solution)/shard_map/pallas_call | solution.py:302
  27.4 1.7 %collective-permute-start = (f32[64,64]{1,0:T(8,128)S(1)}, f32[64,64]{1,0:T(8,128)S(1)}, u32[]{:S(2)}, u32[]{:S(2)}) collective-permute-start(f32[64,64]{1,0:T(8,128)S(1)} %get-tuple-element.14), channel_id=1, source_target_pairs={{0,2},{1,4},{2,0},{3,6},{4,3},{5,7},{6,1},{7,5},{8,10},{9,12},{10,... | collective-permute-start | bytes 49160 | tf_op jit(solution)/shard_map/ppermute | solution.py:349
  29.1 5.0 %collective-permute-done = f32[64,64]{1,0:T(8,128)S(1)} collective-permute-done((f32[64,64]{1,0:T(8,128)S(1)}, f32[64,64]{1,0:T(8,128)S(1)}, u32[]{:S(2)}, u32[]{:S(2)}) %collective-permute-start) | collective-permute-done | bytes 16416 | tf_op jit(solution)/shard_map/ppermute | solution.py:349
  34.0 0.7 %maximum_select_fusion = f32[64,128]{1,0:T(8,128)} fusion(f32[64,64]{1,0:T(8,128)S(1)} %collective-permute-done, f32[64,64]{1,0:T(8,128)S(1)} %get-tuple-element.13, pred[]{:T(512)S(6)} %eq.31), kind=kLoop, calls=%fused_computation | loop fusion | flops 24576 | bytes 65537 | tf_op jit(solution)/shard_map/jit(_where)/select_n | solution.py:352
Async XLA Ops:
  0.0 0.7 %copy-start.9 = (bf16[128]{0:T(256)(128)(2,1)S(1)}, bf16[128]{0:T(256)(128)(2,1)}, u32[]{:S(2)}) copy-start(bf16[128]{0:T(256)(128)(2,1)} %param.19) | copy-start | bytes 772
  0.0 0.7 %copy-start.6 = (s32[64]{0:T(128)S(1)}, s32[64]{0:T(128)}, u32[]{:S(2)}) copy-start(s32[64]{0:T(128)} %param.12) | copy-start | bytes 772
  0.0 0.7 %copy-start.7 = (s32[64]{0:T(128)S(1)}, s32[64]{0:T(128)}, u32[]{:S(2)}) copy-start(s32[64]{0:T(128)} %param.13) | copy-start | bytes 772
  0.0 0.7 %copy-start.8 = (f32[128]{0:T(128)S(1)}, f32[128]{0:T(128)}, u32[]{:S(2)}) copy-start(f32[128]{0:T(128)} %param.16) | copy-start | bytes 1540
  0.7 1.0 %copy-start = (bf16[128,1536]{1,0:T(8,128)(2,1)S(1)}, bf16[128,1536]{1,0:T(8,128)(2,1)}, u32[]{:S(2)}) copy-start(bf16[128,1536]{1,0:T(8,128)(2,1)} %embedding_hbm.1) | copy-start | bytes 1179652
  1.7 1.0 %copy-start.1 = (bf16[1536,128]{1,0:T(8,128)(2,1)S(1)}, bf16[1536,128]{1,0:T(8,128)(2,1)}, u32[]{:S(2)}) copy-start(bf16[1536,128]{1,0:T(8,128)(2,1)} %w_row_hbm.1) | copy-start | bytes 1179652
  2.7 1.0 %copy-start.2 = (bf16[1536,128]{1,0:T(8,128)(2,1)S(1)}, bf16[1536,128]{1,0:T(8,128)(2,1)}, u32[]{:S(2)}) copy-start(bf16[1536,128]{1,0:T(8,128)(2,1)} %w_col_hbm.1) | copy-start | bytes 1179652
  3.7 0.7 %copy-start.5 = (bf16[4,1536]{1,0:T(4,128)(2,1)S(1)}, bf16[4,1536]{1,0:T(4,128)(2,1)}, u32[]{:S(2)}) copy-start(bf16[4,1536]{1,0:T(4,128)(2,1)} %bases_hbm.1) | copy-start | bytes 36868
  4.4 13.2 %copy-start.3 = (bf16[3,3,128,128]{3,2,1,0:T(8,128)(2,1)S(1)}, bf16[3,3,128,128]{3,2,1,0:T(8,128)(2,1)}, u32[]{:S(2)}) copy-start(bf16[3,3,128,128]{3,2,1,0:T(8,128)(2,1)} %param.17) | copy-start | bytes 884740
  4.4 13.2 %copy-start.4 = (bf16[3,3,128,128]{3,2,1,0:T(8,128)(2,1)S(1)}, bf16[3,3,128,128]{3,2,1,0:T(8,128)(2,1)}, u32[]{:S(2)}) copy-start(bf16[3,3,128,128]{3,2,1,0:T(8,128)(2,1)} %param.18) | copy-start | bytes 884740
  27.4 6.6 %collective-permute-start = (f32[64,64]{1,0:T(8,128)S(1)}, f32[64,64]{1,0:T(8,128)S(1)}, u32[]{:S(2)}, u32[]{:S(2)}) collective-permute-start(f32[64,64]{1,0:T(8,128)S(1)} %get-tuple-element.14), channel_id=1, source_target_pairs={{0,2},{1,4},{2,0},{3,6},{4,3},{5,7},{6,1},{7,5},{8,10},{9,12},{10,... | collective-permute-start | bytes 49160 | tf_op jit(solution)/shard_map/ppermute | solution.py:349

commit v2 on v1

--- a/solution.py
+++ b/solution.py
@@ -164,7 +164,7 @@
         in_specs=[pl.BlockSpec(memory_space=pltpu.HBM)] * 8,
         out_specs=(vmem, vmem, vmem),
         scratch_shapes=[pltpu.VMEM(x.shape, x.dtype) for x in operands] + [pltpu.SemaphoreType.DMA((8,))],
-        compiler_params=pltpu.CompilerParams(vmem_limit_bytes=16 * 1024 * 1024),
+        compiler_params=pltpu.CompilerParams(vmem_limit_bytes=60 * 1024 * 1024),
     )(*operands)
 
 
@@ -173,8 +173,9 @@
     kept_ref, sent_ref, row_ref, col_ref, pair_ref, hidden_ref, pairs_one_ref, pairs_two_ref, score_ref,
 ):
     channels = dist_table_ref.shape[1]
-    block_wide = size + 2 * PAD
+    block_wide = size + 2 * SECOND_SPACING
     wide = 2 * block_wide
+    spread = block_wide + PAD
     breadth = 2 * size
     pair_rows = size + 2 * MARGIN
     hidden_rows = size + 2 * SECOND_SPACING
@@ -185,9 +186,9 @@
         (pl.multiple_of(row_a * size, size), pl.multiple_of(col_a * size, size)),
         (pl.multiple_of(row_b * size, size), pl.multiple_of(col_b * size, size)),
     ]
-    outside = jnp.full((PAD, channels), OUTSIDE, jnp.float32)
+    outside = jnp.full((2 * PAD, channels), OUTSIDE, jnp.float32)
     for part, ref in enumerate((row_ref, col_ref)):
-        ref[:PAD] = outside
+        ref[:PAD] = outside[:PAD]
         ref[PAD + map_bins :] = outside
         ref[PAD : PAD + map_bins] = proj_ref[:, part * channels : (part + 1) * channels].astype(
             jnp.float32
@@ -209,11 +210,15 @@
         values = []
         for row, col in blocks:
             row_part = row_ref[pl.ds(row + (PAD - MARGIN + p), 1)]
-            apart = dist_table_ref[pl.ds(col - row + (zero_apart - PAD + MARGIN - p), block_wide)]
-            values.append(relu(col_ref[pl.ds(col, block_wide)] + apart + row_part))
-        value = jnp.concatenate(values, axis=0)
-        shifted = [pltpu.roll(value, FIRST_SPACING, 0), value, pltpu.roll(value, wide - FIRST_SPACING, 0)]
-        pair_ref[p] = jnp.concatenate([x.astype(jnp.bfloat16) for x in shifted], axis=1)
+            apart = dist_table_ref[pl.ds(col - row + (zero_apart - p), spread)]
+            values.append(relu(col_ref[pl.ds(col + (PAD - MARGIN), spread)] + apart + row_part))
+        taps = []
+        for b in range(3):
+            moved = [
+                (pltpu.roll(x, spread - b * FIRST_SPACING, 0) if b else x)[:block_wide] for x in values
+            ]
+            taps.append(jnp.concatenate(moved, axis=0).astype(jnp.bfloat16))
+        pair_ref[p] = jnp.concatenate(taps, axis=1)
 
     def paired(ref, start, offsets, spacing, weight):
         lhs = jnp.concatenate(
@@ -241,9 +246,9 @@
                 before, middle, after = [], [], []
                 for b in range(2):
                     at = b * block_wide
-                    before += [ahead[at : at + PAD] * left[b], ahead[at + PAD : at + size]]
-                    middle += [value[at + PAD : at + PAD + size]]
-                    after += [ahead[at + PAD : at + size], ahead[at + size : at + size + PAD] * right[b]]
+                    before += [value[at : at + PAD] * left[b], value[at + PAD : at + size]]
+                    middle += [ahead[at : at + size]]
+                    after += [value[at + PAD : at + size], value[at + size : at + size + PAD] * right[b]]
                 hidden_ref[a] = jnp.concatenate(
                     [jnp.concatenate(x, axis=0).astype(jnp.bfloat16) for x in (before, middle, after)], axis=1
                 )
@@ -296,7 +301,7 @@
 def block_scores(every, dist_table, first_kernel, second_kernel, head, size, table):
     map_bins = every.shape[0]
     channels = dist_table.shape[1]
-    wide = 2 * (size + 2 * PAD)
+    wide = 2 * (size + 2 * SECOND_SPACING)
     vmem = pl.BlockSpec(memory_space=pltpu.VMEM)
     block = jax.ShapeDtypeStruct((size, size), jnp.float32)
     return pl.pallas_call(
@@ -305,8 +310,8 @@
         in_specs=[vmem] * 5,
         out_specs=(vmem, vmem),
         scratch_shapes=[
-            pltpu.VMEM((map_bins + 2 * PAD, channels), jnp.float32),
-            pltpu.VMEM((map_bins + 2 * PAD, channels), jnp.float32),
+            pltpu.VMEM((map_bins + 3 * PAD, channels), jnp.float32),
+            pltpu.VMEM((map_bins + 3 * PAD, channels), jnp.float32),
             pltpu.VMEM((size + 2 * MARGIN, wide, 3 * channels), jnp.bfloat16),
             pltpu.VMEM((size + 2 * SECOND_SPACING, 2 * size, 3 * channels), jnp.bfloat16),
             pltpu.VMEM((12 * channels, 2 * channels), jnp.bfloat16),

time: 35.1 us -> 33 us (0.940)
  local copies, waits for them, and re-layouts: 4.39 us -> 1.65 us
  Pallas kernels: 11.3 us -> 11.8 us
    unnamed x20 -> x8, local copies, waits for them, and re-layouts: 4.39 us -> 1.65 us
    pallas_call x1, Pallas kernels: 1.5 us -> 2.61 us  [projected(): pl.pallas_call(functools.partial(project_kernel, map_bins), out_shape=(ja...]
    pallas_call x1, Pallas kernels: 9.82 us -> 9.16 us  [block_scores(): pl.pallas_call(functools.partial(map_kernel, map_bins, size, table), out_...]
where the time goes in v2:
time: 33 us; the launch traced here: 32.6 us
  blocking collectives  11.9 us (36%)
  Pallas kernels  11.8 us (36%)
  waiting for transfers between devices  4.96 us (15%)
  starting transfers between devices  1.67 us (5%)
  local copies, waits for them, and re-layouts  1.65 us (5%)
  other arithmetic  0.7 us (2%)
    all_to_all x1, blocking collectives, on_device(): got = lax.all_to_all(copies, ('row', 'col'), 0, 0)  11.9 us
    pallas_call x1, Pallas kernels, block_scores(): pl.pallas_call(functools.partial(map_kernel, map_bins, size, table), out_...  9.16 us
    ppermute x1, waiting for transfers between devices, on_device(): lax.ppermute(sent, ('row', 'col'), [(device, target[device]) for device i...  4.96 us
    pallas_call x1, Pallas kernels, projected(): pl.pallas_call(functools.partial(project_kernel, map_bins), out_shape=(ja...  2.61 us
    ppermute x1, starting transfers between devices, on_device(): lax.ppermute(sent, ('row', 'col'), [(device, target[device]) for device i...  1.67 us
    unnamed x8, local copies, waits for them, and re-layouts  1.65 us
    select_n x1, other arithmetic, on_device(): jnp.where(place == 0, jnp.concatenate([kept, received], axis=axis), jnp.c...  0.7 us
  transfers between devices with their start and end apart: 1, of which 1 were waited for; matrix products, arithmetic and copies ran while one was open for 0% of the time, Pallas kernels for 0%

profile of v2, /device:TPU:4, one launch (start us, length us, event | category | flops | bytes accessed | tf_op | source)
XLA Modules:
  0.0 32.6 jit_solution(15919972985432630082)
XLA Ops:
  0.0 0.0 copy-start
  0.0 0.0 copy-start.1
  0.0 2.6 %shard_map.100 = (bf16[8,32,256]{2,1,0:T(8,128)(2,1)}, f32[544,128]{1,0:T(8,128)}, bf16[16,256]{1,0:T(8,128)(2,1)}) custom-call(bf16[128,1536]{1,0:T(8,128)(2,1)} %embedding_hbm.1, bf16[4,1536]{1,0:T(4,128)(2,1)} %bases_hbm.1, s32[1,64]{1,0:T(1,128)} %bitcast.10, s32[1,64]{1,0:T(1,128)} %bitcast.11, bf16[1536,128]{1,0:T(8,128)(2,1)} %w_row_hbm.1, ...), custom_call_target="tpu_custom_call" | custom-call | tf_op jit(solution)/shard_map/pallas_call | solution.py:157
  2.6 11.9 %all_to_all.5 = bf16[8,32,256]{2,1,0:T(8,128)(2,1)S(1)} all-to-all(bf16[8,32,256]{2,1,0:T(8,128)(2,1)} %get-tuple-element.10), channel_id=1, replica_groups=mesh['cand'=4,'row'=4,'col'=2] {'row','col'}, dimensions={0} | all-to-all | bytes 262144 | tf_op jit(solution)/shard_map/all_to_all | solution.py:351
  14.5 0.0 copy-start.3
  14.5 0.0 copy-done
  14.5 0.0 copy-done.1
  14.5 0.7 %copy-done.3 = bf16[16,256]{1,0:T(8,128)(2,1)S(1)} copy-done((bf16[16,256]{1,0:T(8,128)(2,1)S(1)}, bf16[16,256]{1,0:T(8,128)(2,1)}, u32[]{:S(2)}) %copy-start.3) | copy-done | bytes 8216
  15.2 0.0 copy-start.2
  15.2 1.0 %copy-done.2 = f32[544,128]{1,0:T(8,128)S(1)} copy-done((f32[544,128]{1,0:T(8,128)S(1)}, f32[544,128]{1,0:T(8,128)}, u32[]{:S(2)}) %copy-start.2) | copy-done | bytes 278552
  16.1 9.2 %shard_map.101 = (f32[64,64]{1,0:T(8,128)S(1)}, f32[64,64]{1,0:T(8,128)S(1)}) custom-call(bf16[256,256]{1,0:T(8,128)(2,1)S(1)} %bitcast.7, f32[544,128]{1,0:T(8,128)S(1)} %copy-done.2, bf16[1152,128]{1,0:T(8,128)(2,1)S(1)} %bitcast.8, bf16[1152,128]{1,0:T(8,128)(2,1)S(1)} %bitcast.9, bf16[16,256]{1,0:T(8,128)(2,1)S(1)} %copy-done.3), custom_call_target="tpu_custom_call" | custom-call | tf_op jit(solution)/shard_map/pallas_call | solution.py:307
  25.3 1.7 %collective-permute-start = (f32[64,64]{1,0:T(8,128)S(1)}, f32[64,64]{1,0:T(8,128)S(1)}, u32[]{:S(2)}, u32[]{:S(2)}) collective-permute-start(f32[64,64]{1,0:T(8,128)S(1)} %get-tuple-element.14), channel_id=1, source_target_pairs={{0,2},{1,4},{2,0},{3,6},{4,3},{5,7},{6,1},{7,5},{8,10},{9,12},{10,... | collective-permute-start | bytes 49160 | tf_op jit(solution)/shard_map/ppermute | solution.py:354
  27.0 5.0 %collective-permute-done = f32[64,64]{1,0:T(8,128)S(1)} collective-permute-done((f32[64,64]{1,0:T(8,128)S(1)}, f32[64,64]{1,0:T(8,128)S(1)}, u32[]{:S(2)}, u32[]{:S(2)}) %collective-permute-start) | collective-permute-done | bytes 16416 | tf_op jit(solution)/shard_map/ppermute | solution.py:354
  31.9 0.7 %maximum_select_fusion = f32[64,128]{1,0:T(8,128)} fusion(f32[64,64]{1,0:T(8,128)S(1)} %collective-permute-done, f32[64,64]{1,0:T(8,128)S(1)} %get-tuple-element.13, pred[]{:T(512)S(6)} %eq.31), kind=kLoop, calls=%fused_computation | loop fusion | flops 24576 | bytes 65537 | tf_op jit(solution)/shard_map/jit(_where)/select_n | solution.py:357
Async XLA Ops:
  0.0 14.5 %copy-start = (bf16[3,3,128,128]{3,2,1,0:T(8,128)(2,1)S(1)}, bf16[3,3,128,128]{3,2,1,0:T(8,128)(2,1)}, u32[]{:S(2)}) copy-start(bf16[3,3,128,128]{3,2,1,0:T(8,128)(2,1)} %param.17) | copy-start | bytes 884740
  0.0 14.5 %copy-start.1 = (bf16[3,3,128,128]{3,2,1,0:T(8,128)(2,1)S(1)}, bf16[3,3,128,128]{3,2,1,0:T(8,128)(2,1)}, u32[]{:S(2)}) copy-start(bf16[3,3,128,128]{3,2,1,0:T(8,128)(2,1)} %param.18) | copy-start | bytes 884740
  14.5 0.7 %copy-start.3 = (bf16[16,256]{1,0:T(8,128)(2,1)S(1)}, bf16[16,256]{1,0:T(8,128)(2,1)}, u32[]{:S(2)}) copy-start(bf16[16,256]{1,0:T(8,128)(2,1)} %get-tuple-element.12.head_ref) | copy-start | bytes 24580
  15.2 1.0 %copy-start.2 = (f32[544,128]{1,0:T(8,128)S(1)}, f32[544,128]{1,0:T(8,128)}, u32[]{:S(2)}) copy-start(f32[544,128]{1,0:T(8,128)} %get-tuple-element.11.dist_table_ref) | copy-start | bytes 835588
  25.3 6.6 %collective-permute-start = (f32[64,64]{1,0:T(8,128)S(1)}, f32[64,64]{1,0:T(8,128)S(1)}, u32[]{:S(2)}, u32[]{:S(2)}) collective-permute-start(f32[64,64]{1,0:T(8,128)S(1)} %get-tuple-element.14), channel_id=1, source_target_pairs={{0,2},{1,4},{2,0},{3,6},{4,3},{5,7},{6,1},{7,5},{8,10},{9,12},{10,... | collective-permute-start | bytes 49160 | tf_op jit(solution)/shard_map/ppermute | solution.py:354

commit v3 on v2

--- a/solution.py
+++ b/solution.py
@@ -164,8 +164,8 @@
         in_specs=[pl.BlockSpec(memory_space=pltpu.HBM)] * 8,
         out_specs=(vmem, vmem, vmem),
         scratch_shapes=[pltpu.VMEM(x.shape, x.dtype) for x in operands] + [pltpu.SemaphoreType.DMA((8,))],
-        compiler_params=pltpu.CompilerParams(vmem_limit_bytes=60 * 1024 * 1024),
-    )(*operands)
+        compiler_params=pltpu.CompilerParams(vmem_limit_bytes=16 * 1024 * 1024),
+    )(*(pltpu.with_memory_space_constraint(x, pltpu.HBM) for x in operands))
 
 
 def map_kernel(

time: 33 us -> 30.4 us (0.921)
  local copies, waits for them, and re-layouts: 1.65 us -> 0.01 us
  Pallas kernels: 11.8 us -> 11.2 us
    unnamed x8 -> x4, local copies, waits for them, and re-layouts: 1.65 us -> 0.01 us
    pallas_call x1, Pallas kernels: 2.61 us -> 1.95 us  [projected(): pl.pallas_call(functools.partial(project_kernel, map_bins), out_shape=(ja...]
where the time goes in v3:
time: 30.4 us; the launch traced here: 30.2 us
  blocking collectives  11.7 us (38%)
  Pallas kernels  11.2 us (37%)
  waiting for transfers between devices  4.97 us (16%)
  starting transfers between devices  1.66 us (5%)
  other arithmetic  0.7 us (2%)
    all_to_all x1, blocking collectives, on_device(): got = lax.all_to_all(copies, ('row', 'col'), 0, 0)  11.7 us
    pallas_call x1, Pallas kernels, block_scores(): pl.pallas_call(functools.partial(map_kernel, map_bins, size, table), out_...  9.2 us
    ppermute x1, waiting for transfers between devices, on_device(): lax.ppermute(sent, ('row', 'col'), [(device, target[device]) for device i...  4.97 us
    pallas_call x1, Pallas kernels, projected(): pl.pallas_call(functools.partial(project_kernel, map_bins), out_shape=(ja...  1.95 us
    ppermute x1, starting transfers between devices, on_device(): lax.ppermute(sent, ('row', 'col'), [(device, target[device]) for device i...  1.66 us
    select_n x1, other arithmetic, on_device(): jnp.where(place == 0, jnp.concatenate([kept, received], axis=axis), jnp.c...  0.7 us
  transfers between devices with their start and end apart: 1, of which 1 were waited for; matrix products, arithmetic and copies ran while one was open for 0% of the time, Pallas kernels for 0%

profile of v3, /device:TPU:4, one launch (start us, length us, event | category | flops | bytes accessed | tf_op | source)
XLA Modules:
  0.0 30.2 jit_solution(15203672067823279579)
XLA Ops:
  0.0 0.0 copy-start
  0.0 0.0 copy-start.1
  0.0 2.0 %shard_map.100 = (bf16[8,32,256]{2,1,0:T(8,128)(2,1)S(1)}, f32[544,128]{1,0:T(8,128)S(1)}, bf16[16,256]{1,0:T(8,128)(2,1)S(1)}) custom-call(bf16[128,1536]{1,0:T(8,128)(2,1)} %embedding_hbm.1, bf16[4,1536]{1,0:T(4,128)(2,1)} %bases_hbm.1, s32[1,64]{1,0:T(1,128)} %bitcast.10, s32[1,64]{1,0:T(1,128)} %bitcast.11, bf16[1536,128]{1,0:T(8,128)(2,1)} %w_row_hbm.1, ...), custom_call_target="tpu_custom_call" | custom-call | tf_op jit(solution)/shard_map/pallas_call | solution.py:157
  2.0 11.7 %all_to_all.5 = bf16[8,32,256]{2,1,0:T(8,128)(2,1)S(1)} all-to-all(bf16[8,32,256]{2,1,0:T(8,128)(2,1)S(1)} %get-tuple-element.10), channel_id=1, replica_groups=mesh['cand'=4,'row'=4,'col'=2] {'row','col'}, dimensions={0} | all-to-all | bytes 262144 | tf_op jit(solution)/shard_map/all_to_all | solution.py:351
  13.6 0.0 copy-done
  13.6 0.0 copy-done.1
  13.6 9.2 %shard_map.101 = (f32[64,64]{1,0:T(8,128)S(1)}, f32[64,64]{1,0:T(8,128)S(1)}) custom-call(bf16[256,256]{1,0:T(8,128)(2,1)S(1)} %bitcast.7, f32[544,128]{1,0:T(8,128)S(1)} %get-tuple-element.11.dist_table_ref, bf16[1152,128]{1,0:T(8,128)(2,1)S(1)} %bitcast.8, bf16[1152,128]{1,0:T(8,128)(2,1)S(1)} %bitcast.9, bf16[16,256]{1,0:T(8,128)(2,1)S(1)} %get-tuple-element.12.head_ref), custom_call_target="tpu_custom_call" | custom-call | tf_op jit(solution)/shard_map/pallas_call | solution.py:307
  22.8 1.7 %collective-permute-start = (f32[64,64]{1,0:T(8,128)S(1)}, f32[64,64]{1,0:T(8,128)S(1)}, u32[]{:S(2)}, u32[]{:S(2)}) collective-permute-start(f32[64,64]{1,0:T(8,128)S(1)} %get-tuple-element.14), channel_id=1, source_target_pairs={{0,2},{1,4},{2,0},{3,6},{4,3},{5,7},{6,1},{7,5},{8,10},{9,12},{10,... | collective-permute-start | bytes 49160 | tf_op jit(solution)/shard_map/ppermute | solution.py:354
  24.5 5.0 %collective-permute-done = f32[64,64]{1,0:T(8,128)S(1)} collective-permute-done((f32[64,64]{1,0:T(8,128)S(1)}, f32[64,64]{1,0:T(8,128)S(1)}, u32[]{:S(2)}, u32[]{:S(2)}) %collective-permute-start) | collective-permute-done | bytes 16416 | tf_op jit(solution)/shard_map/ppermute | solution.py:354
  29.5 0.7 %maximum_select_fusion = f32[64,128]{1,0:T(8,128)} fusion(f32[64,64]{1,0:T(8,128)S(1)} %collective-permute-done, f32[64,64]{1,0:T(8,128)S(1)} %get-tuple-element.13, pred[]{:T(512)S(6)} %eq.31), kind=kLoop, calls=%fused_computation | loop fusion | flops 24576 | bytes 65537 | tf_op jit(solution)/shard_map/jit(_where)/select_n | solution.py:357
Async XLA Ops:
  0.0 13.6 %copy-start = (bf16[3,3,128,128]{3,2,1,0:T(8,128)(2,1)S(1)}, bf16[3,3,128,128]{3,2,1,0:T(8,128)(2,1)}, u32[]{:S(2)}) copy-start(bf16[3,3,128,128]{3,2,1,0:T(8,128)(2,1)} %param.17) | copy-start | bytes 884740
  0.0 13.6 %copy-start.1 = (bf16[3,3,128,128]{3,2,1,0:T(8,128)(2,1)S(1)}, bf16[3,3,128,128]{3,2,1,0:T(8,128)(2,1)}, u32[]{:S(2)}) copy-start(bf16[3,3,128,128]{3,2,1,0:T(8,128)(2,1)} %param.18) | copy-start | bytes 884740
  22.8 6.6 %collective-permute-start = (f32[64,64]{1,0:T(8,128)S(1)}, f32[64,64]{1,0:T(8,128)S(1)}, u32[]{:S(2)}, u32[]{:S(2)}) collective-permute-start(f32[64,64]{1,0:T(8,128)S(1)} %get-tuple-element.14), channel_id=1, source_target_pairs={{0,2},{1,4},{2,0},{3,6},{4,3},{5,7},{6,1},{7,5},{8,10},{9,12},{10,... | collective-permute-start | bytes 49160 | tf_op jit(solution)/shard_map/ppermute | solution.py:354

commit v4 on v3

--- a/solution.py
+++ b/solution.py
@@ -15,6 +15,7 @@
 MARGIN = FIRST_SPACING + SECOND_SPACING
 PAD = 8
 GROUP = 8
+PAIRS_PER_DOT = 1
 OUTSIDE = -1e30
 
 
@@ -170,7 +171,7 @@
 
 def map_kernel(
     map_bins, size, table, proj_ref, dist_table_ref, first_ref, second_ref, head_ref,
-    kept_ref, sent_ref, row_ref, col_ref, pair_ref, hidden_ref, pairs_one_ref, pairs_two_ref, score_ref,
+    kept_ref, sent_ref, row_ref, col_ref, pair_ref, hidden_ref, pairs_one_ref, pairs_two_ref, score_ref, filled,
 ):
     channels = dist_table_ref.shape[1]
     block_wide = size + 2 * SECOND_SPACING
@@ -193,11 +194,14 @@
         ref[PAD : PAD + map_bins] = proj_ref[:, part * channels : (part + 1) * channels].astype(
             jnp.float32
         )
+    fills = []
     for ref, given in ((pairs_one_ref, first_ref), (pairs_two_ref, second_ref)):
-        ref[: 3 * depth, :channels] = given[...]
         ref[3 * depth :, :channels] = jnp.zeros((depth, channels), jnp.bfloat16)
         ref[:depth, channels:] = jnp.zeros((depth, channels), jnp.bfloat16)
-        ref[depth:, channels:] = given[...]
+        for half in range(2):
+            place = ref.at[pl.ds(half * depth, 3 * depth), pl.ds(half * channels, channels)]
+            fills.append(pltpu.make_async_copy(given, place, filled.at[len(fills)]))
+            fills[-1].start()
     zero_apart = dist_table_ref.shape[0] // 2
     at_edge = lax.broadcasted_iota(jnp.int32, (PAD, channels), 0)
     last_start = map_bins - size
@@ -221,20 +225,23 @@
         pair_ref[p] = jnp.concatenate(taps, axis=1)
 
     def paired(ref, start, offsets, spacing, weight):
-        lhs = jnp.concatenate(
-            [
+        parts = []
+        for n in range(0, len(offsets), PAIRS_PER_DOT):
+            rows = [
                 jnp.concatenate([ref[start + base + k * spacing] for k in range(4)], axis=1)
-                for base in offsets
-            ],
-            axis=0,
-        )
-        return jnp.dot(lhs, weight[...], preferred_element_type=jnp.float32)
+                for base in offsets[n : n + PAIRS_PER_DOT]
+            ]
+            lhs = rows[0] if len(rows) == 1 else jnp.concatenate(rows, axis=0)
+            out = jnp.dot(lhs, weight[...], preferred_element_type=jnp.float32)
+            height = out.shape[0] // len(rows)
+            parts += [out[k * height : (k + 1) * height] for k in range(len(rows))]
+        return parts
 
     def keep_hidden(start, offsets, out):
         for n, base in enumerate(offsets):
             for half in range(2):
                 a = start + base + half * FIRST_SPACING
-                conv = out[n * wide : (n + 1) * wide, half * channels : (half + 1) * channels]
+                conv = out[n][:, half * channels : (half + 1) * channels]
                 own = pair_ref[a + FIRST_SPACING, :, channels : 2 * channels].astype(jnp.float32)
                 value = own + relu(conv)
                 for rows, flags in ((a < edge, above), (a >= hidden_rows - edge, below)):
@@ -259,7 +266,7 @@
             halves = []
             for half in range(2):
                 o = start + base + half * edge
-                conv = out[n * breadth : (n + 1) * breadth, half * channels : (half + 1) * channels]
+                conv = out[n][:, half * channels : (half + 1) * channels]
                 own = hidden_ref[o + edge, :, channels : 2 * channels].astype(jnp.float32)
                 halves.append((own + relu(conv)).astype(jnp.bfloat16))
             last.append(jnp.concatenate(halves, axis=1))
@@ -277,6 +284,8 @@
     first_groups, second_groups = hidden_rows // GROUP, size // GROUP
     for p in range(2 * GROUP):
         build(p)
+    for fill in fills:
+        fill.wait()
     for s in range(first_groups + 1):
         one = two = None
         if s < first_groups:
@@ -317,6 +326,7 @@
             pltpu.VMEM((12 * channels, 2 * channels), jnp.bfloat16),
             pltpu.VMEM((12 * channels, 2 * channels), jnp.bfloat16),
             pltpu.VMEM((size, 2 * size), jnp.float32),
+            pltpu.SemaphoreType.DMA((4,)),
         ],
         compiler_params=pltpu.CompilerParams(vmem_limit_bytes=40 * 1024 * 1024),
     )(

time: 30.4 us -> 31.6 us (1.039)
  Pallas kernels: 11.2 us -> 12.3 us
    pallas_call x1, Pallas kernels: 9.2 us -> 10.4 us  [block_scores(): pl.pallas_call(functools.partial(map_kernel, map_bins, size, table), out_...]
where the time goes in v4:
time: 31.6 us; the launch traced here: 31.4 us
  Pallas kernels  12.3 us (39%)
  blocking collectives  11.7 us (37%)
  waiting for transfers between devices  4.98 us (16%)
  starting transfers between devices  1.68 us (5%)
  other arithmetic  0.7 us (2%)
    all_to_all x1, blocking collectives, on_device(): got = lax.all_to_all(copies, ('row', 'col'), 0, 0)  11.7 us
    pallas_call x1, Pallas kernels, block_scores(): pl.pallas_call(functools.partial(map_kernel, map_bins, size, table), out_...  10.4 us
    ppermute x1, waiting for transfers between devices, on_device(): lax.ppermute(sent, ('row', 'col'), [(device, target[device]) for device i...  4.98 us
    pallas_call x1, Pallas kernels, projected(): pl.pallas_call(functools.partial(project_kernel, map_bins), out_shape=(ja...  1.95 us
    ppermute x1, starting transfers between devices, on_device(): lax.ppermute(sent, ('row', 'col'), [(device, target[device]) for device i...  1.68 us
    select_n x1, other arithmetic, on_device(): jnp.where(place == 0, jnp.concatenate([kept, received], axis=axis), jnp.c...  0.7 us
  transfers between devices with their start and end apart: 1, of which 1 were waited for; matrix products, arithmetic and copies ran while one was open for 0% of the time, Pallas kernels for 0%

profile of v4, /device:TPU:4, one launch (start us, length us, event | category | flops | bytes accessed | tf_op | source)
XLA Modules:
  0.0 31.4 jit_solution(11529624802777595571)
XLA Ops:
  0.0 0.0 copy-start
  0.0 0.0 copy-start.1
  0.0 2.0 %shard_map.100 = (bf16[8,32,256]{2,1,0:T(8,128)(2,1)S(1)}, f32[544,128]{1,0:T(8,128)S(1)}, bf16[16,256]{1,0:T(8,128)(2,1)S(1)}) custom-call(bf16[128,1536]{1,0:T(8,128)(2,1)} %embedding_hbm.1, bf16[4,1536]{1,0:T(4,128)(2,1)} %bases_hbm.1, s32[1,64]{1,0:T(1,128)} %bitcast.10, s32[1,64]{1,0:T(1,128)} %bitcast.11, bf16[1536,128]{1,0:T(8,128)(2,1)} %w_row_hbm.1, ...), custom_call_target="tpu_custom_call" | custom-call | tf_op jit(solution)/shard_map/pallas_call | solution.py:158
  2.0 11.7 %all_to_all.5 = bf16[8,32,256]{2,1,0:T(8,128)(2,1)S(1)} all-to-all(bf16[8,32,256]{2,1,0:T(8,128)(2,1)S(1)} %get-tuple-element.10), channel_id=1, replica_groups=mesh['cand'=4,'row'=4,'col'=2] {'row','col'}, dimensions={0} | all-to-all | bytes 262144 | tf_op jit(solution)/shard_map/all_to_all | solution.py:361
  13.6 0.0 copy-done
  13.6 0.0 copy-done.1
  13.6 10.4 %shard_map.101 = (f32[64,64]{1,0:T(8,128)S(1)}, f32[64,64]{1,0:T(8,128)S(1)}) custom-call(bf16[256,256]{1,0:T(8,128)(2,1)S(1)} %bitcast.7, f32[544,128]{1,0:T(8,128)S(1)} %get-tuple-element.11.dist_table_ref, bf16[1152,128]{1,0:T(8,128)(2,1)S(1)} %bitcast.8, bf16[1152,128]{1,0:T(8,128)(2,1)S(1)} %bitcast.9, bf16[16,256]{1,0:T(8,128)(2,1)S(1)} %get-tuple-element.12.head_ref), custom_call_target="tpu_custom_call" | custom-call | tf_op jit(solution)/shard_map/pallas_call | solution.py:316
  24.0 1.7 %collective-permute-start = (f32[64,64]{1,0:T(8,128)S(1)}, f32[64,64]{1,0:T(8,128)S(1)}, u32[]{:S(2)}, u32[]{:S(2)}) collective-permute-start(f32[64,64]{1,0:T(8,128)S(1)} %get-tuple-element.14), channel_id=1, source_target_pairs={{0,2},{1,4},{2,0},{3,6},{4,3},{5,7},{6,1},{7,5},{8,10},{9,12},{10,... | collective-permute-start | bytes 49160 | tf_op jit(solution)/shard_map/ppermute | solution.py:364
  25.7 5.0 %collective-permute-done = f32[64,64]{1,0:T(8,128)S(1)} collective-permute-done((f32[64,64]{1,0:T(8,128)S(1)}, f32[64,64]{1,0:T(8,128)S(1)}, u32[]{:S(2)}, u32[]{:S(2)}) %collective-permute-start) | collective-permute-done | bytes 16416 | tf_op jit(solution)/shard_map/ppermute | solution.py:364
  30.7 0.7 %maximum_select_fusion = f32[64,128]{1,0:T(8,128)} fusion(f32[64,64]{1,0:T(8,128)S(1)} %collective-permute-done, f32[64,64]{1,0:T(8,128)S(1)} %get-tuple-element.13, pred[]{:T(512)S(6)} %eq.31), kind=kLoop, calls=%fused_computation | loop fusion | flops 24576 | bytes 65537 | tf_op jit(solution)/shard_map/jit(_where)/select_n | solution.py:367
Async XLA Ops:
  0.0 13.6 %copy-start = (bf16[3,3,128,128]{3,2,1,0:T(8,128)(2,1)S(1)}, bf16[3,3,128,128]{3,2,1,0:T(8,128)(2,1)}, u32[]{:S(2)}) copy-start(bf16[3,3,128,128]{3,2,1,0:T(8,128)(2,1)} %param.17) | copy-start | bytes 884740
  0.0 13.6 %copy-start.1 = (bf16[3,3,128,128]{3,2,1,0:T(8,128)(2,1)S(1)}, bf16[3,3,128,128]{3,2,1,0:T(8,128)(2,1)}, u32[]{:S(2)}) copy-start(bf16[3,3,128,128]{3,2,1,0:T(8,128)(2,1)} %param.18) | copy-start | bytes 884740
  24.0 6.7 %collective-permute-start = (f32[64,64]{1,0:T(8,128)S(1)}, f32[64,64]{1,0:T(8,128)S(1)}, u32[]{:S(2)}, u32[]{:S(2)}) collective-permute-start(f32[64,64]{1,0:T(8,128)S(1)} %get-tuple-element.14), channel_id=1, source_target_pairs={{0,2},{1,4},{2,0},{3,6},{4,3},{5,7},{6,1},{7,5},{8,10},{9,12},{10,... | collective-permute-start | bytes 49160 | tf_op jit(solution)/shard_map/ppermute | solution.py:364

commit v5 on v3

--- a/solution.py
+++ b/solution.py
@@ -169,8 +169,8 @@
 
 
 def map_kernel(
-    map_bins, size, table, proj_ref, dist_table_ref, first_ref, second_ref, head_ref,
-    kept_ref, sent_ref, row_ref, col_ref, pair_ref, hidden_ref, pairs_one_ref, pairs_two_ref, score_ref,
+    map_bins, size, table, proj_ref, dist_table_ref, weights_ref, head_ref,
+    kept_ref, sent_ref, row_ref, col_ref, pair_ref, pair_step_ref, hidden_ref, hidden_step_ref, score_ref,
 ):
     channels = dist_table_ref.shape[1]
     block_wide = size + 2 * SECOND_SPACING
@@ -179,7 +179,6 @@
     breadth = 2 * size
     pair_rows = size + 2 * MARGIN
     hidden_rows = size + 2 * SECOND_SPACING
-    depth = 3 * channels
     edge = SECOND_SPACING
     row_a, col_a, row_b, col_b, diagonal, _ = lookup(table)
     blocks = [
@@ -193,11 +192,6 @@
         ref[PAD : PAD + map_bins] = proj_ref[:, part * channels : (part + 1) * channels].astype(
             jnp.float32
         )
-    for ref, given in ((pairs_one_ref, first_ref), (pairs_two_ref, second_ref)):
-        ref[: 3 * depth, :channels] = given[...]
-        ref[3 * depth :, :channels] = jnp.zeros((depth, channels), jnp.bfloat16)
-        ref[:depth, channels:] = jnp.zeros((depth, channels), jnp.bfloat16)
-        ref[depth:, channels:] = given[...]
     zero_apart = dist_table_ref.shape[0] // 2
     at_edge = lax.broadcasted_iota(jnp.int32, (PAD, channels), 0)
     last_start = map_bins - size
@@ -219,24 +213,43 @@
             ]
             taps.append(jnp.concatenate(moved, axis=0).astype(jnp.bfloat16))
         pair_ref[p] = jnp.concatenate(taps, axis=1)
-
-    def paired(ref, start, offsets, spacing, weight):
-        lhs = jnp.concatenate(
-            [
-                jnp.concatenate([ref[start + base + k * spacing] for k in range(4)], axis=1)
+        if p >= 2 * FIRST_SPACING:
+            before = p - 2 * FIRST_SPACING
+            pair_step_ref[before] = pair_ref[before] - pair_ref[p]
+
+    def four_rows(ref, step_ref, start, offsets, spacing, weights):
+        def pairs_of(source, k):
+            rows = [
+                jnp.concatenate(
+                    [source[start + base + k * spacing], source[start + base + (k + 1) * spacing]], axis=1
+                )
                 for base in offsets
-            ],
-            axis=0,
-        )
-        return jnp.dot(lhs, weight[...], preferred_element_type=jnp.float32)
+            ]
+            return jnp.concatenate(rows, axis=0)
+
+        def times(lhs, which):
+            return jnp.dot(lhs, weights_ref[weights, which], preferred_element_type=jnp.float32)
+
+        shared = times(pairs_of(ref, 2), 1)
+        low = times(pairs_of(step_ref, 0), 0)
+        high = times(pairs_of(step_ref, 2), 2)
+        tall = shared.shape[0] // len(offsets)
+        found = []
+        for n in range(len(offsets)):
+            rows = []
+            for k in range(4):
+                down = slice(n * tall, (n + 1) * tall)
+                across = slice((k % 2) * channels, (k % 2 + 1) * channels)
+                rows.append((low if k < 2 else high)[down, across] + shared[down, across])
+            found.append(rows)
+        return found
 
     def keep_hidden(start, offsets, out):
         for n, base in enumerate(offsets):
-            for half in range(2):
-                a = start + base + half * FIRST_SPACING
-                conv = out[n * wide : (n + 1) * wide, half * channels : (half + 1) * channels]
+            for k in range(4):
+                a = start + base + k * FIRST_SPACING
                 own = pair_ref[a + FIRST_SPACING, :, channels : 2 * channels].astype(jnp.float32)
-                value = own + relu(conv)
+                value = own + relu(out[n][k])
                 for rows, flags in ((a < edge, above), (a >= hidden_rows - edge, below)):
                     if rows:
                         value = jnp.concatenate(
@@ -252,43 +265,48 @@
                 hidden_ref[a] = jnp.concatenate(
                     [jnp.concatenate(x, axis=0).astype(jnp.bfloat16) for x in (before, middle, after)], axis=1
                 )
+        for a in range(start, start + GROUP):
+            if a >= 2 * edge:
+                hidden_step_ref[a - 2 * edge] = hidden_ref[a - 2 * edge] - hidden_ref[a]
 
     def keep_score(start, offsets, out):
         last = []
         for n, base in enumerate(offsets):
-            halves = []
-            for half in range(2):
-                o = start + base + half * edge
-                conv = out[n * breadth : (n + 1) * breadth, half * channels : (half + 1) * channels]
+            rows = []
+            for k in range(4):
+                o = start + base + k * edge
                 own = hidden_ref[o + edge, :, channels : 2 * channels].astype(jnp.float32)
-                halves.append((own + relu(conv)).astype(jnp.bfloat16))
-            last.append(jnp.concatenate(halves, axis=1))
+                rows.append((own + relu(out[n][k])).astype(jnp.bfloat16))
+            last += [jnp.concatenate(rows[:2], axis=1), jnp.concatenate(rows[2:], axis=1)]
         got = lax.dot_general(
             head_ref[...],
             jnp.concatenate(last, axis=0),
             (((1,), (1,)), ((), ())),
             preferred_element_type=jnp.float32,
         )
-        count = len(offsets)
-        lines = [got[half : half + 1, n * breadth : (n + 1) * breadth] for half in range(2) for n in range(count)]
-        score_ref[start : start + 8] = jnp.concatenate(lines, axis=0)
-
-    first_offsets, second_offsets = (0, 1, 4, 5), (0, 1, 2, 3)
-    first_groups, second_groups = hidden_rows // GROUP, size // GROUP
+        lines = []
+        for k in range(4):
+            for n in range(len(offsets)):
+                at = (2 * n + k // 2) * breadth
+                lines.append(got[k % 2 : k % 2 + 1, at : at + breadth])
+        score_ref[start : start + 2 * GROUP] = jnp.concatenate(lines, axis=0)
+
+    first_offsets, second_offsets = (0, 1), (0, 1, 2, 3)
+    first_groups = hidden_rows // GROUP
     for p in range(2 * GROUP):
         build(p)
     for s in range(first_groups + 1):
         one = two = None
         if s < first_groups:
-            one = paired(pair_ref, s * GROUP, first_offsets, FIRST_SPACING, pairs_one_ref)
+            one = four_rows(pair_ref, pair_step_ref, s * GROUP, first_offsets, FIRST_SPACING, 0)
         for p in range((s + 2) * GROUP, min((s + 3) * GROUP, pair_rows)):
             build(p)
-        if 0 <= s - 2 < second_groups:
-            two = paired(hidden_ref, (s - 2) * GROUP, second_offsets, SECOND_SPACING, pairs_two_ref)
+        if s >= 3 and s % 2 == 1:
+            two = four_rows(hidden_ref, hidden_step_ref, (s - 3) * GROUP, second_offsets, edge, 1)
         if one is not None:
             keep_hidden(s * GROUP, first_offsets, one)
         if two is not None:
-            keep_score((s - 2) * GROUP, second_offsets, two)
+            keep_score((s - 3) * GROUP, second_offsets, two)
     score = score_ref[...]
     turned = score.T
     first, second = score[:, :size], score[:, size:]
@@ -298,7 +316,34 @@
     sent_ref[...] = 0.5 * (second + jnp.where(alone, turned_second, turned_first))
 
 
-def block_scores(every, dist_table, first_kernel, second_kernel, head, size, table):
+def weights_kernel(first_ref, second_ref, weights_ref):
+    depth = weights_ref.shape[2] // 2
+    channels = weights_ref.shape[3] // 2
+    for n, ref in enumerate((first_ref, second_ref)):
+        g0, g1, g2 = (ref[a * depth : (a + 1) * depth] for a in range(3))
+        both = (g0.astype(jnp.float32) + g2.astype(jnp.float32)).astype(jnp.bfloat16)
+        none = jnp.zeros_like(g0)
+        for which, quarters in enumerate(
+            ((g0, none, g1, g0), (both, g1, g1, both), (-g2, -g1, none, -g2))
+        ):
+            for q, quarter in enumerate(quarters):
+                down, across = (q // 2) * depth, (q % 2) * channels
+                weights_ref[n, which, down : down + depth, across : across + channels] = quarter
+
+
+def combined_weights(first_kernel, second_kernel):
+    channels = first_kernel.shape[3]
+    vmem = pl.BlockSpec(memory_space=pltpu.VMEM)
+    return pl.pallas_call(
+        weights_kernel,
+        out_shape=jax.ShapeDtypeStruct((2, 3, 6 * channels, 2 * channels), jnp.bfloat16),
+        in_specs=[vmem] * 2,
+        out_specs=vmem,
+        compiler_params=pltpu.CompilerParams(vmem_limit_bytes=8 * 1024 * 1024),
+    )(first_kernel.reshape(9 * channels, channels), second_kernel.reshape(9 * channels, channels))
+
+
+def block_scores(every, dist_table, weights, head, size, table):
     map_bins = every.shape[0]
     channels = dist_table.shape[1]
     wide = 2 * (size + 2 * SECOND_SPACING)
@@ -307,25 +352,19 @@
     return pl.pallas_call(
         functools.partial(map_kernel, map_bins, size, table),
         out_shape=(block, block),
-        in_specs=[vmem] * 5,
+        in_specs=[vmem] * 4,
         out_specs=(vmem, vmem),
         scratch_shapes=[
             pltpu.VMEM((map_bins + 3 * PAD, channels), jnp.float32),
             pltpu.VMEM((map_bins + 3 * PAD, channels), jnp.float32),
             pltpu.VMEM((size + 2 * MARGIN, wide, 3 * channels), jnp.bfloat16),
+            pltpu.VMEM((size + 2 * SECOND_SPACING, wide, 3 * channels), jnp.bfloat16),
             pltpu.VMEM((size + 2 * SECOND_SPACING, 2 * size, 3 * channels), jnp.bfloat16),
-            pltpu.VMEM((12 * channels, 2 * channels), jnp.bfloat16),
-            pltpu.VMEM((12 * channels, 2 * channels), jnp.bfloat16),
+            pltpu.VMEM((size, 2 * size, 3 * channels), jnp.bfloat16),
             pltpu.VMEM((size, 2 * size), jnp.float32),
         ],
         compiler_params=pltpu.CompilerParams(vmem_limit_bytes=40 * 1024 * 1024),
-    )(
-        every,
-        dist_table,
-        first_kernel.reshape(9 * channels, channels),
-        second_kernel.reshape(9 * channels, channels),
-        head,
-    )
+    )(every, dist_table, weights, head)
 
 
 def on_device(
@@ -350,7 +389,8 @@
     )
     got = lax.all_to_all(copies, ("row", "col"), 0, 0)
     every = got.reshape(map_bins, got.shape[2])
-    kept, sent = block_scores(every, dist_table, first_kernel, second_kernel, head, size, table)
+    weights = combined_weights(first_kernel, second_kernel)
+    kept, sent = block_scores(every, dist_table, weights, head, size, table)
     received = lax.ppermute(sent, ("row", "col"), [(device, target[device]) for device in range(devices)])
     place = lookup(table)[5]
     axis = 1 if n_rows > n_cols else 0

time: 30.4 us -> 32 us (1.053)
  blocking collectives: 11.7 us -> 0 us
  starting transfers between devices: 1.66 us -> 8.01 us
  waiting for transfers between devices: 4.97 us -> 8.23 us
  local copies, waits for them, and re-layouts: 0.01 us -> 1.92 us
  Pallas kernels: 11.2 us -> 12.8 us
    all_to_all x1 -> x0, blocking collectives: 11.7 us -> none  [on_device(): got = lax.all_to_all(copies, ('row', 'col'), 0, 0)]
    all_to_all x0 -> x1, starting transfers between devices: none -> 6.34 us  [on_device(): got = lax.all_to_all(copies, ('row', 'col'), 0, 0)]
    all_to_all x0 -> x1, waiting for transfers between devices: none -> 3.26 us  [on_device(): got = lax.all_to_all(copies, ('row', 'col'), 0, 0)]
    unnamed x4, local copies, waits for them, and re-layouts: 0.01 us -> 1.92 us
    pallas_call x1, Pallas kernels: 9.2 us -> 9.94 us  [block_scores(): pl.pallas_call(functools.partial(map_kernel, map_bins, size, table), out_...]
    pallas_call x1, Pallas kernels: 1.95 us -> 2.54 us  [projected(): pl.pallas_call(functools.partial(project_kernel, map_bins), out_shape=(ja...]
    pallas_call x0 -> x1, Pallas kernels: none -> 0.35 us  [combined_weights(): pl.pallas_call(weights_kernel, out_shape=jax.ShapeDtypeStruct((2, 3, 6 *...]
  transfers between devices with their start and end apart: 1 -> 2, of which waited for: 1 -> 2; matrix products, arithmetic and copies ran while one was open for 0% -> 0% of each run, Pallas kernels for 0% -> 1%
where the time goes in v5:
time: 32 us; the launch traced here: 31.7 us
  Pallas kernels  12.8 us (40%)
  waiting for transfers between devices  8.23 us (26%)
  starting transfers between devices  8.01 us (25%)
  local copies, waits for them, and re-layouts  1.92 us (6%)
  other arithmetic  0.7 us (2%)
    pallas_call x1, Pallas kernels, block_scores(): pl.pallas_call(functools.partial(map_kernel, map_bins, size, table), out_...  9.94 us
    all_to_all x1, starting transfers between devices, on_device(): got = lax.all_to_all(copies, ('row', 'col'), 0, 0)  6.34 us
    ppermute x1, waiting for transfers between devices, on_device(): lax.ppermute(sent, ('row', 'col'), [(device, target[device]) for device i...  4.97 us
    all_to_all x1, waiting for transfers between devices, on_device(): got = lax.all_to_all(copies, ('row', 'col'), 0, 0)  3.26 us
    pallas_call x1, Pallas kernels, projected(): pl.pallas_call(functools.partial(project_kernel, map_bins), out_shape=(ja...  2.54 us
    unnamed x4, local copies, waits for them, and re-layouts  1.92 us
    ppermute x1, starting transfers between devices, on_device(): lax.ppermute(sent, ('row', 'col'), [(device, target[device]) for device i...  1.66 us
    select_n x1, other arithmetic, on_device(): jnp.where(place == 0, jnp.concatenate([kept, received], axis=axis), jnp.c...  0.7 us
  transfers between devices with their start and end apart: 2, of which 2 were waited for; matrix products, arithmetic and copies ran while one was open for 0% of the time, Pallas kernels for 1%

profile of v5, /device:TPU:4, one launch (start us, length us, event | category | flops | bytes accessed | tf_op | source)
XLA Modules:
  0.0 31.7 jit_solution(11611037389738544898)
XLA Ops:
  0.0 2.5 %shard_map.100 = (bf16[8,32,256]{2,1,0:T(8,128)(2,1)}, f32[544,128]{1,0:T(8,128)S(1)}, bf16[16,256]{1,0:T(8,128)(2,1)S(1)}) custom-call(bf16[128,1536]{1,0:T(8,128)(2,1)} %embedding_hbm.1, bf16[4,1536]{1,0:T(4,128)(2,1)} %bases_hbm.1, s32[1,64]{1,0:T(1,128)} %bitcast.10, s32[1,64]{1,0:T(1,128)} %bitcast.11, bf16[1536,128]{1,0:T(8,128)(2,1)} %w_row_hbm.1, ...), custom_call_target="tpu_custom_call" | custom-call | tf_op jit(solution)/shard_map/pallas_call | solution.py:157
  2.5 6.3 %all-to-all-start = ((bf16[8,32,256]{2,1,0:T(8,128)(2,1)}), bf16[8,32,256]{2,1,0:T(8,128)(2,1)S(1)}, u32[]{:S(2)}, u32[]{:S(2)}) async-start(bf16[8,32,256]{2,1,0:T(8,128)(2,1)} %get-tuple-element.10), calls=%async_computation | async-start | bytes 262144 | tf_op jit(solution)/shard_map/all_to_all | solution.py:390
  8.9 0.0 copy-start
  8.9 1.0 %copy-done = bf16[3,3,128,128]{3,2,1,0:T(8,128)(2,1)S(1)} copy-done((bf16[3,3,128,128]{3,2,1,0:T(8,128)(2,1)S(1)}, bf16[3,3,128,128]{3,2,1,0:T(8,128)(2,1)}, u32[]{:S(2)}) %copy-start) | copy-done | bytes 294936
  9.9 0.0 copy-start.1
  9.9 1.0 %copy-done.1 = bf16[3,3,128,128]{3,2,1,0:T(8,128)(2,1)S(1)} copy-done((bf16[3,3,128,128]{3,2,1,0:T(8,128)(2,1)S(1)}, bf16[3,3,128,128]{3,2,1,0:T(8,128)(2,1)}, u32[]{:S(2)}) %copy-start.1) | copy-done | bytes 294936
  10.8 0.3 %shard_map.101.weights_ref = bf16[2,3,768,256]{3,2,1,0:T(8,128)(2,1)S(1)} custom-call(bf16[1152,128]{1,0:T(8,128)(2,1)S(1)} %bitcast.8, bf16[1152,128]{1,0:T(8,128)(2,1)S(1)} %bitcast.9), custom_call_target="tpu_custom_call" | custom-call | tf_op jit(solution)/shard_map/pallas_call | solution.py:337
  11.2 3.3 %all-to-all-done = bf16[8,32,256]{2,1,0:T(8,128)(2,1)S(1)} async-done(((bf16[8,32,256]{2,1,0:T(8,128)(2,1)}), bf16[8,32,256]{2,1,0:T(8,128)(2,1)S(1)}, u32[]{:S(2)}, u32[]{:S(2)}) %all-to-all-start) | async-done | bytes 131104 | tf_op jit(solution)/shard_map/all_to_all | solution.py:390
  14.4 9.9 %shard_map.102 = (f32[64,64]{1,0:T(8,128)S(1)}, f32[64,64]{1,0:T(8,128)S(1)}) custom-call(bf16[256,256]{1,0:T(8,128)(2,1)S(1)} %bitcast.7, f32[544,128]{1,0:T(8,128)S(1)} %get-tuple-element.11.dist_table_ref, bf16[2,3,768,256]{3,2,1,0:T(8,128)(2,1)S(1)} %shard_map.101.weights_ref, bf16[16,256]{1,0:T(8,128)(2,1)S(1)} %get-tuple-element.12.head_ref), custom_call_target="tpu_custom_call" | custom-call | tf_op jit(solution)/shard_map/pallas_call | solution.py:352
  24.4 1.7 %collective-permute-start = (f32[64,64]{1,0:T(8,128)S(1)}, f32[64,64]{1,0:T(8,128)S(1)}, u32[]{:S(2)}, u32[]{:S(2)}) collective-permute-start(f32[64,64]{1,0:T(8,128)S(1)} %get-tuple-element.14), channel_id=1, source_target_pairs={{0,2},{1,4},{2,0},{3,6},{4,3},{5,7},{6,1},{7,5},{8,10},{9,12},{10,... | collective-permute-start | bytes 49160 | tf_op jit(solution)/shard_map/ppermute | solution.py:394
  26.0 5.0 %collective-permute-done = f32[64,64]{1,0:T(8,128)S(1)} collective-permute-done((f32[64,64]{1,0:T(8,128)S(1)}, f32[64,64]{1,0:T(8,128)S(1)}, u32[]{:S(2)}, u32[]{:S(2)}) %collective-permute-start) | collective-permute-done | bytes 16416 | tf_op jit(solution)/shard_map/ppermute | solution.py:394
  31.0 0.7 %maximum_select_fusion = f32[64,128]{1,0:T(8,128)} fusion(f32[64,64]{1,0:T(8,128)S(1)} %collective-permute-done, f32[64,64]{1,0:T(8,128)S(1)} %get-tuple-element.13, pred[]{:T(512)S(6)} %eq.31), kind=kLoop, calls=%fused_computation | loop fusion | flops 24576 | bytes 65537 | tf_op jit(solution)/shard_map/jit(_where)/select_n | solution.py:397
Async XLA Ops:
  2.5 11.9 %all-to-all-start = ((bf16[8,32,256]{2,1,0:T(8,128)(2,1)}), bf16[8,32,256]{2,1,0:T(8,128)(2,1)S(1)}, u32[]{:S(2)}, u32[]{:S(2)}) async-start(bf16[8,32,256]{2,1,0:T(8,128)(2,1)} %get-tuple-element.10), calls=%async_computation | async-start | bytes 262144 | tf_op jit(solution)/shard_map/all_to_all | solution.py:390
  8.9 1.0 %copy-start = (bf16[3,3,128,128]{3,2,1,0:T(8,128)(2,1)S(1)}, bf16[3,3,128,128]{3,2,1,0:T(8,128)(2,1)}, u32[]{:S(2)}) copy-start(bf16[3,3,128,128]{3,2,1,0:T(8,128)(2,1)} %param.17) | copy-start | bytes 884740
  9.9 1.0 %copy-start.1 = (bf16[3,3,128,128]{3,2,1,0:T(8,128)(2,1)S(1)}, bf16[3,3,128,128]{3,2,1,0:T(8,128)(2,1)}, u32[]{:S(2)}) copy-start(bf16[3,3,128,128]{3,2,1,0:T(8,128)(2,1)} %param.18) | copy-start | bytes 884740
  24.4 6.6 %collective-permute-start = (f32[64,64]{1,0:T(8,128)S(1)}, f32[64,64]{1,0:T(8,128)S(1)}, u32[]{:S(2)}, u32[]{:S(2)}) collective-permute-start(f32[64,64]{1,0:T(8,128)S(1)} %get-tuple-element.14), channel_id=1, source_target_pairs={{0,2},{1,4},{2,0},{3,6},{4,3},{5,7},{6,1},{7,5},{8,10},{9,12},{10,... | collective-permute-start | bytes 49160 | tf_op jit(solution)/shard_map/ppermute | solution.py:394

commit v6 on v4

v6 whole, which is shorter than its diff:
```python
import functools
import math

import jax
import jax.numpy as jnp
from jax import lax
from jax.experimental import pallas as pl
from jax.experimental.pallas import tpu as pltpu
from jax.sharding import PartitionSpec as P

POOL = 4
FIRST_SPACING = 2
SECOND_SPACING = 4
BASES = 4
MARGIN = FIRST_SPACING + SECOND_SPACING
PAD = 8
GROUP = 8
OUTSIDE = -1e30


def plan(n_rows, n_cols):
    wide = n_rows > n_cols
    blocks = max(n_rows, n_cols)
    assert blocks == 2 * min(n_rows, n_cols)

    def owner(i, j):
        return i * n_cols + j // 2 if wide else (i // 2) * n_cols + j

    held = {}
    for i in range(blocks):
        for j in range(blocks):
            held.setdefault(owner(i, j), []).append((i, j))

    def other(device, block):
        return next(b for b in held[device] if b != block)

    jobs, target = {}, {}

    def assign(device, kept, sent):
        place = held[device].index(kept)
        jobs[device] = (*kept, *sent, int(kept[0] == kept[1]), place)
        target[device] = owner(*sent)

    def walk(device, block):
        while device not in jobs:
            if block[0] == block[1]:
                return device, block
            sent = (block[1], block[0])
            assign(device, block, sent)
            device = owner(*sent)
            block = other(device, sent)
        return None, None

    for d in range(blocks):
        start = owner(d, d)
        if start not in jobs:
            end, last = walk(start, other(start, (d, d)))
            assign(end, last, (d, d))
    for device in sorted(held):
        if device not in jobs:
            walk(device, held[device][0])
    return [jobs[device] for device in sorted(jobs)], target


def tiles_of(size):
    return (size + 2 * PAD) // 4


def relu(x):
    return jnp.maximum(x, 0.0)


def lookup(table):
    n_cols = lax.axis_size("col")
    here = lax.axis_index("row") * n_cols + lax.axis_index("col")
    found = []
    for values in zip(*table):
        value = jnp.int32(values[0])
        for device in range(1, len(values)):
            value = jnp.where(here == device, jnp.int32(values[device]), value)
        found.append(value)
    return found


def project_kernel(
    map_bins, size, table, embedding_hbm, bases_hbm, pos_hbm, tok_hbm, w_row_hbm, w_col_hbm, gain_hbm, head_hbm,
    copies_ref, dist_ref, head_ref,
    embedding_ref, bases_ref, pos_ref, tok_ref, w_row_ref, w_col_ref, gain_ref, weight_ref, arrived,
):
    moves = [
        pltpu.make_async_copy(source, target, arrived.at[n])
        for n, (source, target) in enumerate(
            (
                (embedding_hbm, embedding_ref),
                (w_row_hbm, w_row_ref),
                (w_col_hbm, w_col_ref),
                (pos_hbm, pos_ref),
                (tok_hbm, tok_ref),
                (bases_hbm, bases_ref),
                (gain_hbm, gain_ref),
                (head_hbm, weight_ref),
            )
        )
    ]
    for move in moves:
        move.start()
    got_embedding, got_w_row, got_w_col, *small = moves
    shard_bins = embedding_ref.shape[0]
    copies, pooled_bins, _ = copies_ref.shape
    channels = gain_ref.shape[1]
    edits = pos_ref.shape[1]
    row_a, col_a, row_b, col_b, _, _ = lookup(table)
    phases, count, _ = dist_ref.shape
    at = lax.broadcasted_iota(jnp.int32, (count, channels), 0)
    lane = at & 7
    start = jnp.where((lane & 2) == 0, (col_a - row_a) * size, (col_b - row_b) * size)
    start = start + 4 * (at >> 3) + 2 * (lane >> 2) + (lane & 1) - 2 - 4 * ((size + 2 * MARGIN) // 4 - 1)
    feature = [
        jnp.log1p(jnp.abs(start - phase).astype(jnp.float32)) * (1.0 / math.log(map_bins))
        for phase in range(phases)
    ]
    first_bin = (lax.axis_index("row") * lax.axis_size("col") + lax.axis_index("col")) * shard_bins
    bins = first_bin + lax.broadcasted_iota(jnp.int32, (pooled_bins, edits), 0) * POOL
    back = lax.broadcasted_iota(jnp.int32, (pooled_bins, shard_bins), 1) - POOL * (
        lax.broadcasted_iota(jnp.int32, (pooled_bins, shard_bins), 0)
    )
    take = ((back >= 0) & (back < POOL)).astype(jnp.float32).astype(jnp.bfloat16)
    for move in small:
        move.wait()
    for phase in range(phases):
        dist_ref[phase] = gain_ref[...] * feature[phase]
    weight = jnp.concatenate([weight_ref[...].astype(jnp.float32)] * 2, axis=1)
    line = lax.broadcasted_iota(jnp.int32, head_ref.shape, 0)
    half = lax.broadcasted_iota(jnp.int32, head_ref.shape, 1) >= channels
    head_ref[...] = jnp.where(line == half.astype(jnp.int32), weight, 0.0).astype(jnp.bfloat16)
    ahead = pos_ref[...] - bins
    in_bin = ((ahead >= 0) & (ahead < POOL)).astype(jnp.float32)
    edited = None
    for base in range(BASES):
        is_base = (tok_ref[...] == base).astype(jnp.float32)
        count = jnp.sum(in_bin * is_base, axis=1, keepdims=True)
        term = count * bases_ref[base : base + 1].astype(jnp.float32)
        edited = term if edited is None else edited + term
    got_embedding.wait()
    summed = edited + jnp.dot(take, embedding_ref[...], preferred_element_type=jnp.float32)
    pooled = (summed * (1.0 / POOL)).astype(jnp.bfloat16)
    sides = []
    for move, ref in ((got_w_row, w_row_ref), (got_w_col, w_col_ref)):
        move.wait()
        sides.append(jnp.dot(pooled, ref[...], preferred_element_type=jnp.float32).astype(jnp.bfloat16))
    both = jnp.concatenate(sides, axis=1)
    for k in range(copies):
        copies_ref[k] = both


def projected(embedding, bases_table, edit_pos, edit_tok, w_row, w_col, dist_gain, head_weight, map_bins, copies, size, table):
    vmem = pl.BlockSpec(memory_space=pltpu.VMEM)
    operands = (
        embedding,
        bases_table,
        edit_pos[None],
        edit_tok[None],
        w_row,
        w_col,
        dist_gain[None],
        head_weight[None],
    )
    channels = w_row.shape[1]
    return pl.pallas_call(
        functools.partial(project_kernel, map_bins, size, table),
        out_shape=(
            jax.ShapeDtypeStruct((copies, embedding.shape[0] // POOL, 2 * channels), jnp.bfloat16),
            jax.ShapeDtypeStruct((4, 8 * (tiles_of(size) + (size + 2 * MARGIN) // 4 - 1), channels), jnp.float32),
            jax.ShapeDtypeStruct((16, 2 * channels), jnp.bfloat16),
        ),
        in_specs=[pl.BlockSpec(memory_space=pltpu.HBM)] * 8,
        out_specs=(vmem, vmem, vmem),
        scratch_shapes=[pltpu.VMEM(x.shape, x.dtype) for x in operands] + [pltpu.SemaphoreType.DMA((8,))],
        compiler_params=pltpu.CompilerParams(vmem_limit_bytes=16 * 1024 * 1024),
    )(*(pltpu.with_memory_space_constraint(x, pltpu.HBM) for x in operands))


def map_kernel(
    map_bins, size, table, proj_ref, dist_ref, first_ref, second_ref, head_ref,
    kept_ref, sent_ref, row_ref, col_ref, own_ref, moved_ref, hidden_ref, pairs_one_ref, pairs_two_ref,
    mixed_ref, score_ref, filled,
):
    channels = head_ref.shape[1] // 2
    tiles = tiles_of(size)
    wide = 16 * (tiles - 2)
    breadth = 4 * size
    pair_rows = size + 2 * MARGIN
    couples = pair_rows // 2
    hidden_couples = size // 2 + SECOND_SPACING
    depth = 3 * channels
    row_a, col_a, row_b, col_b, diagonal, _ = lookup(table)
    rows, cols = (row_a * size, row_b * size), (col_a * size, col_b * size)
    fills = []
    for ref, given in ((pairs_one_ref, first_ref), (pairs_two_ref, second_ref)):
        ref[3 * depth :, :channels] = jnp.zeros((depth, channels), jnp.bfloat16)
        ref[:depth, channels:] = jnp.zeros((depth, channels), jnp.bfloat16)
        for half in range(2):
            place = ref.at[pl.ds(half * depth, 3 * depth), pl.ds(half * channels, channels)]
            fills.append(pltpu.make_async_copy(given, place, filled.at[len(fills)]))
            fills[-1].start()

    def of_block(lane, values):
        return jnp.where((lane & 2) == 0, values[0], values[1])

    def spread(ref, part, offset, along):
        count = ref.shape[0]
        at = lax.broadcasted_iota(jnp.int32, (count, map_bins), 0)
        lane = at & 7
        bins = along(at >> 3, lane) + of_block(lane, offset)
        hot = (bins == lax.broadcasted_iota(jnp.int32, (count, map_bins), 1)).astype(jnp.float32)
        found = jnp.dot(
            hot.astype(jnp.bfloat16),
            proj_ref[:, part * channels : (part + 1) * channels],
            preferred_element_type=jnp.float32,
        )
        bins = bins[:, :channels]
        ref[...] = jnp.where((bins >= 0) & (bins < map_bins), found, OUTSIDE)

    spread(col_ref, 1, cols, lambda tile, lane: 4 * tile + 2 * (lane >> 2) + (lane & 1) - PAD)
    spread(row_ref, 0, rows, lambda row, lane: row - MARGIN)
    lane = lax.broadcasted_iota(jnp.int32, (16, channels), 0) & 7
    last_start = map_bins - size
    left = of_block(lane, [jnp.where(col > 0, 1.0, 0.0) for col in cols])
    right = of_block(lane, [jnp.where(col < last_start, 1.0, 0.0) for col in cols])
    above = of_block(lane, [jnp.where(row > 0, 1.0, 0.0) for row in rows])
    below = of_block(lane, [jnp.where(row < last_start, 1.0, 0.0) for row in rows])

    def couple(two):
        parts = [x.reshape(-1, 1, 8, channels) for x in two]
        return jnp.concatenate(parts, axis=1).reshape(-1, channels).astype(jnp.bfloat16)

    def build(c):
        values, ahead = [], []
        for p in (2 * c, 2 * c + 1):
            at = 8 * (pair_rows // 4 - 1 - p // 4)
            apart = dist_ref[p % 4, at : at + 8 * tiles]
            line = jnp.concatenate([row_ref[8 * p : 8 * p + 8]] * tiles, axis=0)
            value = relu(col_ref[...] + apart + line)
            values.append(value[8 : 8 * (tiles - 1)])
            ahead.append(pltpu.roll(value, 8 * tiles - 4, 0)[: 8 * (tiles - 1)])
        own_ref[c] = couple(values)
        moved_ref[c] = couple(ahead)

    def paired(taps, bases, step, weight):
        lhs = [
            jnp.concatenate([tap for k in range(4) for tap in taps(base + k * step)], axis=1) for base in bases
        ]
        out = jnp.dot(jnp.concatenate(lhs, axis=0), weight[...], preferred_element_type=jnp.float32)
        tall = out.shape[0] // len(bases)
        return [
            [out[n * tall : (n + 1) * tall, half * channels : (half + 1) * channels] for half in range(2)]
            for n in range(len(bases))
        ]

    def first_taps(c):
        return moved_ref[c, :wide], own_ref[c], moved_ref[c, 16 : wide + 16]

    def second_taps(c):
        return tuple(hidden_ref[c, 16 * b : 16 * b + breadth] for b in range(3))

    def keep_hidden(bases, out):
        for n, base in enumerate(bases):
            for half in range(2):
                c = base + half
                value = own_ref[c + 1].astype(jnp.float32) + relu(out[n][half])
                for edge, flags in ((c < 2, above), (c >= hidden_couples - 2, below)):
                    if edge:
                        value = value * jnp.concatenate([flags] * (tiles - 2), axis=0)
                value = jnp.concatenate(
                    [value[:16] * left, value[16 : wide - 16], value[wide - 16 :] * right], axis=0
                )
                hidden_ref[c] = value.astype(jnp.bfloat16)

    def keep_score(bases, out):
        last = []
        for n, base in enumerate(bases):
            halves = []
            for half in range(2):
                own = hidden_ref[base + 2 * half + 2, 16 : 16 + breadth].astype(jnp.float32)
                halves.append((own + relu(out[n][half])).astype(jnp.bfloat16))
            last.append(jnp.concatenate(halves, axis=1))
        got = lax.dot_general(
            head_ref[...],
            jnp.concatenate(last, axis=0),
            (((1,), (1,)), ((), ())),
            preferred_element_type=jnp.float32,
        )
        lines = [got[half : half + 1, n * breadth : (n + 1) * breadth] for half in range(2) for n in range(2)]
        mixed_ref[bases[0] : bases[0] + 4] = jnp.concatenate(lines, axis=0)

    first_groups, second_groups = hidden_couples // 4, size // 8
    for c in range(8):
        build(c)
    for fill in fills:
        fill.wait()
    for s in range(first_groups + 1):
        one = two = None
        first_bases, second_bases = (4 * s, 4 * s + 2), (4 * (s - 2), 4 * (s - 2) + 1)
        if s < first_groups:
            one = paired(first_taps, first_bases, 1, pairs_one_ref)
        for c in range(4 * (s + 2), min(4 * (s + 3), couples)):
            build(c)
        if 0 <= s - 2 < second_groups:
            two = paired(second_taps, second_bases, 2, pairs_two_ref)
        if one is not None:
            keep_hidden(first_bases, one)
        if two is not None:
            keep_score(second_bases, two)
    source = lax.broadcasted_iota(jnp.int32, (breadth, breadth), 0)
    place = ((source >> 3) & 1) * (2 * size) + ((source >> 1) & 1) * size
    place = place + 4 * (source >> 4) + 2 * ((source >> 2) & 1) + (source & 1)
    order = (place == lax.broadcasted_iota(jnp.int32, (breadth, breadth), 1)).astype(jnp.float32)
    order = order.astype(jnp.bfloat16)
    rest, ordered = mixed_ref[...], None
    for _ in range(3):
        piece = rest.astype(jnp.bfloat16)
        rest = rest - piece.astype(jnp.float32)
        moved = jnp.dot(piece, order, preferred_element_type=jnp.float32)
        ordered = moved if ordered is None else ordered + moved
    for row in range(2):
        score_ref[pl.ds(row, size // 2, 2)] = ordered[:, row * 2 * size : (row + 1) * 2 * size]
    score = score_ref[...]
    turned = score.T
    first, second = score[:, :size], score[:, size:]
    turned_first, turned_second = turned[:size], turned[size:]
    alone = diagonal == 1
    kept_ref[...] = 0.5 * (first + jnp.where(alone, turned_first, turned_second))
    sent_ref[...] = 0.5 * (second + jnp.where(alone, turned_second, turned_first))


def block_scores(every, dist_table, first_kernel, second_kernel, head, size, table):
    map_bins = every.shape[0]
    channels = dist_table.shape[2]
    tiles = tiles_of(size)
    pair_rows = size + 2 * MARGIN
    vmem = pl.BlockSpec(memory_space=pltpu.VMEM)
    block = jax.ShapeDtypeStruct((size, size), jnp.float32)
    return pl.pallas_call(
        functools.partial(map_kernel, map_bins, size, table),
        out_shape=(block, block),
        in_specs=[vmem] * 5,
        out_specs=(vmem, vmem),
        scratch_shapes=[
            pltpu.VMEM((8 * pair_rows, channels), jnp.float32),
            pltpu.VMEM((8 * tiles, channels), jnp.float32),
            pltpu.VMEM((pair_rows // 2, 16 * (tiles - 2), channels), jnp.bfloat16),
            pltpu.VMEM((pair_rows // 2, 16 * (tiles - 1), channels), jnp.bfloat16),
            pltpu.VMEM((size // 2 + SECOND_SPACING, 16 * (tiles - 2), channels), jnp.bfloat16),
            pltpu.VMEM((12 * channels, 2 * channels), jnp.bfloat16),
            pltpu.VMEM((12 * channels, 2 * channels), jnp.bfloat16),
            pltpu.VMEM((size // 2, 4 * size), jnp.float32),
            pltpu.VMEM((size, 2 * size), jnp.float32),
            pltpu.SemaphoreType.DMA((4,)),
        ],
        compiler_params=pltpu.CompilerParams(vmem_limit_bytes=40 * 1024 * 1024),
    )(
        every,
        dist_table,
        first_kernel.reshape(9 * channels, channels),
        second_kernel.reshape(9 * channels, channels),
        head,
    )


def on_device(
    embedding,
    bases_table,
    edit_pos,
    edit_tok,
    w_row,
    w_col,
    dist_gain,
    first_kernel,
    second_kernel,
    head_weight,
):
    n_rows, n_cols = lax.axis_size("row"), lax.axis_size("col")
    devices = n_rows * n_cols
    map_bins = embedding.shape[0] * devices // POOL
    table, target = plan(n_rows, n_cols)
    size = map_bins // max(n_rows, n_cols)
    copies, dist_table, head = projected(
        embedding, bases_table, edit_pos, edit_tok, w_row, w_col, dist_gain, head_weight, map_bins, devices, size, table
    )
    got = lax.all_to_all(copies, ("row", "col"), 0, 0)
    every = got.reshape(map_bins, got.shape[2])
    kept, sent = block_scores(every, dist_table, first_kernel, second_kernel, head, size, table)
    received = lax.ppermute(sent, ("row", "col"), [(device, target[device]) for device in range(devices)])
    place = lookup(table)[5]
    axis = 1 if n_rows > n_cols else 0
    return jnp.where(
        place == 0,
        jnp.concatenate([kept, received], axis=axis),
        jnp.concatenate([received, kept], axis=axis),
    )


def solution(mesh):
    placed = (P(("row", "col"), None), P(), P("cand"), P("cand"), P(), P(), P(), P(), P(), P())
    return jax.shard_map(
        on_device, mesh=mesh, in_specs=placed, out_specs=P(("cand", "row"), "col"), check_vma=False
    )
```

time: 31.6 us -> 31.4 us (level)
  no operation moved by 1% of the time
where the time goes in v6:
time: 31.4 us; the launch traced here: 31.2 us
  Pallas kernels  12.1 us (39%)
  blocking collectives  11.7 us (37%)
  waiting for transfers between devices  4.97 us (16%)
  starting transfers between devices  1.69 us (5%)
  other arithmetic  0.7 us (2%)
    all_to_all x1, blocking collectives, on_device(): got = lax.all_to_all(copies, ('row', 'col'), 0, 0)  11.7 us
    pallas_call x1, Pallas kernels, block_scores(): pl.pallas_call(functools.partial(map_kernel, map_bins, size, table), out_...  10.1 us
    ppermute x1, waiting for transfers between devices, on_device(): lax.ppermute(sent, ('row', 'col'), [(device, target[device]) for device i...  4.97 us
    pallas_call x1, Pallas kernels, projected(): pl.pallas_call(functools.partial(project_kernel, map_bins, size, table),...  1.98 us
    ppermute x1, starting transfers between devices, on_device(): lax.ppermute(sent, ('row', 'col'), [(device, target[device]) for device i...  1.69 us
    select_n x1, other arithmetic, on_device(): jnp.where(place == 0, jnp.concatenate([kept, received], axis=axis), jnp.c...  0.7 us
  transfers between devices with their start and end apart: 1, of which 1 were waited for; matrix products, arithmetic and copies ran while one was open for 0% of the time, Pallas kernels for 0%

profile of v6, /device:TPU:4, one launch (start us, length us, event | category | flops | bytes accessed | tf_op | source)
XLA Modules:
  0.0 31.2 jit_solution(13115889661018252731)
XLA Ops:
  0.0 0.0 copy-start
  0.0 0.0 copy-start.1
  0.0 2.0 %shard_map.100 = (bf16[8,32,256]{2,1,0:T(8,128)(2,1)S(1)}, f32[4,304,128]{2,1,0:T(8,128)S(1)}, bf16[16,256]{1,0:T(8,128)(2,1)S(1)}) custom-call(bf16[128,1536]{1,0:T(8,128)(2,1)} %embedding_hbm.1, bf16[4,1536]{1,0:T(4,128)(2,1)} %bases_hbm.1, s32[1,64]{1,0:T(1,128)} %bitcast.10, s32[1,64]{1,0:T(1,128)} %bitcast.11, bf16[1536,128]{1,0:T(8,128)(2,1)} %w_row_hbm.1, ...), custom_call_target="tpu_custom_call" | custom-call | tf_op jit(solution)/shard_map/pallas_call | solution.py:169
  2.0 11.7 %all_to_all.5 = bf16[8,32,256]{2,1,0:T(8,128)(2,1)S(1)} all-to-all(bf16[8,32,256]{2,1,0:T(8,128)(2,1)S(1)} %get-tuple-element.10), channel_id=1, replica_groups=mesh['cand'=4,'row'=4,'col'=2] {'row','col'}, dimensions={0} | all-to-all | bytes 262144 | tf_op jit(solution)/shard_map/all_to_all | solution.py:390
  13.7 0.0 copy-done
  13.7 0.0 copy-done.1
  13.7 10.1 %shard_map.101 = (f32[64,64]{1,0:T(8,128)S(1)}, f32[64,64]{1,0:T(8,128)S(1)}) custom-call(bf16[256,256]{1,0:T(8,128)(2,1)S(1)} %bitcast.7, f32[4,304,128]{2,1,0:T(8,128)S(1)} %get-tuple-element.11.dist_ref, bf16[1152,128]{1,0:T(8,128)(2,1)S(1)} %bitcast.8, bf16[1152,128]{1,0:T(8,128)(2,1)S(1)} %bitcast.9, bf16[16,256]{1,0:T(8,128)(2,1)S(1)} %get-tuple-element.12.head_ref), custom_call_target="tpu_custom_call" | custom-call | tf_op jit(solution)/shard_map/pallas_call | solution.py:343
  23.8 1.7 %collective-permute-start = (f32[64,64]{1,0:T(8,128)S(1)}, f32[64,64]{1,0:T(8,128)S(1)}, u32[]{:S(2)}, u32[]{:S(2)}) collective-permute-start(f32[64,64]{1,0:T(8,128)S(1)} %get-tuple-element.14), channel_id=1, source_target_pairs={{0,2},{1,4},{2,0},{3,6},{4,3},{5,7},{6,1},{7,5},{8,10},{9,12},{10,... | collective-permute-start | bytes 49160 | tf_op jit(solution)/shard_map/ppermute | solution.py:393
  25.5 5.0 %collective-permute-done = f32[64,64]{1,0:T(8,128)S(1)} collective-permute-done((f32[64,64]{1,0:T(8,128)S(1)}, f32[64,64]{1,0:T(8,128)S(1)}, u32[]{:S(2)}, u32[]{:S(2)}) %collective-permute-start) | collective-permute-done | bytes 16416 | tf_op jit(solution)/shard_map/ppermute | solution.py:393
  30.5 0.7 %maximum_select_fusion = f32[64,128]{1,0:T(8,128)} fusion(f32[64,64]{1,0:T(8,128)S(1)} %collective-permute-done, f32[64,64]{1,0:T(8,128)S(1)} %get-tuple-element.13, pred[]{:T(512)S(6)} %eq.31), kind=kLoop, calls=%fused_computation | loop fusion | flops 24576 | bytes 65537 | tf_op jit(solution)/shard_map/jit(_where)/select_n | solution.py:396
Async XLA Ops:
  0.0 13.7 %copy-start = (bf16[3,3,128,128]{3,2,1,0:T(8,128)(2,1)S(1)}, bf16[3,3,128,128]{3,2,1,0:T(8,128)(2,1)}, u32[]{:S(2)}) copy-start(bf16[3,3,128,128]{3,2,1,0:T(8,128)(2,1)} %param.17) | copy-start | bytes 884740
  0.0 13.7 %copy-start.1 = (bf16[3,3,128,128]{3,2,1,0:T(8,128)(2,1)S(1)}, bf16[3,3,128,128]{3,2,1,0:T(8,128)(2,1)}, u32[]{:S(2)}) copy-start(bf16[3,3,128,128]{3,2,1,0:T(8,128)(2,1)} %param.18) | copy-start | bytes 884740
  23.8 6.7 %collective-permute-start = (f32[64,64]{1,0:T(8,128)S(1)}, f32[64,64]{1,0:T(8,128)S(1)}, u32[]{:S(2)}, u32[]{:S(2)}) collective-permute-start(f32[64,64]{1,0:T(8,128)S(1)} %get-tuple-element.14), channel_id=1, source_target_pairs={{0,2},{1,4},{2,0},{3,6},{4,3},{5,7},{6,1},{7,5},{8,10},{9,12},{10,... | collective-permute-start | bytes 49160 | tf_op jit(solution)/shard_map/ppermute | solution.py:393

commit v7 on v6

--- a/solution.py
+++ b/solution.py
@@ -183,7 +183,7 @@
 def map_kernel(
     map_bins, size, table, proj_ref, dist_ref, first_ref, second_ref, head_ref,
     kept_ref, sent_ref, row_ref, col_ref, own_ref, moved_ref, hidden_ref, pairs_one_ref, pairs_two_ref,
-    mixed_ref, score_ref, filled,
+    mixed_ref, score_ref,
 ):
     channels = head_ref.shape[1] // 2
     tiles = tiles_of(size)
@@ -195,14 +195,11 @@
     depth = 3 * channels
     row_a, col_a, row_b, col_b, diagonal, _ = lookup(table)
     rows, cols = (row_a * size, row_b * size), (col_a * size, col_b * size)
-    fills = []
     for ref, given in ((pairs_one_ref, first_ref), (pairs_two_ref, second_ref)):
         ref[3 * depth :, :channels] = jnp.zeros((depth, channels), jnp.bfloat16)
         ref[:depth, channels:] = jnp.zeros((depth, channels), jnp.bfloat16)
-        for half in range(2):
-            place = ref.at[pl.ds(half * depth, 3 * depth), pl.ds(half * channels, channels)]
-            fills.append(pltpu.make_async_copy(given, place, filled.at[len(fills)]))
-            fills[-1].start()
+        ref[: 3 * depth, :channels] = given[...]
+        ref[depth:, channels:] = given[...]
 
     def of_block(lane, values):
         return jnp.where((lane & 2) == 0, values[0], values[1])
@@ -296,8 +293,6 @@
     first_groups, second_groups = hidden_couples // 4, size // 8
     for c in range(8):
         build(c)
-    for fill in fills:
-        fill.wait()
     for s in range(first_groups + 1):
         one = two = None
         first_bases, second_bases = (4 * s, 4 * s + 2), (4 * (s - 2), 4 * (s - 2) + 1)
@@ -355,7 +350,6 @@
             pltpu.VMEM((12 * channels, 2 * channels), jnp.bfloat16),
             pltpu.VMEM((size // 2, 4 * size), jnp.float32),
             pltpu.VMEM((size, 2 * size), jnp.float32),
-            pltpu.SemaphoreType.DMA((4,)),
         ],
         compiler_params=pltpu.CompilerParams(vmem_limit_bytes=40 * 1024 * 1024),
     )(

time: 31.4 us -> 30.9 us (0.984)
  Pallas kernels: 12.1 us -> 11.6 us
    pallas_call x1, Pallas kernels: 10.1 us -> 9.6 us  [block_scores(): pl.pallas_call(functools.partial(map_kernel, map_bins, size, table), out_...]
where the time goes in v7:
time: 30.9 us; the launch traced here: 30.6 us
  blocking collectives  11.7 us (38%)
  Pallas kernels  11.6 us (38%)
  waiting for transfers between devices  4.97 us (16%)
  starting transfers between devices  1.66 us (5%)
  other arithmetic  0.7 us (2%)
    all_to_all x1, blocking collectives, on_device(): got = lax.all_to_all(copies, ('row', 'col'), 0, 0)  11.7 us
    pallas_call x1, Pallas kernels, block_scores(): pl.pallas_call(functools.partial(map_kernel, map_bins, size, table), out_...  9.6 us
    ppermute x1, waiting for transfers between devices, on_device(): lax.ppermute(sent, ('row', 'col'), [(device, target[device]) for device i...  4.97 us
    pallas_call x1, Pallas kernels, projected(): pl.pallas_call(functools.partial(project_kernel, map_bins, size, table),...  1.98 us
    ppermute x1, starting transfers between devices, on_device(): lax.ppermute(sent, ('row', 'col'), [(device, target[device]) for device i...  1.66 us
    select_n x1, other arithmetic, on_device(): jnp.where(place == 0, jnp.concatenate([kept, received], axis=axis), jnp.c...  0.7 us
  transfers between devices with their start and end apart: 1, of which 1 were waited for; matrix products, arithmetic and copies ran while one was open for 0% of the time, Pallas kernels for 0%

profile of v7, /device:TPU:4, one launch (start us, length us, event | category | flops | bytes accessed | tf_op | source)
XLA Modules:
  0.0 30.6 jit_solution(7581057841612930251)
XLA Ops:
  0.0 0.0 copy-start
  0.0 0.0 copy-start.1
  0.0 2.0 %shard_map.100 = (bf16[8,32,256]{2,1,0:T(8,128)(2,1)S(1)}, f32[4,304,128]{2,1,0:T(8,128)S(1)}, bf16[16,256]{1,0:T(8,128)(2,1)S(1)}) custom-call(bf16[128,1536]{1,0:T(8,128)(2,1)} %embedding_hbm.1, bf16[4,1536]{1,0:T(4,128)(2,1)} %bases_hbm.1, s32[1,64]{1,0:T(1,128)} %bitcast.10, s32[1,64]{1,0:T(1,128)} %bitcast.11, bf16[1536,128]{1,0:T(8,128)(2,1)} %w_row_hbm.1, ...), custom_call_target="tpu_custom_call" | custom-call | tf_op jit(solution)/shard_map/pallas_call | solution.py:169
  2.0 11.7 %all_to_all.5 = bf16[8,32,256]{2,1,0:T(8,128)(2,1)S(1)} all-to-all(bf16[8,32,256]{2,1,0:T(8,128)(2,1)S(1)} %get-tuple-element.10), channel_id=1, replica_groups=mesh['cand'=4,'row'=4,'col'=2] {'row','col'}, dimensions={0} | all-to-all | bytes 262144 | tf_op jit(solution)/shard_map/all_to_all | solution.py:384
  13.7 0.0 copy-done
  13.7 0.0 copy-done.1
  13.7 9.6 %shard_map.101 = (f32[64,64]{1,0:T(8,128)S(1)}, f32[64,64]{1,0:T(8,128)S(1)}) custom-call(bf16[256,256]{1,0:T(8,128)(2,1)S(1)} %bitcast.7, f32[4,304,128]{2,1,0:T(8,128)S(1)} %get-tuple-element.11.dist_ref, bf16[1152,128]{1,0:T(8,128)(2,1)S(1)} %bitcast.8, bf16[1152,128]{1,0:T(8,128)(2,1)S(1)} %bitcast.9, bf16[16,256]{1,0:T(8,128)(2,1)S(1)} %get-tuple-element.12.head_ref), custom_call_target="tpu_custom_call" | custom-call | tf_op jit(solution)/shard_map/pallas_call | solution.py:338
  23.3 1.7 %collective-permute-start = (f32[64,64]{1,0:T(8,128)S(1)}, f32[64,64]{1,0:T(8,128)S(1)}, u32[]{:S(2)}, u32[]{:S(2)}) collective-permute-start(f32[64,64]{1,0:T(8,128)S(1)} %get-tuple-element.14), channel_id=1, source_target_pairs={{0,2},{1,4},{2,0},{3,6},{4,3},{5,7},{6,1},{7,5},{8,10},{9,12},{10,... | collective-permute-start | bytes 49160 | tf_op jit(solution)/shard_map/ppermute | solution.py:387
  24.9 5.0 %collective-permute-done = f32[64,64]{1,0:T(8,128)S(1)} collective-permute-done((f32[64,64]{1,0:T(8,128)S(1)}, f32[64,64]{1,0:T(8,128)S(1)}, u32[]{:S(2)}, u32[]{:S(2)}) %collective-permute-start) | collective-permute-done | bytes 16416 | tf_op jit(solution)/shard_map/ppermute | solution.py:387
  29.9 0.7 %maximum_select_fusion = f32[64,128]{1,0:T(8,128)} fusion(f32[64,64]{1,0:T(8,128)S(1)} %collective-permute-done, f32[64,64]{1,0:T(8,128)S(1)} %get-tuple-element.13, pred[]{:T(512)S(6)} %eq.31), kind=kLoop, calls=%fused_computation | loop fusion | flops 24576 | bytes 65537 | tf_op jit(solution)/shard_map/jit(_where)/select_n | solution.py:390
Async XLA Ops:
  0.0 13.7 %copy-start = (bf16[3,3,128,128]{3,2,1,0:T(8,128)(2,1)S(1)}, bf16[3,3,128,128]{3,2,1,0:T(8,128)(2,1)}, u32[]{:S(2)}) copy-start(bf16[3,3,128,128]{3,2,1,0:T(8,128)(2,1)} %param.17) | copy-start | bytes 884740
  0.0 13.7 %copy-start.1 = (bf16[3,3,128,128]{3,2,1,0:T(8,128)(2,1)S(1)}, bf16[3,3,128,128]{3,2,1,0:T(8,128)(2,1)}, u32[]{:S(2)}) copy-start(bf16[3,3,128,128]{3,2,1,0:T(8,128)(2,1)} %param.18) | copy-start | bytes 884740
  23.3 6.6 %collective-permute-start = (f32[64,64]{1,0:T(8,128)S(1)}, f32[64,64]{1,0:T(8,128)S(1)}, u32[]{:S(2)}, u32[]{:S(2)}) collective-permute-start(f32[64,64]{1,0:T(8,128)S(1)} %get-tuple-element.14), channel_id=1, source_target_pairs={{0,2},{1,4},{2,0},{3,6},{4,3},{5,7},{6,1},{7,5},{8,10},{9,12},{10,... | collective-permute-start | bytes 49160 | tf_op jit(solution)/shard_map/ppermute | solution.py:387

commit v8 on v7

--- a/solution.py
+++ b/solution.py
@@ -247,7 +247,8 @@
         lhs = [
             jnp.concatenate([tap for k in range(4) for tap in taps(base + k * step)], axis=1) for base in bases
         ]
-        out = jnp.dot(jnp.concatenate(lhs, axis=0), weight[...], preferred_element_type=jnp.float32)
+        lhs = lhs[0] if len(lhs) == 1 else jnp.concatenate(lhs, axis=0)
+        out = jnp.dot(lhs, weight[...], preferred_element_type=jnp.float32)
         tall = out.shape[0] // len(bases)
         return [
             [out[n * tall : (n + 1) * tall, half * channels : (half + 1) * channels] for half in range(2)]
@@ -294,18 +295,21 @@
     for c in range(8):
         build(c)
     for s in range(first_groups + 1):
-        one = two = None
-        first_bases, second_bases = (4 * s, 4 * s + 2), (4 * (s - 2), 4 * (s - 2) + 1)
-        if s < first_groups:
-            one = paired(first_taps, first_bases, 1, pairs_one_ref)
-        for c in range(4 * (s + 2), min(4 * (s + 3), couples)):
-            build(c)
-        if 0 <= s - 2 < second_groups:
-            two = paired(second_taps, second_bases, 2, pairs_two_ref)
-        if one is not None:
-            keep_hidden(first_bases, one)
-        if two is not None:
-            keep_score(second_bases, two)
+        later = list(range(4 * (s + 2), min(4 * (s + 3), couples)))
+        seconds = []
+        for part in range(2):
+            one = None
+            first_base, second_base = 4 * s + 2 * part, 4 * (s - 2) + part
+            if s < first_groups:
+                one = paired(first_taps, (first_base,), 1, pairs_one_ref)
+            for c in later[2 * part : 2 * part + 2]:
+                build(c)
+            if 0 <= s - 2 < second_groups:
+                seconds += paired(second_taps, (second_base,), 2, pairs_two_ref)
+            if one is not None:
+                keep_hidden((first_base,), one)
+        if seconds:
+            keep_score((4 * (s - 2), 4 * (s - 2) + 1), seconds)
     source = lax.broadcasted_iota(jnp.int32, (breadth, breadth), 0)
     place = ((source >> 3) & 1) * (2 * size) + ((source >> 1) & 1) * size
     place = place + 4 * (source >> 4) + 2 * ((source >> 2) & 1) + (source & 1)

time: 30.9 us -> 30.1 us (0.974)
  Pallas kernels: 11.6 us -> 10.8 us
    pallas_call x1, Pallas kernels: 9.6 us -> 8.85 us  [block_scores(): pl.pallas_call(functools.partial(map_kernel, map_bins, size, table), out_...]
where the time goes in v8:
time: 30.1 us; the launch traced here: 29.9 us
  blocking collectives  11.7 us (39%)
  Pallas kernels  10.8 us (36%)
  waiting for transfers between devices  4.97 us (17%)
  starting transfers between devices  1.66 us (6%)
  other arithmetic  0.7 us (2%)
    all_to_all x1, blocking collectives, on_device(): got = lax.all_to_all(copies, ('row', 'col'), 0, 0)  11.7 us
    pallas_call x1, Pallas kernels, block_scores(): pl.pallas_call(functools.partial(map_kernel, map_bins, size, table), out_...  8.85 us
    ppermute x1, waiting for transfers between devices, on_device(): lax.ppermute(sent, ('row', 'col'), [(device, target[device]) for device i...  4.97 us
    pallas_call x1, Pallas kernels, projected(): pl.pallas_call(functools.partial(project_kernel, map_bins, size, table),...  1.98 us
    ppermute x1, starting transfers between devices, on_device(): lax.ppermute(sent, ('row', 'col'), [(device, target[device]) for device i...  1.66 us
    select_n x1, other arithmetic, on_device(): jnp.where(place == 0, jnp.concatenate([kept, received], axis=axis), jnp.c...  0.7 us
  transfers between devices with their start and end apart: 1, of which 1 were waited for; matrix products, arithmetic and copies ran while one was open for 0% of the time, Pallas kernels for 0%

profile of v8, /device:TPU:4, one launch (start us, length us, event | category | flops | bytes accessed | tf_op | source)
XLA Modules:
  0.0 29.9 jit_solution(10804994511617691600)
XLA Ops:
  0.0 0.0 copy-start
  0.0 0.0 copy-start.1
  0.0 2.0 %shard_map.100 = (bf16[8,32,256]{2,1,0:T(8,128)(2,1)S(1)}, f32[4,304,128]{2,1,0:T(8,128)S(1)}, bf16[16,256]{1,0:T(8,128)(2,1)S(1)}) custom-call(bf16[128,1536]{1,0:T(8,128)(2,1)} %embedding_hbm.1, bf16[4,1536]{1,0:T(4,128)(2,1)} %bases_hbm.1, s32[1,64]{1,0:T(1,128)} %bitcast.10, s32[1,64]{1,0:T(1,128)} %bitcast.11, bf16[1536,128]{1,0:T(8,128)(2,1)} %w_row_hbm.1, ...), custom_call_target="tpu_custom_call" | custom-call | tf_op jit(solution)/shard_map/pallas_call | solution.py:169
  2.0 11.7 %all_to_all.5 = bf16[8,32,256]{2,1,0:T(8,128)(2,1)S(1)} all-to-all(bf16[8,32,256]{2,1,0:T(8,128)(2,1)S(1)} %get-tuple-element.10), channel_id=1, replica_groups=mesh['cand'=4,'row'=4,'col'=2] {'row','col'}, dimensions={0} | all-to-all | bytes 262144 | tf_op jit(solution)/shard_map/all_to_all | solution.py:388
  13.7 0.0 copy-done
  13.7 0.0 copy-done.1
  13.7 8.9 %shard_map.101 = (f32[64,64]{1,0:T(8,128)S(1)}, f32[64,64]{1,0:T(8,128)S(1)}) custom-call(bf16[256,256]{1,0:T(8,128)(2,1)S(1)} %bitcast.7, f32[4,304,128]{2,1,0:T(8,128)S(1)} %get-tuple-element.11.dist_ref, bf16[1152,128]{1,0:T(8,128)(2,1)S(1)} %bitcast.8, bf16[1152,128]{1,0:T(8,128)(2,1)S(1)} %bitcast.9, bf16[16,256]{1,0:T(8,128)(2,1)S(1)} %get-tuple-element.12.head_ref), custom_call_target="tpu_custom_call" | custom-call | tf_op jit(solution)/shard_map/pallas_call | solution.py:342
  22.5 1.7 %collective-permute-start = (f32[64,64]{1,0:T(8,128)S(1)}, f32[64,64]{1,0:T(8,128)S(1)}, u32[]{:S(2)}, u32[]{:S(2)}) collective-permute-start(f32[64,64]{1,0:T(8,128)S(1)} %get-tuple-element.14), channel_id=1, source_target_pairs={{0,2},{1,4},{2,0},{3,6},{4,3},{5,7},{6,1},{7,5},{8,10},{9,12},{10,... | collective-permute-start | bytes 49160 | tf_op jit(solution)/shard_map/ppermute | solution.py:391
  24.2 5.0 %collective-permute-done = f32[64,64]{1,0:T(8,128)S(1)} collective-permute-done((f32[64,64]{1,0:T(8,128)S(1)}, f32[64,64]{1,0:T(8,128)S(1)}, u32[]{:S(2)}, u32[]{:S(2)}) %collective-permute-start) | collective-permute-done | bytes 16416 | tf_op jit(solution)/shard_map/ppermute | solution.py:391
  29.2 0.7 %maximum_select_fusion = f32[64,128]{1,0:T(8,128)} fusion(f32[64,64]{1,0:T(8,128)S(1)} %collective-permute-done, f32[64,64]{1,0:T(8,128)S(1)} %get-tuple-element.13, pred[]{:T(512)S(6)} %eq.31), kind=kLoop, calls=%fused_computation | loop fusion | flops 24576 | bytes 65537 | tf_op jit(solution)/shard_map/jit(_where)/select_n | solution.py:394
Async XLA Ops:
  0.0 13.7 %copy-start = (bf16[3,3,128,128]{3,2,1,0:T(8,128)(2,1)S(1)}, bf16[3,3,128,128]{3,2,1,0:T(8,128)(2,1)}, u32[]{:S(2)}) copy-start(bf16[3,3,128,128]{3,2,1,0:T(8,128)(2,1)} %param.17) | copy-start | bytes 884740
  0.0 13.7 %copy-start.1 = (bf16[3,3,128,128]{3,2,1,0:T(8,128)(2,1)S(1)}, bf16[3,3,128,128]{3,2,1,0:T(8,128)(2,1)}, u32[]{:S(2)}) copy-start(bf16[3,3,128,128]{3,2,1,0:T(8,128)(2,1)} %param.18) | copy-start | bytes 884740
  22.5 6.6 %collective-permute-start = (f32[64,64]{1,0:T(8,128)S(1)}, f32[64,64]{1,0:T(8,128)S(1)}, u32[]{:S(2)}, u32[]{:S(2)}) collective-permute-start(f32[64,64]{1,0:T(8,128)S(1)} %get-tuple-element.14), channel_id=1, source_target_pairs={{0,2},{1,4},{2,0},{3,6},{4,3},{5,7},{6,1},{7,5},{8,10},{9,12},{10,... | collective-permute-start | bytes 49160 | tf_op jit(solution)/shard_map/ppermute | solution.py:391

commit v9 on v8

--- a/solution.py
+++ b/solution.py
@@ -195,11 +195,13 @@
     depth = 3 * channels
     row_a, col_a, row_b, col_b, diagonal, _ = lookup(table)
     rows, cols = (row_a * size, row_b * size), (col_a * size, col_b * size)
-    for ref, given in ((pairs_one_ref, first_ref), (pairs_two_ref, second_ref)):
+    def place_weights(ref, given):
         ref[3 * depth :, :channels] = jnp.zeros((depth, channels), jnp.bfloat16)
         ref[:depth, channels:] = jnp.zeros((depth, channels), jnp.bfloat16)
         ref[: 3 * depth, :channels] = given[...]
         ref[depth:, channels:] = given[...]
+
+    place_weights(pairs_one_ref, first_ref)
 
     def of_block(lane, values):
         return jnp.where((lane & 2) == 0, values[0], values[1])
@@ -274,42 +276,44 @@
                 )
                 hidden_ref[c] = value.astype(jnp.bfloat16)
 
-    def keep_score(bases, out):
-        last = []
-        for n, base in enumerate(bases):
-            halves = []
-            for half in range(2):
-                own = hidden_ref[base + 2 * half + 2, 16 : 16 + breadth].astype(jnp.float32)
-                halves.append((own + relu(out[n][half])).astype(jnp.bfloat16))
-            last.append(jnp.concatenate(halves, axis=1))
+    def keep_score(base, out):
+        halves = []
+        for half in range(2):
+            own = hidden_ref[base + 2 * half + 2, 16 : 16 + breadth].astype(jnp.float32)
+            halves.append((own + relu(out[half])).astype(jnp.bfloat16))
         got = lax.dot_general(
             head_ref[...],
-            jnp.concatenate(last, axis=0),
+            jnp.concatenate(halves, axis=1),
             (((1,), (1,)), ((), ())),
             preferred_element_type=jnp.float32,
         )
-        lines = [got[half : half + 1, n * breadth : (n + 1) * breadth] for half in range(2) for n in range(2)]
-        mixed_ref[bases[0] : bases[0] + 4] = jnp.concatenate(lines, axis=0)
+        for half in range(2):
+            mixed_ref[base + 2 * half : base + 2 * half + 1] = got[half : half + 1]
 
     first_groups, second_groups = hidden_couples // 4, size // 8
-    for c in range(8):
+    for c in range(6):
         build(c)
+    waiting = None
     for s in range(first_groups + 1):
-        later = list(range(4 * (s + 2), min(4 * (s + 3), couples)))
-        seconds = []
         for part in range(2):
-            one = None
+            one = two = None
             first_base, second_base = 4 * s + 2 * part, 4 * (s - 2) + part
             if s < first_groups:
                 one = paired(first_taps, (first_base,), 1, pairs_one_ref)
-            for c in later[2 * part : 2 * part + 2]:
+            if first_base == 0:
+                place_weights(pairs_two_ref, second_ref)
+            if waiting is not None:
+                keep_score(*waiting)
+                waiting = None
+            for c in range(first_base + 6, min(first_base + 8, couples)):
                 build(c)
             if 0 <= s - 2 < second_groups:
-                seconds += paired(second_taps, (second_base,), 2, pairs_two_ref)
+                two = paired(second_taps, (second_base,), 2, pairs_two_ref)
             if one is not None:
                 keep_hidden((first_base,), one)
-        if seconds:
-            keep_score((4 * (s - 2), 4 * (s - 2) + 1), seconds)
+            if two is not None:
+                waiting = second_base, two[0]
+    keep_score(*waiting)
     source = lax.broadcasted_iota(jnp.int32, (breadth, breadth), 0)
     place = ((source >> 3) & 1) * (2 * size) + ((source >> 1) & 1) * size
     place = place + 4 * (source >> 4) + 2 * ((source >> 2) & 1) + (source & 1)

time: 30.1 us -> 31.8 us (1.056)
  Pallas kernels: 10.8 us -> 12.5 us
    pallas_call x1, Pallas kernels: 8.85 us -> 10.6 us  [block_scores(): pl.pallas_call(functools.partial(map_kernel, map_bins, size, table), out_...]
where the time goes in v9:
time: 31.8 us; the launch traced here: 31.6 us
  Pallas kernels  12.5 us (39%)
  blocking collectives  11.7 us (37%)
  waiting for transfers between devices  4.97 us (16%)
  starting transfers between devices  1.66 us (5%)
  other arithmetic  0.7 us (2%)
    all_to_all x1, blocking collectives, on_device(): got = lax.all_to_all(copies, ('row', 'col'), 0, 0)  11.7 us
    pallas_call x1, Pallas kernels, block_scores(): pl.pallas_call(functools.partial(map_kernel, map_bins, size, table), out_...  10.6 us
    ppermute x1, waiting for transfers between devices, on_device(): lax.ppermute(sent, ('row', 'col'), [(device, target[device]) for device i...  4.97 us
    pallas_call x1, Pallas kernels, projected(): pl.pallas_call(functools.partial(project_kernel, map_bins, size, table),...  1.98 us
    ppermute x1, starting transfers between devices, on_device(): lax.ppermute(sent, ('row', 'col'), [(device, target[device]) for device i...  1.66 us
    select_n x1, other arithmetic, on_device(): jnp.where(place == 0, jnp.concatenate([kept, received], axis=axis), jnp.c...  0.7 us
  transfers between devices with their start and end apart: 1, of which 1 were waited for; matrix products, arithmetic and copies ran while one was open for 0% of the time, Pallas kernels for 0%

profile of v9, /device:TPU:4, one launch (start us, length us, event | category | flops | bytes accessed | tf_op | source)
XLA Modules:
  0.0 31.6 jit_solution(14851888194797256896)
XLA Ops:
  0.0 0.0 copy-start
  0.0 0.0 copy-start.1
  0.0 2.0 %shard_map.100 = (bf16[8,32,256]{2,1,0:T(8,128)(2,1)S(1)}, f32[4,304,128]{2,1,0:T(8,128)S(1)}, bf16[16,256]{1,0:T(8,128)(2,1)S(1)}) custom-call(bf16[128,1536]{1,0:T(8,128)(2,1)} %embedding_hbm.1, bf16[4,1536]{1,0:T(4,128)(2,1)} %bases_hbm.1, s32[1,64]{1,0:T(1,128)} %bitcast.10, s32[1,64]{1,0:T(1,128)} %bitcast.11, bf16[1536,128]{1,0:T(8,128)(2,1)} %w_row_hbm.1, ...), custom_call_target="tpu_custom_call" | custom-call | tf_op jit(solution)/shard_map/pallas_call | solution.py:169
  2.0 11.7 %all_to_all.5 = bf16[8,32,256]{2,1,0:T(8,128)(2,1)S(1)} all-to-all(bf16[8,32,256]{2,1,0:T(8,128)(2,1)S(1)} %get-tuple-element.10), channel_id=1, replica_groups=mesh['cand'=4,'row'=4,'col'=2] {'row','col'}, dimensions={0} | all-to-all | bytes 262144 | tf_op jit(solution)/shard_map/all_to_all | solution.py:392
  13.7 0.0 copy-done
  13.7 0.0 copy-done.1
  13.7 10.6 %shard_map.101 = (f32[64,64]{1,0:T(8,128)S(1)}, f32[64,64]{1,0:T(8,128)S(1)}) custom-call(bf16[256,256]{1,0:T(8,128)(2,1)S(1)} %bitcast.7, f32[4,304,128]{2,1,0:T(8,128)S(1)} %get-tuple-element.11.dist_ref, bf16[1152,128]{1,0:T(8,128)(2,1)S(1)} %bitcast.8, bf16[1152,128]{1,0:T(8,128)(2,1)S(1)} %bitcast.9, bf16[16,256]{1,0:T(8,128)(2,1)S(1)} %get-tuple-element.12.head_ref), custom_call_target="tpu_custom_call" | custom-call | tf_op jit(solution)/shard_map/pallas_call | solution.py:346
  24.2 1.7 %collective-permute-start = (f32[64,64]{1,0:T(8,128)S(1)}, f32[64,64]{1,0:T(8,128)S(1)}, u32[]{:S(2)}, u32[]{:S(2)}) collective-permute-start(f32[64,64]{1,0:T(8,128)S(1)} %get-tuple-element.14), channel_id=1, source_target_pairs={{0,2},{1,4},{2,0},{3,6},{4,3},{5,7},{6,1},{7,5},{8,10},{9,12},{10,... | collective-permute-start | bytes 49160 | tf_op jit(solution)/shard_map/ppermute | solution.py:395
  25.9 5.0 %collective-permute-done = f32[64,64]{1,0:T(8,128)S(1)} collective-permute-done((f32[64,64]{1,0:T(8,128)S(1)}, f32[64,64]{1,0:T(8,128)S(1)}, u32[]{:S(2)}, u32[]{:S(2)}) %collective-permute-start) | collective-permute-done | bytes 16416 | tf_op jit(solution)/shard_map/ppermute | solution.py:395
  30.9 0.7 %maximum_select_fusion = f32[64,128]{1,0:T(8,128)} fusion(f32[64,64]{1,0:T(8,128)S(1)} %collective-permute-done, f32[64,64]{1,0:T(8,128)S(1)} %get-tuple-element.13, pred[]{:T(512)S(6)} %eq.31), kind=kLoop, calls=%fused_computation | loop fusion | flops 24576 | bytes 65537 | tf_op jit(solution)/shard_map/jit(_where)/select_n | solution.py:398
Async XLA Ops:
  0.0 13.7 %copy-start = (bf16[3,3,128,128]{3,2,1,0:T(8,128)(2,1)S(1)}, bf16[3,3,128,128]{3,2,1,0:T(8,128)(2,1)}, u32[]{:S(2)}) copy-start(bf16[3,3,128,128]{3,2,1,0:T(8,128)(2,1)} %param.17) | copy-start | bytes 884740
  0.0 13.7 %copy-start.1 = (bf16[3,3,128,128]{3,2,1,0:T(8,128)(2,1)S(1)}, bf16[3,3,128,128]{3,2,1,0:T(8,128)(2,1)}, u32[]{:S(2)}) copy-start(bf16[3,3,128,128]{3,2,1,0:T(8,128)(2,1)} %param.18) | copy-start | bytes 884740
  24.2 6.6 %collective-permute-start = (f32[64,64]{1,0:T(8,128)S(1)}, f32[64,64]{1,0:T(8,128)S(1)}, u32[]{:S(2)}, u32[]{:S(2)}) collective-permute-start(f32[64,64]{1,0:T(8,128)S(1)} %get-tuple-element.14), channel_id=1, source_target_pairs={{0,2},{1,4},{2,0},{3,6},{4,3},{5,7},{6,1},{7,5},{8,10},{9,12},{10,... | collective-permute-start | bytes 49160 | tf_op jit(solution)/shard_map/ppermute | solution.py:395

commit v10 on v8

--- a/solution.py
+++ b/solution.py
@@ -183,7 +183,7 @@
 def map_kernel(
     map_bins, size, table, proj_ref, dist_ref, first_ref, second_ref, head_ref,
     kept_ref, sent_ref, row_ref, col_ref, own_ref, moved_ref, hidden_ref, pairs_one_ref, pairs_two_ref,
-    mixed_ref, score_ref,
+    last_ref, mixed_ref, score_ref,
 ):
     channels = head_ref.shape[1] // 2
     tiles = tiles_of(size)
@@ -274,42 +274,48 @@
                 )
                 hidden_ref[c] = value.astype(jnp.bfloat16)
 
-    def keep_score(bases, out):
-        last = []
-        for n, base in enumerate(bases):
-            halves = []
-            for half in range(2):
-                own = hidden_ref[base + 2 * half + 2, 16 : 16 + breadth].astype(jnp.float32)
-                halves.append((own + relu(out[n][half])).astype(jnp.bfloat16))
-            last.append(jnp.concatenate(halves, axis=1))
+    def keep_last(base, out):
+        for half in range(2):
+            own = hidden_ref[base + 2 * half + 2, 16 : 16 + breadth].astype(jnp.float32)
+            last_ref[base // 4 * 2 + base % 4, :, half * channels : (half + 1) * channels] = (
+                own + relu(out[half])
+            ).astype(jnp.bfloat16)
+
+    def keep_scores(start, count):
         got = lax.dot_general(
             head_ref[...],
-            jnp.concatenate(last, axis=0),
+            last_ref[start : start + count].reshape(count * breadth, 2 * channels),
             (((1,), (1,)), ((), ())),
             preferred_element_type=jnp.float32,
         )
-        lines = [got[half : half + 1, n * breadth : (n + 1) * breadth] for half in range(2) for n in range(2)]
-        mixed_ref[bases[0] : bases[0] + 4] = jnp.concatenate(lines, axis=0)
+        lines = [
+            got[half : half + 1, n * breadth : (n + 1) * breadth]
+            for pair in range(0, count, 2)
+            for half in range(2)
+            for n in (pair, pair + 1)
+        ]
+        mixed_ref[2 * start : 2 * (start + count)] = jnp.concatenate(lines, axis=0)
 
     first_groups, second_groups = hidden_couples // 4, size // 8
     for c in range(8):
         build(c)
     for s in range(first_groups + 1):
         later = list(range(4 * (s + 2), min(4 * (s + 3), couples)))
-        seconds = []
         for part in range(2):
-            one = None
+            one = seconds = None
             first_base, second_base = 4 * s + 2 * part, 4 * (s - 2) + part
             if s < first_groups:
                 one = paired(first_taps, (first_base,), 1, pairs_one_ref)
             for c in later[2 * part : 2 * part + 2]:
                 build(c)
             if 0 <= s - 2 < second_groups:
-                seconds += paired(second_taps, (second_base,), 2, pairs_two_ref)
+                seconds = paired(second_taps, (second_base,), 2, pairs_two_ref)
             if one is not None:
                 keep_hidden((first_base,), one)
-        if seconds:
-            keep_score((4 * (s - 2), 4 * (s - 2) + 1), seconds)
+            if seconds:
+                keep_last(second_base, seconds[0])
+    for start in range(0, size // 4, 4):
+        keep_scores(start, 4)
     source = lax.broadcasted_iota(jnp.int32, (breadth, breadth), 0)
     place = ((source >> 3) & 1) * (2 * size) + ((source >> 1) & 1) * size
     place = place + 4 * (source >> 4) + 2 * ((source >> 2) & 1) + (source & 1)
@@ -352,6 +358,7 @@
             pltpu.VMEM((size // 2 + SECOND_SPACING, 16 * (tiles - 2), channels), jnp.bfloat16),
             pltpu.VMEM((12 * channels, 2 * channels), jnp.bfloat16),
             pltpu.VMEM((12 * channels, 2 * channels), jnp.bfloat16),
+            pltpu.VMEM((size // 4, 4 * size, 2 * channels), jnp.bfloat16),
             pltpu.VMEM((size // 2, 4 * size), jnp.float32),
             pltpu.VMEM((size, 2 * size), jnp.float32),
         ],

time: 30.1 us -> 30 us (level)
  no operation moved by 1% of the time
where the time goes in v10:
time: 30 us; the launch traced here: 29.8 us
  blocking collectives  11.7 us (39%)
  Pallas kernels  10.8 us (36%)
  waiting for transfers between devices  4.97 us (17%)
  starting transfers between devices  1.66 us (6%)
  other arithmetic  0.7 us (2%)
    all_to_all x1, blocking collectives, on_device(): got = lax.all_to_all(copies, ('row', 'col'), 0, 0)  11.7 us
    pallas_call x1, Pallas kernels, block_scores(): pl.pallas_call(functools.partial(map_kernel, map_bins, size, table), out_...  8.78 us
    ppermute x1, waiting for transfers between devices, on_device(): lax.ppermute(sent, ('row', 'col'), [(device, target[device]) for device i...  4.97 us
    pallas_call x1, Pallas kernels, projected(): pl.pallas_call(functools.partial(project_kernel, map_bins, size, table),...  1.98 us
    ppermute x1, starting transfers between devices, on_device(): lax.ppermute(sent, ('row', 'col'), [(device, target[device]) for device i...  1.66 us
    select_n x1, other arithmetic, on_device(): jnp.where(place == 0, jnp.concatenate([kept, received], axis=axis), jnp.c...  0.7 us
  transfers between devices with their start and end apart: 1, of which 1 were waited for; matrix products, arithmetic and copies ran while one was open for 0% of the time, Pallas kernels for 0%

profile of v10, /device:TPU:4, one launch (start us, length us, event | category | flops | bytes accessed | tf_op | source)
XLA Modules:
  0.0 29.8 jit_solution(11434803384213337057)
XLA Ops:
  0.0 0.0 copy-start
  0.0 0.0 copy-start.1
  0.0 2.0 %shard_map.100 = (bf16[8,32,256]{2,1,0:T(8,128)(2,1)S(1)}, f32[4,304,128]{2,1,0:T(8,128)S(1)}, bf16[16,256]{1,0:T(8,128)(2,1)S(1)}) custom-call(bf16[128,1536]{1,0:T(8,128)(2,1)} %embedding_hbm.1, bf16[4,1536]{1,0:T(4,128)(2,1)} %bases_hbm.1, s32[1,64]{1,0:T(1,128)} %bitcast.10, s32[1,64]{1,0:T(1,128)} %bitcast.11, bf16[1536,128]{1,0:T(8,128)(2,1)} %w_row_hbm.1, ...), custom_call_target="tpu_custom_call" | custom-call | tf_op jit(solution)/shard_map/pallas_call | solution.py:169
  2.0 11.7 %all_to_all.5 = bf16[8,32,256]{2,1,0:T(8,128)(2,1)S(1)} all-to-all(bf16[8,32,256]{2,1,0:T(8,128)(2,1)S(1)} %get-tuple-element.10), channel_id=1, replica_groups=mesh['cand'=4,'row'=4,'col'=2] {'row','col'}, dimensions={0} | all-to-all | bytes 262144 | tf_op jit(solution)/shard_map/all_to_all | solution.py:395
  13.7 0.0 copy-done
  13.7 0.0 copy-done.1
  13.7 8.8 %shard_map.101 = (f32[64,64]{1,0:T(8,128)S(1)}, f32[64,64]{1,0:T(8,128)S(1)}) custom-call(bf16[256,256]{1,0:T(8,128)(2,1)S(1)} %bitcast.7, f32[4,304,128]{2,1,0:T(8,128)S(1)} %get-tuple-element.11.dist_ref, bf16[1152,128]{1,0:T(8,128)(2,1)S(1)} %bitcast.8, bf16[1152,128]{1,0:T(8,128)(2,1)S(1)} %bitcast.9, bf16[16,256]{1,0:T(8,128)(2,1)S(1)} %get-tuple-element.12.head_ref), custom_call_target="tpu_custom_call" | custom-call | tf_op jit(solution)/shard_map/pallas_call | solution.py:348
  22.5 1.7 %collective-permute-start = (f32[64,64]{1,0:T(8,128)S(1)}, f32[64,64]{1,0:T(8,128)S(1)}, u32[]{:S(2)}, u32[]{:S(2)}) collective-permute-start(f32[64,64]{1,0:T(8,128)S(1)} %get-tuple-element.14), channel_id=1, source_target_pairs={{0,2},{1,4},{2,0},{3,6},{4,3},{5,7},{6,1},{7,5},{8,10},{9,12},{10,... | collective-permute-start | bytes 49160 | tf_op jit(solution)/shard_map/ppermute | solution.py:398
  24.1 5.0 %collective-permute-done = f32[64,64]{1,0:T(8,128)S(1)} collective-permute-done((f32[64,64]{1,0:T(8,128)S(1)}, f32[64,64]{1,0:T(8,128)S(1)}, u32[]{:S(2)}, u32[]{:S(2)}) %collective-permute-start) | collective-permute-done | bytes 16416 | tf_op jit(solution)/shard_map/ppermute | solution.py:398
  29.1 0.7 %maximum_select_fusion = f32[64,128]{1,0:T(8,128)} fusion(f32[64,64]{1,0:T(8,128)S(1)} %collective-permute-done, f32[64,64]{1,0:T(8,128)S(1)} %get-tuple-element.13, pred[]{:T(512)S(6)} %eq.31), kind=kLoop, calls=%fused_computation | loop fusion | flops 24576 | bytes 65537 | tf_op jit(solution)/shard_map/jit(_where)/select_n | solution.py:401
Async XLA Ops:
  0.0 13.7 %copy-start = (bf16[3,3,128,128]{3,2,1,0:T(8,128)(2,1)S(1)}, bf16[3,3,128,128]{3,2,1,0:T(8,128)(2,1)}, u32[]{:S(2)}) copy-start(bf16[3,3,128,128]{3,2,1,0:T(8,128)(2,1)} %param.17) | copy-start | bytes 884740
  0.0 13.7 %copy-start.1 = (bf16[3,3,128,128]{3,2,1,0:T(8,128)(2,1)S(1)}, bf16[3,3,128,128]{3,2,1,0:T(8,128)(2,1)}, u32[]{:S(2)}) copy-start(bf16[3,3,128,128]{3,2,1,0:T(8,128)(2,1)} %param.18) | copy-start | bytes 884740
  22.5 6.6 %collective-permute-start = (f32[64,64]{1,0:T(8,128)S(1)}, f32[64,64]{1,0:T(8,128)S(1)}, u32[]{:S(2)}, u32[]{:S(2)}) collective-permute-start(f32[64,64]{1,0:T(8,128)S(1)} %get-tuple-element.14), channel_id=1, source_target_pairs={{0,2},{1,4},{2,0},{3,6},{4,3},{5,7},{6,1},{7,5},{8,10},{9,12},{10,... | collective-permute-start | bytes 49160 | tf_op jit(solution)/shard_map/ppermute | solution.py:398

commit v11 on v10

--- a/solution.py
+++ b/solution.py
@@ -129,10 +129,13 @@
         move.wait()
     for phase in range(phases):
         dist_ref[phase] = gain_ref[...] * feature[phase]
-    weight = jnp.concatenate([weight_ref[...].astype(jnp.float32)] * 2, axis=1)
-    line = lax.broadcasted_iota(jnp.int32, head_ref.shape, 0)
-    half = lax.broadcasted_iota(jnp.int32, head_ref.shape, 1) >= channels
-    head_ref[...] = jnp.where(line == half.astype(jnp.int32), weight, 0.0).astype(jnp.bfloat16)
+    weight = jnp.broadcast_to(weight_ref[...].astype(jnp.float32), (channels, channels)).T
+    column = lax.broadcasted_iota(jnp.int32, (channels, channels), 1)
+    for n in range(head_ref.shape[0] // (2 * channels)):
+        for half in range(2):
+            at = (2 * n + half) * channels
+            of_couple = 4 * (n // 2) + n % 2 + 2 * half
+            head_ref[at : at + channels] = jnp.where(column == of_couple, weight, 0.0).astype(jnp.bfloat16)
     ahead = pos_ref[...] - bins
     in_bin = ((ahead >= 0) & (ahead < POOL)).astype(jnp.float32)
     edited = None
@@ -171,7 +174,7 @@
         out_shape=(
             jax.ShapeDtypeStruct((copies, embedding.shape[0] // POOL, 2 * channels), jnp.bfloat16),
             jax.ShapeDtypeStruct((4, 8 * (tiles_of(size) + (size + 2 * MARGIN) // 4 - 1), channels), jnp.float32),
-            jax.ShapeDtypeStruct((16, 2 * channels), jnp.bfloat16),
+            jax.ShapeDtypeStruct((size // 2 * channels, channels), jnp.bfloat16),
         ),
         in_specs=[pl.BlockSpec(memory_space=pltpu.HBM)] * 8,
         out_specs=(vmem, vmem, vmem),
@@ -183,9 +186,9 @@
 def map_kernel(
     map_bins, size, table, proj_ref, dist_ref, first_ref, second_ref, head_ref,
     kept_ref, sent_ref, row_ref, col_ref, own_ref, moved_ref, hidden_ref, pairs_one_ref, pairs_two_ref,
-    last_ref, mixed_ref, score_ref,
+    last_ref, score_ref,
 ):
-    channels = head_ref.shape[1] // 2
+    channels = head_ref.shape[1]
     tiles = tiles_of(size)
     wide = 16 * (tiles - 2)
     breadth = 4 * size
@@ -280,21 +283,6 @@
             last_ref[base // 4 * 2 + base % 4, :, half * channels : (half + 1) * channels] = (
                 own + relu(out[half])
             ).astype(jnp.bfloat16)
-
-    def keep_scores(start, count):
-        got = lax.dot_general(
-            head_ref[...],
-            last_ref[start : start + count].reshape(count * breadth, 2 * channels),
-            (((1,), (1,)), ((), ())),
-            preferred_element_type=jnp.float32,
-        )
-        lines = [
-            got[half : half + 1, n * breadth : (n + 1) * breadth]
-            for pair in range(0, count, 2)
-            for half in range(2)
-            for n in (pair, pair + 1)
-        ]
-        mixed_ref[2 * start : 2 * (start + count)] = jnp.concatenate(lines, axis=0)
 
     first_groups, second_groups = hidden_couples // 4, size // 8
     for c in range(8):
@@ -314,14 +302,15 @@
                 keep_hidden((first_base,), one)
             if seconds:
                 keep_last(second_base, seconds[0])
-    for start in range(0, size // 4, 4):
-        keep_scores(start, 4)
+    every_last = jnp.concatenate([last_ref[n] for n in range(size // 4)], axis=1)
+    by_couple = jnp.dot(every_last, head_ref[...], preferred_element_type=jnp.float32)
+    mixed = by_couple.T[: size // 2]
     source = lax.broadcasted_iota(jnp.int32, (breadth, breadth), 0)
     place = ((source >> 3) & 1) * (2 * size) + ((source >> 1) & 1) * size
     place = place + 4 * (source >> 4) + 2 * ((source >> 2) & 1) + (source & 1)
     order = (place == lax.broadcasted_iota(jnp.int32, (breadth, breadth), 1)).astype(jnp.float32)
     order = order.astype(jnp.bfloat16)
-    rest, ordered = mixed_ref[...], None
+    rest, ordered = mixed, None
     for _ in range(3):
         piece = rest.astype(jnp.bfloat16)
         rest = rest - piece.astype(jnp.float32)
@@ -359,7 +348,6 @@
             pltpu.VMEM((12 * channels, 2 * channels), jnp.bfloat16),
             pltpu.VMEM((12 * channels, 2 * channels), jnp.bfloat16),
             pltpu.VMEM((size // 4, 4 * size, 2 * channels), jnp.bfloat16),
-            pltpu.VMEM((size // 2, 4 * size), jnp.float32),
             pltpu.VMEM((size, 2 * size), jnp.float32),
         ],
         compiler_params=pltpu.CompilerParams(vmem_limit_bytes=40 * 1024 * 1024),

time: 30 us -> 30.4 us (1.013)
  no operation moved by 1% of the time
where the time goes in v11:
time: 30.4 us; the launch traced here: 30.1 us
  blocking collectives  11.7 us (38%)
  Pallas kernels  11.1 us (37%)
  waiting for transfers between devices  4.97 us (16%)
  starting transfers between devices  1.66 us (5%)
  other arithmetic  0.7 us (2%)
    all_to_all x1, blocking collectives, on_device(): got = lax.all_to_all(copies, ('row', 'col'), 0, 0)  11.7 us
    pallas_call x1, Pallas kernels, block_scores(): pl.pallas_call(functools.partial(map_kernel, map_bins, size, table), out_...  8.91 us
    ppermute x1, waiting for transfers between devices, on_device(): lax.ppermute(sent, ('row', 'col'), [(device, target[device]) for device i...  4.97 us
    pallas_call x1, Pallas kernels, projected(): pl.pallas_call(functools.partial(project_kernel, map_bins, size, table),...  2.17 us
    ppermute x1, starting transfers between devices, on_device(): lax.ppermute(sent, ('row', 'col'), [(device, target[device]) for device i...  1.66 us
    select_n x1, other arithmetic, on_device(): jnp.where(place == 0, jnp.concatenate([kept, received], axis=axis), jnp.c...  0.7 us
  transfers between devices with their start and end apart: 1, of which 1 were waited for; matrix products, arithmetic and copies ran while one was open for 0% of the time, Pallas kernels for 0%

profile of v11, /device:TPU:4, one launch (start us, length us, event | category | flops | bytes accessed | tf_op | source)
XLA Modules:
  0.0 30.1 jit_solution(12140485181155126260)
XLA Ops:
  0.0 0.0 copy-start
  0.0 0.0 copy-start.1
  0.0 2.2 %shard_map.100 = (bf16[8,32,256]{2,1,0:T(8,128)(2,1)S(1)}, f32[4,304,128]{2,1,0:T(8,128)S(1)}, bf16[4096,128]{1,0:T(8,128)(2,1)S(1)}) custom-call(bf16[128,1536]{1,0:T(8,128)(2,1)} %embedding_hbm.1, bf16[4,1536]{1,0:T(4,128)(2,1)} %bases_hbm.1, s32[1,64]{1,0:T(1,128)} %bitcast.10, s32[1,64]{1,0:T(1,128)} %bitcast.11, bf16[1536,128]{1,0:T(8,128)(2,1)} %w_row_hbm.1, ...), custom_call_target="tpu_custom_call" | custom-call | tf_op jit(solution)/shard_map/pallas_call | solution.py:172
  2.2 11.7 %all_to_all.5 = bf16[8,32,256]{2,1,0:T(8,128)(2,1)S(1)} all-to-all(bf16[8,32,256]{2,1,0:T(8,128)(2,1)S(1)} %get-tuple-element.10), channel_id=1, replica_groups=mesh['cand'=4,'row'=4,'col'=2] {'row','col'}, dimensions={0} | all-to-all | bytes 262144 | tf_op jit(solution)/shard_map/all_to_all | solution.py:383
  13.9 0.0 copy-done
  13.9 0.0 copy-done.1
  13.9 8.9 %shard_map.101 = (f32[64,64]{1,0:T(8,128)S(1)}, f32[64,64]{1,0:T(8,128)S(1)}) custom-call(bf16[256,256]{1,0:T(8,128)(2,1)S(1)} %bitcast.7, f32[4,304,128]{2,1,0:T(8,128)S(1)} %get-tuple-element.11.dist_ref, bf16[1152,128]{1,0:T(8,128)(2,1)S(1)} %bitcast.8, bf16[1152,128]{1,0:T(8,128)(2,1)S(1)} %bitcast.9, bf16[4096,128]{1,0:T(8,128)(2,1)S(1)} %get-tuple-element.12.head_ref), custom_call_target="tpu_custom_call" | custom-call | tf_op jit(solution)/shard_map/pallas_call | solution.py:337
  22.8 1.7 %collective-permute-start = (f32[64,64]{1,0:T(8,128)S(1)}, f32[64,64]{1,0:T(8,128)S(1)}, u32[]{:S(2)}, u32[]{:S(2)}) collective-permute-start(f32[64,64]{1,0:T(8,128)S(1)} %get-tuple-element.14), channel_id=1, source_target_pairs={{0,2},{1,4},{2,0},{3,6},{4,3},{5,7},{6,1},{7,5},{8,10},{9,12},{10,... | collective-permute-start | bytes 49160 | tf_op jit(solution)/shard_map/ppermute | solution.py:386
  24.4 5.0 %collective-permute-done = f32[64,64]{1,0:T(8,128)S(1)} collective-permute-done((f32[64,64]{1,0:T(8,128)S(1)}, f32[64,64]{1,0:T(8,128)S(1)}, u32[]{:S(2)}, u32[]{:S(2)}) %collective-permute-start) | collective-permute-done | bytes 16416 | tf_op jit(solution)/shard_map/ppermute | solution.py:386
  29.4 0.7 %maximum_select_fusion = f32[64,128]{1,0:T(8,128)} fusion(f32[64,64]{1,0:T(8,128)S(1)} %collective-permute-done, f32[64,64]{1,0:T(8,128)S(1)} %get-tuple-element.13, pred[]{:T(512)S(6)} %eq.31), kind=kLoop, calls=%fused_computation | loop fusion | flops 24576 | bytes 65537 | tf_op jit(solution)/shard_map/jit(_where)/select_n | solution.py:389
Async XLA Ops:
  0.0 13.9 %copy-start = (bf16[3,3,128,128]{3,2,1,0:T(8,128)(2,1)S(1)}, bf16[3,3,128,128]{3,2,1,0:T(8,128)(2,1)}, u32[]{:S(2)}) copy-start(bf16[3,3,128,128]{3,2,1,0:T(8,128)(2,1)} %param.17) | copy-start | bytes 884740
  0.0 13.9 %copy-start.1 = (bf16[3,3,128,128]{3,2,1,0:T(8,128)(2,1)S(1)}, bf16[3,3,128,128]{3,2,1,0:T(8,128)(2,1)}, u32[]{:S(2)}) copy-start(bf16[3,3,128,128]{3,2,1,0:T(8,128)(2,1)} %param.18) | copy-start | bytes 884740
  22.8 6.6 %collective-permute-start = (f32[64,64]{1,0:T(8,128)S(1)}, f32[64,64]{1,0:T(8,128)S(1)}, u32[]{:S(2)}, u32[]{:S(2)}) collective-permute-start(f32[64,64]{1,0:T(8,128)S(1)} %get-tuple-element.14), channel_id=1, source_target_pairs={{0,2},{1,4},{2,0},{3,6},{4,3},{5,7},{6,1},{7,5},{8,10},{9,12},{10,... | collective-permute-start | bytes 49160 | tf_op jit(solution)/shard_map/ppermute | solution.py:386

commit v12 on v10

--- a/solution.py
+++ b/solution.py
@@ -195,11 +195,13 @@
     depth = 3 * channels
     row_a, col_a, row_b, col_b, diagonal, _ = lookup(table)
     rows, cols = (row_a * size, row_b * size), (col_a * size, col_b * size)
-    for ref, given in ((pairs_one_ref, first_ref), (pairs_two_ref, second_ref)):
+    def place_weights(ref, given):
         ref[3 * depth :, :channels] = jnp.zeros((depth, channels), jnp.bfloat16)
         ref[:depth, channels:] = jnp.zeros((depth, channels), jnp.bfloat16)
         ref[: 3 * depth, :channels] = given[...]
         ref[depth:, channels:] = given[...]
+
+    place_weights(pairs_one_ref, first_ref)
 
     def of_block(lane, values):
         return jnp.where((lane & 2) == 0, values[0], values[1])
@@ -297,7 +299,7 @@
         mixed_ref[2 * start : 2 * (start + count)] = jnp.concatenate(lines, axis=0)
 
     first_groups, second_groups = hidden_couples // 4, size // 8
-    for c in range(8):
+    for c in range(4):
         build(c)
     for s in range(first_groups + 1):
         later = list(range(4 * (s + 2), min(4 * (s + 3), couples)))
@@ -306,6 +308,10 @@
             first_base, second_base = 4 * s + 2 * part, 4 * (s - 2) + part
             if s < first_groups:
                 one = paired(first_taps, (first_base,), 1, pairs_one_ref)
+            if first_base == 0:
+                for c in range(4, 8):
+                    build(c)
+                place_weights(pairs_two_ref, second_ref)
             for c in later[2 * part : 2 * part + 2]:
                 build(c)
             if 0 <= s - 2 < second_groups:

time: 30 us -> 30 us (level)
  no operation moved by 1% of the time
where the time goes in v12:
time: 30 us; the launch traced here: 29.8 us
  blocking collectives  11.7 us (39%)
  Pallas kernels  10.8 us (36%)
  waiting for transfers between devices  4.97 us (17%)
  starting transfers between devices  1.66 us (6%)
  other arithmetic  0.7 us (2%)
    all_to_all x1, blocking collectives, on_device(): got = lax.all_to_all(copies, ('row', 'col'), 0, 0)  11.7 us
    pallas_call x1, Pallas kernels, block_scores(): pl.pallas_call(functools.partial(map_kernel, map_bins, size, table), out_...  8.78 us
    ppermute x1, waiting for transfers between devices, on_device(): lax.ppermute(sent, ('row', 'col'), [(device, target[device]) for device i...  4.97 us
    pallas_call x1, Pallas kernels, projected(): pl.pallas_call(functools.partial(project_kernel, map_bins, size, table),...  1.98 us
    ppermute x1, starting transfers between devices, on_device(): lax.ppermute(sent, ('row', 'col'), [(device, target[device]) for device i...  1.66 us
    select_n x1, other arithmetic, on_device(): jnp.where(place == 0, jnp.concatenate([kept, received], axis=axis), jnp.c...  0.7 us
  transfers between devices with their start and end apart: 1, of which 1 were waited for; matrix products, arithmetic and copies ran while one was open for 0% of the time, Pallas kernels for 0%

profile of v12, /device:TPU:4, one launch (start us, length us, event | category | flops | bytes accessed | tf_op | source)
XLA Modules:
  0.0 29.8 jit_solution(11434803384213337057)
XLA Ops:
  0.0 0.0 copy-start
  0.0 0.0 copy-start.1
  0.0 2.0 %shard_map.100 = (bf16[8,32,256]{2,1,0:T(8,128)(2,1)S(1)}, f32[4,304,128]{2,1,0:T(8,128)S(1)}, bf16[16,256]{1,0:T(8,128)(2,1)S(1)}) custom-call(bf16[128,1536]{1,0:T(8,128)(2,1)} %embedding_hbm.1, bf16[4,1536]{1,0:T(4,128)(2,1)} %bases_hbm.1, s32[1,64]{1,0:T(1,128)} %bitcast.10, s32[1,64]{1,0:T(1,128)} %bitcast.11, bf16[1536,128]{1,0:T(8,128)(2,1)} %w_row_hbm.1, ...), custom_call_target="tpu_custom_call" | custom-call | tf_op jit(solution)/shard_map/pallas_call | solution.py:169
  2.0 11.7 %all_to_all.5 = bf16[8,32,256]{2,1,0:T(8,128)(2,1)S(1)} all-to-all(bf16[8,32,256]{2,1,0:T(8,128)(2,1)S(1)} %get-tuple-element.10), channel_id=1, replica_groups=mesh['cand'=4,'row'=4,'col'=2] {'row','col'}, dimensions={0} | all-to-all | bytes 262144 | tf_op jit(solution)/shard_map/all_to_all | solution.py:401
  13.7 0.0 copy-done
  13.7 0.0 copy-done.1
  13.7 8.8 %shard_map.101 = (f32[64,64]{1,0:T(8,128)S(1)}, f32[64,64]{1,0:T(8,128)S(1)}) custom-call(bf16[256,256]{1,0:T(8,128)(2,1)S(1)} %bitcast.7, f32[4,304,128]{2,1,0:T(8,128)S(1)} %get-tuple-element.11.dist_ref, bf16[1152,128]{1,0:T(8,128)(2,1)S(1)} %bitcast.8, bf16[1152,128]{1,0:T(8,128)(2,1)S(1)} %bitcast.9, bf16[16,256]{1,0:T(8,128)(2,1)S(1)} %get-tuple-element.12.head_ref), custom_call_target="tpu_custom_call" | custom-call | tf_op jit(solution)/shard_map/pallas_call | solution.py:354
  22.5 1.7 %collective-permute-start = (f32[64,64]{1,0:T(8,128)S(1)}, f32[64,64]{1,0:T(8,128)S(1)}, u32[]{:S(2)}, u32[]{:S(2)}) collective-permute-start(f32[64,64]{1,0:T(8,128)S(1)} %get-tuple-element.14), channel_id=1, source_target_pairs={{0,2},{1,4},{2,0},{3,6},{4,3},{5,7},{6,1},{7,5},{8,10},{9,12},{10,... | collective-permute-start | bytes 49160 | tf_op jit(solution)/shard_map/ppermute | solution.py:404
  24.1 5.0 %collective-permute-done = f32[64,64]{1,0:T(8,128)S(1)} collective-permute-done((f32[64,64]{1,0:T(8,128)S(1)}, f32[64,64]{1,0:T(8,128)S(1)}, u32[]{:S(2)}, u32[]{:S(2)}) %collective-permute-start) | collective-permute-done | bytes 16416 | tf_op jit(solution)/shard_map/ppermute | solution.py:404
  29.1 0.7 %maximum_select_fusion = f32[64,128]{1,0:T(8,128)} fusion(f32[64,64]{1,0:T(8,128)S(1)} %collective-permute-done, f32[64,64]{1,0:T(8,128)S(1)} %get-tuple-element.13, pred[]{:T(512)S(6)} %eq.31), kind=kLoop, calls=%fused_computation | loop fusion | flops 24576 | bytes 65537 | tf_op jit(solution)/shard_map/jit(_where)/select_n | solution.py:407
Async XLA Ops:
  0.0 13.7 %copy-start = (bf16[3,3,128,128]{3,2,1,0:T(8,128)(2,1)S(1)}, bf16[3,3,128,128]{3,2,1,0:T(8,128)(2,1)}, u32[]{:S(2)}) copy-start(bf16[3,3,128,128]{3,2,1,0:T(8,128)(2,1)} %param.17) | copy-start | bytes 884740
  0.0 13.7 %copy-start.1 = (bf16[3,3,128,128]{3,2,1,0:T(8,128)(2,1)S(1)}, bf16[3,3,128,128]{3,2,1,0:T(8,128)(2,1)}, u32[]{:S(2)}) copy-start(bf16[3,3,128,128]{3,2,1,0:T(8,128)(2,1)} %param.18) | copy-start | bytes 884740
  22.5 6.6 %collective-permute-start = (f32[64,64]{1,0:T(8,128)S(1)}, f32[64,64]{1,0:T(8,128)S(1)}, u32[]{:S(2)}, u32[]{:S(2)}) collective-permute-start(f32[64,64]{1,0:T(8,128)S(1)} %get-tuple-element.14), channel_id=1, source_target_pairs={{0,2},{1,4},{2,0},{3,6},{4,3},{5,7},{6,1},{7,5},{8,10},{9,12},{10,... | collective-permute-start | bytes 49160 | tf_op jit(solution)/shard_map/ppermute | solution.py:404

commit v13 on v3

--- a/solution.py
+++ b/solution.py
@@ -259,7 +259,7 @@
             halves = []
             for half in range(2):
                 o = start + base + half * edge
-                conv = out[n * breadth : (n + 1) * breadth, half * channels : (half + 1) * channels]
+                conv = out[n // 2][n % 2 * breadth : (n % 2 + 1) * breadth, half * channels : (half + 1) * channels]
                 own = hidden_ref[o + edge, :, channels : 2 * channels].astype(jnp.float32)
                 halves.append((own + relu(conv)).astype(jnp.bfloat16))
             last.append(jnp.concatenate(halves, axis=1))
@@ -278,16 +278,21 @@
     for p in range(2 * GROUP):
         build(p)
     for s in range(first_groups + 1):
-        one = two = None
-        if s < first_groups:
-            one = paired(pair_ref, s * GROUP, first_offsets, FIRST_SPACING, pairs_one_ref)
-        for p in range((s + 2) * GROUP, min((s + 3) * GROUP, pair_rows)):
-            build(p)
-        if 0 <= s - 2 < second_groups:
-            two = paired(hidden_ref, (s - 2) * GROUP, second_offsets, SECOND_SPACING, pairs_two_ref)
-        if one is not None:
-            keep_hidden(s * GROUP, first_offsets, one)
-        if two is not None:
+        later = list(range((s + 2) * GROUP, min((s + 3) * GROUP, pair_rows)))
+        two = []
+        for part in range(2):
+            one = None
+            some = first_offsets[2 * part : 2 * part + 2]
+            if s < first_groups:
+                one = paired(pair_ref, s * GROUP, some, FIRST_SPACING, pairs_one_ref)
+            for p in later[4 * part : 4 * part + 4]:
+                build(p)
+            if 0 <= s - 2 < second_groups:
+                start, offsets = (s - 2) * GROUP, second_offsets[2 * part : 2 * part + 2]
+                two.append(paired(hidden_ref, start, offsets, SECOND_SPACING, pairs_two_ref))
+            if one is not None:
+                keep_hidden(s * GROUP, some, one)
+        if two:
             keep_score((s - 2) * GROUP, second_offsets, two)
     score = score_ref[...]
     turned = score.T

time: 30.4 us -> 30.1 us (level)
  no operation moved by 1% of the time
where the time goes in v13:
time: 30.1 us; the launch traced here: 29.9 us
  blocking collectives  11.7 us (39%)
  Pallas kernels  10.9 us (36%)
  waiting for transfers between devices  4.96 us (16%)
  starting transfers between devices  1.67 us (6%)
  other arithmetic  0.7 us (2%)
    all_to_all x1, blocking collectives, on_device(): got = lax.all_to_all(copies, ('row', 'col'), 0, 0)  11.7 us
    pallas_call x1, Pallas kernels, block_scores(): pl.pallas_call(functools.partial(map_kernel, map_bins, size, table), out_...  8.9 us
    ppermute x1, waiting for transfers between devices, on_device(): lax.ppermute(sent, ('row', 'col'), [(device, target[device]) for device i...  4.96 us
    pallas_call x1, Pallas kernels, projected(): pl.pallas_call(functools.partial(project_kernel, map_bins), out_shape=(ja...  1.95 us
    ppermute x1, starting transfers between devices, on_device(): lax.ppermute(sent, ('row', 'col'), [(device, target[device]) for device i...  1.67 us
    select_n x1, other arithmetic, on_device(): jnp.where(place == 0, jnp.concatenate([kept, received], axis=axis), jnp.c...  0.7 us
  transfers between devices with their start and end apart: 1, of which 1 were waited for; matrix products, arithmetic and copies ran while one was open for 0% of the time, Pallas kernels for 0%

profile of v13, /device:TPU:4, one launch (start us, length us, event | category | flops | bytes accessed | tf_op | source)
XLA Modules:
  0.0 29.9 jit_solution(2420706007513600254)
XLA Ops:
  0.0 0.0 copy-start
  0.0 0.0 copy-start.1
  0.0 2.0 %shard_map.100 = (bf16[8,32,256]{2,1,0:T(8,128)(2,1)S(1)}, f32[544,128]{1,0:T(8,128)S(1)}, bf16[16,256]{1,0:T(8,128)(2,1)S(1)}) custom-call(bf16[128,1536]{1,0:T(8,128)(2,1)} %embedding_hbm.1, bf16[4,1536]{1,0:T(4,128)(2,1)} %bases_hbm.1, s32[1,64]{1,0:T(1,128)} %bitcast.10, s32[1,64]{1,0:T(1,128)} %bitcast.11, bf16[1536,128]{1,0:T(8,128)(2,1)} %w_row_hbm.1, ...), custom_call_target="tpu_custom_call" | custom-call | tf_op jit(solution)/shard_map/pallas_call | solution.py:157
  2.0 11.7 %all_to_all.5 = bf16[8,32,256]{2,1,0:T(8,128)(2,1)S(1)} all-to-all(bf16[8,32,256]{2,1,0:T(8,128)(2,1)S(1)} %get-tuple-element.10), channel_id=1, replica_groups=mesh['cand'=4,'row'=4,'col'=2] {'row','col'}, dimensions={0} | all-to-all | bytes 262144 | tf_op jit(solution)/shard_map/all_to_all | solution.py:356
  13.6 0.0 copy-done
  13.6 0.0 copy-done.1
  13.6 8.9 %shard_map.101 = (f32[64,64]{1,0:T(8,128)S(1)}, f32[64,64]{1,0:T(8,128)S(1)}) custom-call(bf16[256,256]{1,0:T(8,128)(2,1)S(1)} %bitcast.7, f32[544,128]{1,0:T(8,128)S(1)} %get-tuple-element.11.dist_table_ref, bf16[1152,128]{1,0:T(8,128)(2,1)S(1)} %bitcast.8, bf16[1152,128]{1,0:T(8,128)(2,1)S(1)} %bitcast.9, bf16[16,256]{1,0:T(8,128)(2,1)S(1)} %get-tuple-element.12.head_ref), custom_call_target="tpu_custom_call" | custom-call | tf_op jit(solution)/shard_map/pallas_call | solution.py:312
  22.5 1.7 %collective-permute-start = (f32[64,64]{1,0:T(8,128)S(1)}, f32[64,64]{1,0:T(8,128)S(1)}, u32[]{:S(2)}, u32[]{:S(2)}) collective-permute-start(f32[64,64]{1,0:T(8,128)S(1)} %get-tuple-element.14), channel_id=1, source_target_pairs={{0,2},{1,4},{2,0},{3,6},{4,3},{5,7},{6,1},{7,5},{8,10},{9,12},{10,... | collective-permute-start | bytes 49160 | tf_op jit(solution)/shard_map/ppermute | solution.py:359
  24.2 5.0 %collective-permute-done = f32[64,64]{1,0:T(8,128)S(1)} collective-permute-done((f32[64,64]{1,0:T(8,128)S(1)}, f32[64,64]{1,0:T(8,128)S(1)}, u32[]{:S(2)}, u32[]{:S(2)}) %collective-permute-start) | collective-permute-done | bytes 16416 | tf_op jit(solution)/shard_map/ppermute | solution.py:359
  29.2 0.7 %maximum_select_fusion = f32[64,128]{1,0:T(8,128)} fusion(f32[64,64]{1,0:T(8,128)S(1)} %collective-permute-done, f32[64,64]{1,0:T(8,128)S(1)} %get-tuple-element.13, pred[]{:T(512)S(6)} %eq.31), kind=kLoop, calls=%fused_computation | loop fusion | flops 24576 | bytes 65537 | tf_op jit(solution)/shard_map/jit(_where)/select_n | solution.py:362
Async XLA Ops:
  0.0 13.6 %copy-start = (bf16[3,3,128,128]{3,2,1,0:T(8,128)(2,1)S(1)}, bf16[3,3,128,128]{3,2,1,0:T(8,128)(2,1)}, u32[]{:S(2)}) copy-start(bf16[3,3,128,128]{3,2,1,0:T(8,128)(2,1)} %param.17) | copy-start | bytes 884740
  0.0 13.6 %copy-start.1 = (bf16[3,3,128,128]{3,2,1,0:T(8,128)(2,1)S(1)}, bf16[3,3,128,128]{3,2,1,0:T(8,128)(2,1)}, u32[]{:S(2)}) copy-start(bf16[3,3,128,128]{3,2,1,0:T(8,128)(2,1)} %param.18) | copy-start | bytes 884740
  22.5 6.6 %collective-permute-start = (f32[64,64]{1,0:T(8,128)S(1)}, f32[64,64]{1,0:T(8,128)S(1)}, u32[]{:S(2)}, u32[]{:S(2)}) collective-permute-start(f32[64,64]{1,0:T(8,128)S(1)} %get-tuple-element.14), channel_id=1, source_target_pairs={{0,2},{1,4},{2,0},{3,6},{4,3},{5,7},{6,1},{7,5},{8,10},{9,12},{10,... | collective-permute-start | bytes 49160 | tf_op jit(solution)/shard_map/ppermute | solution.py:359

commit v14 on v10

--- a/solution.py
+++ b/solution.py
@@ -314,8 +314,9 @@
                 keep_hidden((first_base,), one)
             if seconds:
                 keep_last(second_base, seconds[0])
-    for start in range(0, size // 4, 4):
-        keep_scores(start, 4)
+            if part == 0 and s >= 4 and s % 2 == 0:
+                keep_scores(2 * (s - 4), 4)
+    keep_scores(size // 4 - 4, 4)
     source = lax.broadcasted_iota(jnp.int32, (breadth, breadth), 0)
     place = ((source >> 3) & 1) * (2 * size) + ((source >> 1) & 1) * size
     place = place + 4 * (source >> 4) + 2 * ((source >> 2) & 1) + (source & 1)

time: 30 us -> 30 us (level)
  no operation moved by 1% of the time
where the time goes in v14:
time: 30 us; the launch traced here: 29.8 us
  blocking collectives  11.7 us (39%)
  Pallas kernels  10.8 us (36%)
  waiting for transfers between devices  4.97 us (17%)
  starting transfers between devices  1.66 us (6%)
  other arithmetic  0.7 us (2%)
    all_to_all x1, blocking collectives, on_device(): got = lax.all_to_all(copies, ('row', 'col'), 0, 0)  11.7 us
    pallas_call x1, Pallas kernels, block_scores(): pl.pallas_call(functools.partial(map_kernel, map_bins, size, table), out_...  8.78 us
    ppermute x1, waiting for transfers between devices, on_device(): lax.ppermute(sent, ('row', 'col'), [(device, target[device]) for device i...  4.97 us
    pallas_call x1, Pallas kernels, projected(): pl.pallas_call(functools.partial(project_kernel, map_bins, size, table),...  1.98 us
    ppermute x1, starting transfers between devices, on_device(): lax.ppermute(sent, ('row', 'col'), [(device, target[device]) for device i...  1.66 us
    select_n x1, other arithmetic, on_device(): jnp.where(place == 0, jnp.concatenate([kept, received], axis=axis), jnp.c...  0.7 us
  transfers between devices with their start and end apart: 1, of which 1 were waited for; matrix products, arithmetic and copies ran while one was open for 0% of the time, Pallas kernels for 0%

profile of v14, /device:TPU:4, one launch (start us, length us, event | category | flops | bytes accessed | tf_op | source)
XLA Modules:
  0.0 29.8 jit_solution(4836551776643270753)
XLA Ops:
  0.0 0.0 copy-start
  0.0 0.0 copy-start.1
  0.0 2.0 %shard_map.100 = (bf16[8,32,256]{2,1,0:T(8,128)(2,1)S(1)}, f32[4,304,128]{2,1,0:T(8,128)S(1)}, bf16[16,256]{1,0:T(8,128)(2,1)S(1)}) custom-call(bf16[128,1536]{1,0:T(8,128)(2,1)} %embedding_hbm.1, bf16[4,1536]{1,0:T(4,128)(2,1)} %bases_hbm.1, s32[1,64]{1,0:T(1,128)} %bitcast.10, s32[1,64]{1,0:T(1,128)} %bitcast.11, bf16[1536,128]{1,0:T(8,128)(2,1)} %w_row_hbm.1, ...), custom_call_target="tpu_custom_call" | custom-call | tf_op jit(solution)/shard_map/pallas_call | solution.py:169
  2.0 11.7 %all_to_all.5 = bf16[8,32,256]{2,1,0:T(8,128)(2,1)S(1)} all-to-all(bf16[8,32,256]{2,1,0:T(8,128)(2,1)S(1)} %get-tuple-element.10), channel_id=1, replica_groups=mesh['cand'=4,'row'=4,'col'=2] {'row','col'}, dimensions={0} | all-to-all | bytes 262144 | tf_op jit(solution)/shard_map/all_to_all | solution.py:396
  13.7 0.0 copy-done
  13.7 0.0 copy-done.1
  13.7 8.8 %shard_map.101 = (f32[64,64]{1,0:T(8,128)S(1)}, f32[64,64]{1,0:T(8,128)S(1)}) custom-call(bf16[256,256]{1,0:T(8,128)(2,1)S(1)} %bitcast.7, f32[4,304,128]{2,1,0:T(8,128)S(1)} %get-tuple-element.11.dist_ref, bf16[1152,128]{1,0:T(8,128)(2,1)S(1)} %bitcast.8, bf16[1152,128]{1,0:T(8,128)(2,1)S(1)} %bitcast.9, bf16[16,256]{1,0:T(8,128)(2,1)S(1)} %get-tuple-element.12.head_ref), custom_call_target="tpu_custom_call" | custom-call | tf_op jit(solution)/shard_map/pallas_call | solution.py:349
  22.4 1.7 %collective-permute-start = (f32[64,64]{1,0:T(8,128)S(1)}, f32[64,64]{1,0:T(8,128)S(1)}, u32[]{:S(2)}, u32[]{:S(2)}) collective-permute-start(f32[64,64]{1,0:T(8,128)S(1)} %get-tuple-element.14), channel_id=1, source_target_pairs={{0,2},{1,4},{2,0},{3,6},{4,3},{5,7},{6,1},{7,5},{8,10},{9,12},{10,... | collective-permute-start | bytes 49160 | tf_op jit(solution)/shard_map/ppermute | solution.py:399
  24.1 5.0 %collective-permute-done = f32[64,64]{1,0:T(8,128)S(1)} collective-permute-done((f32[64,64]{1,0:T(8,128)S(1)}, f32[64,64]{1,0:T(8,128)S(1)}, u32[]{:S(2)}, u32[]{:S(2)}) %collective-permute-start) | collective-permute-done | bytes 16416 | tf_op jit(solution)/shard_map/ppermute | solution.py:399
  29.1 0.7 %maximum_select_fusion = f32[64,128]{1,0:T(8,128)} fusion(f32[64,64]{1,0:T(8,128)S(1)} %collective-permute-done, f32[64,64]{1,0:T(8,128)S(1)} %get-tuple-element.13, pred[]{:T(512)S(6)} %eq.31), kind=kLoop, calls=%fused_computation | loop fusion | flops 24576 | bytes 65537 | tf_op jit(solution)/shard_map/jit(_where)/select_n | solution.py:402
Async XLA Ops:
  0.0 13.7 %copy-start = (bf16[3,3,128,128]{3,2,1,0:T(8,128)(2,1)S(1)}, bf16[3,3,128,128]{3,2,1,0:T(8,128)(2,1)}, u32[]{:S(2)}) copy-start(bf16[3,3,128,128]{3,2,1,0:T(8,128)(2,1)} %param.17) | copy-start | bytes 884740
  0.0 13.7 %copy-start.1 = (bf16[3,3,128,128]{3,2,1,0:T(8,128)(2,1)S(1)}, bf16[3,3,128,128]{3,2,1,0:T(8,128)(2,1)}, u32[]{:S(2)}) copy-start(bf16[3,3,128,128]{3,2,1,0:T(8,128)(2,1)} %param.18) | copy-start | bytes 884740
  22.4 6.6 %collective-permute-start = (f32[64,64]{1,0:T(8,128)S(1)}, f32[64,64]{1,0:T(8,128)S(1)}, u32[]{:S(2)}, u32[]{:S(2)}) collective-permute-start(f32[64,64]{1,0:T(8,128)S(1)} %get-tuple-element.14), channel_id=1, source_target_pairs={{0,2},{1,4},{2,0},{3,6},{4,3},{5,7},{6,1},{7,5},{8,10},{9,12},{10,... | collective-permute-start | bytes 49160 | tf_op jit(solution)/shard_map/ppermute | solution.py:399

commit v15 on v12

--- a/solution.py
+++ b/solution.py
@@ -320,8 +320,9 @@
                 keep_hidden((first_base,), one)
             if seconds:
                 keep_last(second_base, seconds[0])
-    for start in range(0, size // 4, 4):
-        keep_scores(start, 4)
+            if part == 0 and s >= 4 and s % 2 == 0:
+                keep_scores(2 * (s - 4), 4)
+    keep_scores(size // 4 - 4, 4)
     source = lax.broadcasted_iota(jnp.int32, (breadth, breadth), 0)
     place = ((source >> 3) & 1) * (2 * size) + ((source >> 1) & 1) * size
     place = place + 4 * (source >> 4) + 2 * ((source >> 2) & 1) + (source & 1)

time: 30 us -> 30 us (level)
  no operation moved by 1% of the time
where the time goes in v15:
time: 30 us; the launch traced here: 29.8 us
  blocking collectives  11.7 us (39%)
  Pallas kernels  10.8 us (36%)
  waiting for transfers between devices  4.97 us (17%)
  starting transfers between devices  1.66 us (6%)
  other arithmetic  0.7 us (2%)
    all_to_all x1, blocking collectives, on_device(): got = lax.all_to_all(copies, ('row', 'col'), 0, 0)  11.7 us
    pallas_call x1, Pallas kernels, block_scores(): pl.pallas_call(functools.partial(map_kernel, map_bins, size, table), out_...  8.78 us
    ppermute x1, waiting for transfers between devices, on_device(): lax.ppermute(sent, ('row', 'col'), [(device, target[device]) for device i...  4.97 us
    pallas_call x1, Pallas kernels, projected(): pl.pallas_call(functools.partial(project_kernel, map_bins, size, table),...  1.98 us
    ppermute x1, starting transfers between devices, on_device(): lax.ppermute(sent, ('row', 'col'), [(device, target[device]) for device i...  1.66 us
    select_n x1, other arithmetic, on_device(): jnp.where(place == 0, jnp.concatenate([kept, received], axis=axis), jnp.c...  0.7 us
  transfers between devices with their start and end apart: 1, of which 1 were waited for; matrix products, arithmetic and copies ran while one was open for 0% of the time, Pallas kernels for 0%

profile of v15, /device:TPU:4, one launch (start us, length us, event | category | flops | bytes accessed | tf_op | source)
XLA Modules:
  0.0 29.8 jit_solution(4836551776643270753)
XLA Ops:
  0.0 0.0 copy-start
  0.0 0.0 copy-start.1
  0.0 2.0 %shard_map.100 = (bf16[8,32,256]{2,1,0:T(8,128)(2,1)S(1)}, f32[4,304,128]{2,1,0:T(8,128)S(1)}, bf16[16,256]{1,0:T(8,128)(2,1)S(1)}) custom-call(bf16[128,1536]{1,0:T(8,128)(2,1)} %embedding_hbm.1, bf16[4,1536]{1,0:T(4,128)(2,1)} %bases_hbm.1, s32[1,64]{1,0:T(1,128)} %bitcast.10, s32[1,64]{1,0:T(1,128)} %bitcast.11, bf16[1536,128]{1,0:T(8,128)(2,1)} %w_row_hbm.1, ...), custom_call_target="tpu_custom_call" | custom-call | tf_op jit(solution)/shard_map/pallas_call | solution.py:169
  2.0 11.7 %all_to_all.5 = bf16[8,32,256]{2,1,0:T(8,128)(2,1)S(1)} all-to-all(bf16[8,32,256]{2,1,0:T(8,128)(2,1)S(1)} %get-tuple-element.10), channel_id=1, replica_groups=mesh['cand'=4,'row'=4,'col'=2] {'row','col'}, dimensions={0} | all-to-all | bytes 262144 | tf_op jit(solution)/shard_map/all_to_all | solution.py:402
  13.7 0.0 copy-done
  13.7 0.0 copy-done.1
  13.7 8.8 %shard_map.101 = (f32[64,64]{1,0:T(8,128)S(1)}, f32[64,64]{1,0:T(8,128)S(1)}) custom-call(bf16[256,256]{1,0:T(8,128)(2,1)S(1)} %bitcast.7, f32[4,304,128]{2,1,0:T(8,128)S(1)} %get-tuple-element.11.dist_ref, bf16[1152,128]{1,0:T(8,128)(2,1)S(1)} %bitcast.8, bf16[1152,128]{1,0:T(8,128)(2,1)S(1)} %bitcast.9, bf16[16,256]{1,0:T(8,128)(2,1)S(1)} %get-tuple-element.12.head_ref), custom_call_target="tpu_custom_call" | custom-call | tf_op jit(solution)/shard_map/pallas_call | solution.py:355
  22.4 1.7 %collective-permute-start = (f32[64,64]{1,0:T(8,128)S(1)}, f32[64,64]{1,0:T(8,128)S(1)}, u32[]{:S(2)}, u32[]{:S(2)}) collective-permute-start(f32[64,64]{1,0:T(8,128)S(1)} %get-tuple-element.14), channel_id=1, source_target_pairs={{0,2},{1,4},{2,0},{3,6},{4,3},{5,7},{6,1},{7,5},{8,10},{9,12},{10,... | collective-permute-start | bytes 49160 | tf_op jit(solution)/shard_map/ppermute | solution.py:405
  24.1 5.0 %collective-permute-done = f32[64,64]{1,0:T(8,128)S(1)} collective-permute-done((f32[64,64]{1,0:T(8,128)S(1)}, f32[64,64]{1,0:T(8,128)S(1)}, u32[]{:S(2)}, u32[]{:S(2)}) %collective-permute-start) | collective-permute-done | bytes 16416 | tf_op jit(solution)/shard_map/ppermute | solution.py:405
  29.1 0.7 %maximum_select_fusion = f32[64,128]{1,0:T(8,128)} fusion(f32[64,64]{1,0:T(8,128)S(1)} %collective-permute-done, f32[64,64]{1,0:T(8,128)S(1)} %get-tuple-element.13, pred[]{:T(512)S(6)} %eq.31), kind=kLoop, calls=%fused_computation | loop fusion | flops 24576 | bytes 65537 | tf_op jit(solution)/shard_map/jit(_where)/select_n | solution.py:408
Async XLA Ops:
  0.0 13.7 %copy-start = (bf16[3,3,128,128]{3,2,1,0:T(8,128)(2,1)S(1)}, bf16[3,3,128,128]{3,2,1,0:T(8,128)(2,1)}, u32[]{:S(2)}) copy-start(bf16[3,3,128,128]{3,2,1,0:T(8,128)(2,1)} %param.17) | copy-start | bytes 884740
  0.0 13.7 %copy-start.1 = (bf16[3,3,128,128]{3,2,1,0:T(8,128)(2,1)S(1)}, bf16[3,3,128,128]{3,2,1,0:T(8,128)(2,1)}, u32[]{:S(2)}) copy-start(bf16[3,3,128,128]{3,2,1,0:T(8,128)(2,1)} %param.18) | copy-start | bytes 884740
  22.4 6.6 %collective-permute-start = (f32[64,64]{1,0:T(8,128)S(1)}, f32[64,64]{1,0:T(8,128)S(1)}, u32[]{:S(2)}, u32[]{:S(2)}) collective-permute-start(f32[64,64]{1,0:T(8,128)S(1)} %get-tuple-element.14), channel_id=1, source_target_pairs={{0,2},{1,4},{2,0},{3,6},{4,3},{5,7},{6,1},{7,5},{8,10},{9,12},{10,... | collective-permute-start | bytes 49160 | tf_op jit(solution)/shard_map/ppermute | solution.py:405

commit v16 on v14

--- a/solution.py
+++ b/solution.py
@@ -299,6 +299,7 @@
     first_groups, second_groups = hidden_couples // 4, size // 8
     for c in range(8):
         build(c)
+    waiting = None
     for s in range(first_groups + 1):
         later = list(range(4 * (s + 2), min(4 * (s + 3), couples)))
         for part in range(2):
@@ -306,6 +307,9 @@
             first_base, second_base = 4 * s + 2 * part, 4 * (s - 2) + part
             if s < first_groups:
                 one = paired(first_taps, (first_base,), 1, pairs_one_ref)
+            if waiting is not None:
+                keep_last(*waiting)
+                waiting = None
             for c in later[2 * part : 2 * part + 2]:
                 build(c)
             if 0 <= s - 2 < second_groups:
@@ -313,9 +317,10 @@
             if one is not None:
                 keep_hidden((first_base,), one)
             if seconds:
-                keep_last(second_base, seconds[0])
+                waiting = second_base, seconds[0]
             if part == 0 and s >= 4 and s % 2 == 0:
                 keep_scores(2 * (s - 4), 4)
+    keep_last(*waiting)
     keep_scores(size // 4 - 4, 4)
     source = lax.broadcasted_iota(jnp.int32, (breadth, breadth), 0)
     place = ((source >> 3) & 1) * (2 * size) + ((source >> 1) & 1) * size

time: 30 us -> 30 us (level)
  no operation moved by 1% of the time
where the time goes in v16:
time: 30 us; the launch traced here: 29.8 us
  blocking collectives  11.7 us (39%)
  Pallas kernels  10.8 us (36%)
  waiting for transfers between devices  4.97 us (17%)
  starting transfers between devices  1.66 us (6%)
  other arithmetic  0.7 us (2%)
    all_to_all x1, blocking collectives, on_device(): got = lax.all_to_all(copies, ('row', 'col'), 0, 0)  11.7 us
    pallas_call x1, Pallas kernels, block_scores(): pl.pallas_call(functools.partial(map_kernel, map_bins, size, table), out_...  8.78 us
    ppermute x1, waiting for transfers between devices, on_device(): lax.ppermute(sent, ('row', 'col'), [(device, target[device]) for device i...  4.97 us
    pallas_call x1, Pallas kernels, projected(): pl.pallas_call(functools.partial(project_kernel, map_bins, size, table),...  1.98 us
    ppermute x1, starting transfers between devices, on_device(): lax.ppermute(sent, ('row', 'col'), [(device, target[device]) for device i...  1.66 us
    select_n x1, other arithmetic, on_device(): jnp.where(place == 0, jnp.concatenate([kept, received], axis=axis), jnp.c...  0.7 us
  transfers between devices with their start and end apart: 1, of which 1 were waited for; matrix products, arithmetic and copies ran while one was open for 0% of the time, Pallas kernels for 0%

profile of v16, /device:TPU:4, one launch (start us, length us, event | category | flops | bytes accessed | tf_op | source)
XLA Modules:
  0.0 29.8 jit_solution(5617874597269805272)
XLA Ops:
  0.0 0.0 copy-start
  0.0 0.0 copy-start.1
  0.0 2.0 %shard_map.100 = (bf16[8,32,256]{2,1,0:T(8,128)(2,1)S(1)}, f32[4,304,128]{2,1,0:T(8,128)S(1)}, bf16[16,256]{1,0:T(8,128)(2,1)S(1)}) custom-call(bf16[128,1536]{1,0:T(8,128)(2,1)} %embedding_hbm.1, bf16[4,1536]{1,0:T(4,128)(2,1)} %bases_hbm.1, s32[1,64]{1,0:T(1,128)} %bitcast.10, s32[1,64]{1,0:T(1,128)} %bitcast.11, bf16[1536,128]{1,0:T(8,128)(2,1)} %w_row_hbm.1, ...), custom_call_target="tpu_custom_call" | custom-call | tf_op jit(solution)/shard_map/pallas_call | solution.py:169
  2.0 11.7 %all_to_all.5 = bf16[8,32,256]{2,1,0:T(8,128)(2,1)S(1)} all-to-all(bf16[8,32,256]{2,1,0:T(8,128)(2,1)S(1)} %get-tuple-element.10), channel_id=1, replica_groups=mesh['cand'=4,'row'=4,'col'=2] {'row','col'}, dimensions={0} | all-to-all | bytes 262144 | tf_op jit(solution)/shard_map/all_to_all | solution.py:401
  13.7 0.0 copy-done
  13.7 0.0 copy-done.1
  13.7 8.8 %shard_map.101 = (f32[64,64]{1,0:T(8,128)S(1)}, f32[64,64]{1,0:T(8,128)S(1)}) custom-call(bf16[256,256]{1,0:T(8,128)(2,1)S(1)} %bitcast.7, f32[4,304,128]{2,1,0:T(8,128)S(1)} %get-tuple-element.11.dist_ref, bf16[1152,128]{1,0:T(8,128)(2,1)S(1)} %bitcast.8, bf16[1152,128]{1,0:T(8,128)(2,1)S(1)} %bitcast.9, bf16[16,256]{1,0:T(8,128)(2,1)S(1)} %get-tuple-element.12.head_ref), custom_call_target="tpu_custom_call" | custom-call | tf_op jit(solution)/shard_map/pallas_call | solution.py:354
  22.4 1.7 %collective-permute-start = (f32[64,64]{1,0:T(8,128)S(1)}, f32[64,64]{1,0:T(8,128)S(1)}, u32[]{:S(2)}, u32[]{:S(2)}) collective-permute-start(f32[64,64]{1,0:T(8,128)S(1)} %get-tuple-element.14), channel_id=1, source_target_pairs={{0,2},{1,4},{2,0},{3,6},{4,3},{5,7},{6,1},{7,5},{8,10},{9,12},{10,... | collective-permute-start | bytes 49160 | tf_op jit(solution)/shard_map/ppermute | solution.py:404
  24.1 5.0 %collective-permute-done = f32[64,64]{1,0:T(8,128)S(1)} collective-permute-done((f32[64,64]{1,0:T(8,128)S(1)}, f32[64,64]{1,0:T(8,128)S(1)}, u32[]{:S(2)}, u32[]{:S(2)}) %collective-permute-start) | collective-permute-done | bytes 16416 | tf_op jit(solution)/shard_map/ppermute | solution.py:404
  29.1 0.7 %maximum_select_fusion = f32[64,128]{1,0:T(8,128)} fusion(f32[64,64]{1,0:T(8,128)S(1)} %collective-permute-done, f32[64,64]{1,0:T(8,128)S(1)} %get-tuple-element.13, pred[]{:T(512)S(6)} %eq.31), kind=kLoop, calls=%fused_computation | loop fusion | flops 24576 | bytes 65537 | tf_op jit(solution)/shard_map/jit(_where)/select_n | solution.py:407
Async XLA Ops:
  0.0 13.7 %copy-start = (bf16[3,3,128,128]{3,2,1,0:T(8,128)(2,1)S(1)}, bf16[3,3,128,128]{3,2,1,0:T(8,128)(2,1)}, u32[]{:S(2)}) copy-start(bf16[3,3,128,128]{3,2,1,0:T(8,128)(2,1)} %param.17) | copy-start | bytes 884740
  0.0 13.7 %copy-start.1 = (bf16[3,3,128,128]{3,2,1,0:T(8,128)(2,1)S(1)}, bf16[3,3,128,128]{3,2,1,0:T(8,128)(2,1)}, u32[]{:S(2)}) copy-start(bf16[3,3,128,128]{3,2,1,0:T(8,128)(2,1)} %param.18) | copy-start | bytes 884740
  22.4 6.6 %collective-permute-start = (f32[64,64]{1,0:T(8,128)S(1)}, f32[64,64]{1,0:T(8,128)S(1)}, u32[]{:S(2)}, u32[]{:S(2)}) collective-permute-start(f32[64,64]{1,0:T(8,128)S(1)} %get-tuple-element.14), channel_id=1, source_target_pairs={{0,2},{1,4},{2,0},{3,6},{4,3},{5,7},{6,1},{7,5},{8,10},{9,12},{10,... | collective-permute-start | bytes 49160 | tf_op jit(solution)/shard_map/ppermute | solution.py:404
